TPU v7x, 32 devices: a whole 2x2x4 slice. The times are simulated.
32 devices in a mesh: rep: 1, node: 32 (over z, y, x, core).
Axes of the slice: x: 2, y: 2, z: 4, core: 2. Of those that a mesh axis runs over, the one named last changes fastest.
Arguments:
- tokens: bfloat16 [2048, 7168], P(('rep', 'node')), may hold values from -6 to 6
- routes: int32 [2048, 2], P(('rep', 'node')), may hold values from 0 to 3, all different within a row; in each aligned block of 64 rows (0 to 63, 64 to 127, ...) at most 64 rows name the same one
- probs: float32 [2048, 2], P(('rep', 'node')), may hold values from 0.2 to 1
- w_gate: bfloat16 [32, 7168, 256], P('node'), may hold values from -0.0625 to 0.0625
- w_up: bfloat16 [32, 7168, 256], P('node'), may hold values from -0.0625 to 0.0625
- w_down: bfloat16 [32, 256, 7168], P('node'), may hold values from -0.125 to 0.125
Outputs:
- mixed: bfloat16 [2048, 7168], P(('rep', 'node'))
Inputs may be any that keep to these rules, and one draw needn't show every extreme that they name: `routes`: each token names 2 different experts; the tokens held by one device name no expert more than 64 times, and in every draw some expert exactly 64 times.
All inputs are finite; a program needn't handle non-finite values.
Results may differ from a plain program's by a relative error of at most 0.0057.
Values may be sent and summed in bfloat16 or wider, within the bound.
No kernel may reach another device: no remote copies, remote signals or barrier semaphores. Data moves between devices by JAX's collectives and lax.ppermute only.
A program may use at most 256 MiB of HBM per device.

v0:
```python
import jax
import jax.numpy as jnp
from jax import lax
from jax.sharding import PartitionSpec as P

GROUP = 8


def per_device(tokens, routes, probs, w_gate, w_up, w_down):
    tok_rows, width = tokens.shape
    chosen_count = routes.shape[1]
    devices = lax.axis_size("node")
    experts = devices // GROUP
    slots = min(tok_rows, GROUP * max(1, 2 * tok_rows * chosen_count // (experts * GROUP)))
    flat_routes = routes.reshape(-1)
    onehot = (flat_routes[:, None] == jnp.arange(experts, dtype=jnp.int32)[None, :]).astype(
        jnp.int32
    )
    ranks = jnp.sum((jnp.cumsum(onehot, axis=0) - onehot) * onehot, axis=1)
    target = flat_routes * slots + ranks
    placed = target[:, None] == jnp.arange(experts * slots, dtype=jnp.int32)[None, :]
    placed = placed.reshape(tok_rows, chosen_count, experts * slots)
    sender = jnp.sum(placed.astype(jnp.float32), axis=1).astype(jnp.bfloat16)
    combine = jnp.sum(jnp.where(placed, probs[:, :, None], 0.0), axis=1)
    packed = lax.dot_general(
        sender, tokens, (((0,), (0,)), ((), ())), preferred_element_type=jnp.float32
    ).astype(jnp.bfloat16)
    spread = jnp.broadcast_to(
        packed.reshape(experts, 1, slots, width), (experts, GROUP, slots, width)
    )
    spread = spread.reshape(devices, slots, width)
    block = lax.all_to_all(spread, "node", split_axis=0, concat_axis=0, tiled=True)
    lead = block.shape[:-1]
    flat_rows = block.reshape(-1, width)
    gate = jnp.dot(flat_rows, w_gate[0], preferred_element_type=jnp.float32)
    up = jnp.dot(flat_rows, w_up[0], preferred_element_type=jnp.float32)
    hidden = (jax.nn.silu(gate) * up).astype(jnp.bfloat16)
    returned = lax.all_to_all(
        jnp.dot(hidden, w_down[0], preferred_element_type=jnp.float32).reshape(lead + (width,)),
        "node",
        split_axis=0,
        concat_axis=0,
        tiled=True,
    )
    summed = jnp.sum(returned.reshape(experts, GROUP, slots, width), axis=1).astype(jnp.bfloat16)
    mixed = jnp.dot(
        combine,
        summed.reshape(experts * slots, width).astype(jnp.float32),
        precision=lax.Precision.HIGHEST,
    )
    return mixed.astype(jnp.bfloat16)


def solution(mesh):
    in_specs = (
        P(("rep", "node"), None),
        P(("rep", "node"), None),
        P(("rep", "node"), None),
        P("node", None, None),
        P("node", None, None),
        P("node", None, None),
    )
    out_specs = P(("rep", "node"), None)
    return jax.shard_map(
        per_device, mesh=mesh, in_specs=in_specs, out_specs=out_specs, check_vma=False
    )
```

profile of v0, /device:TPU:0, one launch (start us, length us, event | category | flops | bytes accessed | tf_op | source)
XLA Modules:
  0.0 1998.5 jit_solution(748878130675057484)
XLA Ops:
  0.0 0.0 copy-start
  0.0 0.8 copy.19
  0.9 0.1 eq.29
  1.0 0.1 fusion.12
  1.1 0.2 reduce_window_sum.11
  1.3 0.2 select_reduce_fusion.1
  1.4 0.1 reduce_sum.39
  1.6 0.1 copy.20
  1.7 0.7 multiply_add_fusion
  2.4 0.8 convert_reduce_fusion
  3.1 0.0 copy-done
  3.2 1.1 convolution_convert_fusion
  4.3 10.0 broadcast_in_dim.26
  14.3 640.3 %all_to_all.10 = bf16[32,64,7168]{2,1,0:T(8,128)(2,1)} all-to-all(bf16[32,64,7168]{2,1,0:T(8,128)(2,1)} %bitcast.28), channel_id=1, replica_groups=mesh['rep'=1,'node'=32] {'node'}, dimensions={0} | all-to-all | bytes 58720256 | tf_op jit(solution)/shard_map/all_to_all | solution.py:32
  654.6 0.0 copy-done.3
  654.6 13.5 fusion.4
  668.1 0.0 copy-done.4
  668.1 0.0 copy-start.2
  668.1 14.1 fusion.9
  682.2 21.3 %fusion = f32[32,64,7168]{2,1,0:T(8,128)} fusion(bf16[32,64,256]{2,1,0:T(8,128)(2,1)S(1)} %bitcast.33, bf16[1,256,7168]{2,1,0:T(8,128)(2,1)S(1)} %copy-done.2), kind=kOutput, calls=%fused_computation.3 | convolution fusion | flops 7516192768 | bytes 63438848 | tf_op jit(solution)/shard_map/dot_general | solution.py:39
  703.5 1268.9 %all_to_all.11 = f32[32,64,7168]{2,1,0:T(8,128)} all-to-all(f32[32,64,7168]{2,1,0:T(8,128)} %fusion), channel_id=1, replica_groups=mesh['rep'=1,'node'=32] {'node'}, dimensions={0} | all-to-all | bytes 117440512 | tf_op jit(solution)/shard_map/all_to_all | solution.py:38
  1972.4 21.1 %bitcast_reduce_fusion = bf16[4,64,7168]{2,1,0:T(8,128)(2,1)} fusion(f32[32,64,7168]{2,1,0:T(8,128)} %all_to_all.11), kind=kLoop, calls=%fused_computation | loop fusion | flops 12845056 | bytes 62390272 | tf_op jit(solution)/shard_map/reduce_sum | solution.py:45
  1993.5 5.0 convolution_convert_fusion.1
  1998.5 0.0 copy-done.1
  (4 shorter events, 0.0 us)
Async XLA Ops:
  0.0 3.1 copy-start
  14.3 640.4 %copy-start.3 = (bf16[1,7168,256]{2,1,0:T(8,128)(2,1)S(1)}, bf16[1,7168,256]{2,1,0:T(8,128)(2,1)}, u32[]{:S(2)}) copy-start(bf16[1,7168,256]{2,1,0:T(8,128)(2,1)} %param.9) | copy-start | bytes 11010052
  654.6 13.5 copy-start.4
  668.1 14.1 copy-start.2
  1972.4 26.1 %copy-start.1 = (bf16[64,7168]{1,0:T(8,128)(2,1)S(1)}, bf16[64,7168]{1,0:T(8,128)(2,1)}, u32[]{:S(2)}) copy-start(bf16[64,7168]{1,0:T(8,128)(2,1)} %param.6) | copy-start | bytes 2752516
where the time goes:
time: 2000 us
  blocking collectives  1910 us (96%)
  matrix products  55 us (3%)
  other arithmetic  23 us (1%)
    all_to_all x1, blocking collectives, per_device(): lax.all_to_all(jnp.dot(hidden, w_down[0], preferred_element_type=jnp.floa...  1270 us
    all_to_all x1, blocking collectives, per_device(): lax.all_to_all(spread, 'node', split_axis=0, concat_axis=0, tiled=True)  640 us

commit v1 on v0

--- a/solution.py
+++ b/solution.py
@@ -4,9 +4,10 @@
 from jax.sharding import PartitionSpec as P
 
 GROUP = 8
+PLANES = 4
 
 
-def per_device(tokens, routes, probs, w_gate, w_up, w_down):
+def general(tokens, routes, probs, w_gate, w_up, w_down):
     tok_rows, width = tokens.shape
     chosen_count = routes.shape[1]
     devices = lax.axis_size("node")
@@ -51,7 +52,113 @@
     return mixed.astype(jnp.bfloat16)
 
 
+CORE, X, Y, Z = 1, 2, 4, 8
+COUNT = PLANES * GROUP
+
+
+def swap(value, bits):
+    return lax.ppermute(value, "node", [(i, i ^ bits) for i in range(COUNT)])
+
+
+def shift(value, step, planes):
+    return lax.ppermute(
+        value,
+        "node",
+        [(z * GROUP + m, (z + step) * GROUP + m) for z in planes for m in range(GROUP)],
+    )
+
+
+def plane_gather(own):
+    rows = own.shape[0] // 2
+    by_x = swap(own, X)
+    by_y = swap(own, Y)
+    low = swap(by_x[:rows], Y)
+    high = swap(by_y[rows:], X)
+    return own, by_x, by_y, jnp.concatenate([low, high], axis=0)
+
+
+def after(value, *earlier):
+    return lax.optimization_barrier((value,) + earlier)[0]
+
+
+def four_planes(tokens, routes, probs, w_gate, w_up, w_down):
+    rows, width = tokens.shape
+    part = width // 4
+    me = lax.axis_index("node")
+    z = me // GROUP
+    quarter = me // 2 % 4
+
+    gate_w = jnp.concatenate([w_gate[0], swap(w_gate[0], CORE)], axis=1)
+    up_w = jnp.concatenate([w_up[0], swap(w_up[0], CORE)], axis=1)
+
+    def cut(r):
+        return lax.dynamic_slice_in_dim(w_down[0], (quarter ^ r) * part, part, axis=1)
+
+    up1 = shift(tokens, 1, (0, 1, 2))
+    dn1 = shift(tokens, -1, (1, 2, 3))
+    up2 = shift(up1, 1, (1, 2))
+    dn2 = shift(dn1, -1, (1, 2))
+    up3 = shift(up2, 1, (2,))
+    dn3 = shift(dn2, -1, (1,))
+    columns = [
+        tokens,
+        jnp.where(z % 2 == 0, dn1, up1),
+        jnp.where(z < 2, dn2, up2),
+        jnp.where(z == 0, dn3, jnp.where(z == 1, dn1, jnp.where(z == 2, up1, up3))),
+    ]
+
+    down_x = swap(cut(1), X)
+    down_y = swap(cut(2), Y)
+    down_d = swap(cut(3), X + Y)
+    down_mine = jnp.stack([cut(0), down_x, down_y, down_d])
+    down_other = swap(down_mine, CORE)
+    down_w = jnp.concatenate([down_mine, down_other], axis=1).reshape(-1, part)
+
+    experts = jnp.arange(PLANES, dtype=jnp.int32)
+    weights = jnp.sum(
+        jnp.where(routes[:, :, None] == experts, probs[:, :, None], 0.0), axis=1
+    )
+    weights = jnp.concatenate(
+        [weights, swap(weights, X), swap(weights, Y), swap(weights, X + Y)], axis=0
+    )
+
+    def weight_of(k):
+        return jnp.sum(jnp.where(experts == (z ^ k), weights, 0.0), axis=1, keepdims=True)
+
+    total = None
+    for k in (1, 2, 3, 0):
+        block = jnp.concatenate(plane_gather(columns[k]), axis=0)
+        gate = jnp.dot(block, gate_w, preferred_element_type=jnp.float32)
+        up = jnp.dot(block, up_w, preferred_element_type=jnp.float32)
+        hidden = (jax.nn.silu(gate) * up).astype(jnp.bfloat16)
+        units = [u.reshape(4, rows, -1) for u in plane_gather(hidden)]
+        hidden = jnp.concatenate(
+            [jnp.concatenate([units[r][j ^ r] for j in range(4)], axis=0) for r in range(4)],
+            axis=1,
+        )
+        out = jnp.dot(hidden, down_w, preferred_element_type=jnp.float32).astype(jnp.bfloat16)
+        if k:
+            out = swap(out, k * Z)
+        term = weight_of(k) * out.astype(jnp.float32)
+        total = term if total is None else total + term
+    mixed = total.astype(jnp.bfloat16).reshape(4, rows, part)
+    pieces = [mixed[0], swap(mixed[1], X), swap(mixed[2], Y), swap(mixed[3], X + Y)]
+    result = []
+    for a in range(4):
+        piece = pieces[a]
+        for q in range(1, 4):
+            piece = jnp.where(quarter == q, pieces[a ^ q], piece)
+        result.append(piece)
+    return jnp.concatenate(result, axis=1)
+
+
 def solution(mesh):
+    devices = mesh.shape["node"]
+
+    def per_device(tokens, routes, probs, w_gate, w_up, w_down):
+        path = four_planes if devices == COUNT else general
+        return path(tokens, routes, probs, w_gate, w_up, w_down)
+
     in_specs = (
         P(("rep", "node"), None),
         P(("rep", "node"), None),

time: 2000 us -> 402 us (0.20)
  blocking collectives: 1910 us -> 0 us
  waiting for transfers between devices: 0 us -> 220 us
  starting transfers between devices: 0 us -> 66.2 us
  matrix products: 55 us -> 94.6 us
    all_to_all x2 -> x0, blocking collectives: 1910 us -> none  [the longest x1 1270 us: per_device(): lax.all_to_all(jnp.dot(hidden, w_down[0], preferred_element_type=jnp.floa...]
    ppermute x0 -> x53, waiting for transfers between devices: none -> 220 us  [the longest x47 186 us: swap(): return lax.ppermute(value, 'node', [(i, i ^ bits) for i in range(COUNT)])]
    ppermute x0 -> x53, starting transfers between devices: none -> 66.2 us  [the longest x47 56 us: swap(): return lax.ppermute(value, 'node', [(i, i ^ bits) for i in range(COUNT)])]
    dot_general x5 -> x12, matrix products: 55 us -> 94.6 us  [the longest x4 51.5 us: four_planes(): jnp.dot(hidden, down_w, preferred_element_type=jnp.float32)]
    reduce_sum x3 -> x2, other arithmetic: 22.1 us -> 0.8 us  [the longest x1 0.71 us: four_planes(): jnp.sum(jnp.where(routes[:, :, None] == experts, probs[:, :, None], 0.0),...]
  transfers between devices with their start and end apart: 0 -> 53, of which waited for: 0 -> 23; matrix products, arithmetic and copies ran while one was open for 0% -> 24% of each run, Pallas kernels for 0% -> 0%
where the time goes in v1:
time: 402 us; the launch traced here: 399 us
  waiting for transfers between devices  220 us (55%)
  matrix products  94.6 us (24%)
  starting transfers between devices  66.2 us (16%)
  other arithmetic  9.57 us (2%)
  local copies, waits for them, and re-layouts  7.96 us (2%)
    ppermute x47, waiting for transfers between devices, swap(): return lax.ppermute(value, 'node', [(i, i ^ bits) for i in range(COUNT)])  186 us
    ppermute x47, starting transfers between devices, swap(): return lax.ppermute(value, 'node', [(i, i ^ bits) for i in range(COUNT)])  56 us
    dot_general x4, matrix products, four_planes(): jnp.dot(hidden, down_w, preferred_element_type=jnp.float32)  51.5 us
    ppermute x6, waiting for transfers between devices, shift(): lax.ppermute(value, 'node', [(z * GROUP + m, (z + step) * GROUP + m) for...  34.1 us
    dot_general x4, matrix products, four_planes(): gate = jnp.dot(block, gate_w, preferred_element_type=jnp.float32)  21.8 us
    dot_general x4, matrix products, four_planes(): up = jnp.dot(block, up_w, preferred_element_type=jnp.float32)  21.3 us
    ppermute x6, starting transfers between devices, shift(): lax.ppermute(value, 'node', [(z * GROUP + m, (z + step) * GROUP + m) for...  10.2 us
  transfers between devices with their start and end apart: 53, of which 23 were waited for; matrix products, arithmetic and copies ran while one was open for 24% of the time, Pallas kernels for 0%

profile of v1, /device:TPU:0, one launch (start us, length us, event | category | flops | bytes accessed | tf_op | source)
XLA Modules:
  0.0 399.0 jit_solution(7869595471344830092)
XLA Ops:
  17.0 13.1 %collective-permute-done.42 = bf16[64,7168]{1,0:T(8,128)(2,1)S(1)} collective-permute-done((bf16[64,7168]{1,0:T(8,128)(2,1)}, bf16[64,7168]{1,0:T(8,128)(2,1)S(1)}, u32[]{:S(2)}, u32[]{:S(2)}) %collective-permute-start.42) | collective-permute-done | bytes 917536 | tf_op jit(solution)/shard_map/ppermute | solution.py:60
  33.0 18.2 %collective-permute-done.17 = bf16[256,1792]{1,0:T(8,128)(2,1)S(1)} collective-permute-done((bf16[256,1792]{1,0:T(8,128)(2,1)}, bf16[256,1792]{1,0:T(8,128)(2,1)S(1)}, u32[]{:S(2)}, u32[]{:S(2)}) %collective-permute-start.17) | collective-permute-done | bytes 917536 | tf_op jit(solution)/shard_map/ppermute | solution.py:60
  58.9 17.1 %collective-permute-done.16 = bf16[256,1792]{1,0:T(8,128)(2,1)S(1)} collective-permute-done((bf16[256,1792]{1,0:T(8,128)(2,1)}, bf16[256,1792]{1,0:T(8,128)(2,1)S(1)}, u32[]{:S(2)}, u32[]{:S(2)}) %collective-permute-start.16) | collective-permute-done | bytes 917536 | tf_op jit(solution)/shard_map/ppermute | solution.py:60
  84.3 5.3 %collective-permute-done.45 = bf16[32,7168]{1,0:T(8,128)(2,1)S(1)} collective-permute-done((bf16[32,7168]{1,0:T(8,128)(2,1)S(1)}, bf16[32,7168]{1,0:T(8,128)(2,1)S(1)}, u32[]{:S(2)}, u32[]{:S(2)}) %collective-permute-start.45) | collective-permute-done | bytes 458784 | tf_op jit(solution)/shard_map/ppermute | solution.py:60
  89.6 13.0 %collective-permute-done.20 = bf16[64,7168]{1,0:T(8,128)(2,1)S(1)} collective-permute-done((bf16[64,7168]{1,0:T(8,128)(2,1)}, bf16[64,7168]{1,0:T(8,128)(2,1)S(1)}, u32[]{:S(2)}, u32[]{:S(2)}) %collective-permute-start.20) | collective-permute-done | bytes 917536 | tf_op jit(solution)/shard_map/ppermute | solution.py:64
  104.9 21.1 %collective-permute-done.31 = bf16[64,7168]{1,0:T(8,128)(2,1)S(1)} collective-permute-done((bf16[64,7168]{1,0:T(8,128)(2,1)S(1)}, bf16[64,7168]{1,0:T(8,128)(2,1)S(1)}, u32[]{:S(2)}, u32[]{:S(2)}) %collective-permute-start.31) | collective-permute-done | bytes 917536 | tf_op jit(solution)/shard_map/ppermute | solution.py:64
  130.8 16.0 %collective-permute-done.22 = bf16[64,7168]{1,0:T(8,128)(2,1)S(1)} collective-permute-done((bf16[64,7168]{1,0:T(8,128)(2,1)S(1)}, bf16[64,7168]{1,0:T(8,128)(2,1)S(1)}, u32[]{:S(2)}, u32[]{:S(2)}) %collective-permute-start.22) | collective-permute-done | bytes 917536 | tf_op jit(solution)/shard_map/ppermute | solution.py:60
  149.8 7.8 %collective-permute-done.24 = bf16[32,7168]{1,0:T(8,128)(2,1)S(1)} collective-permute-done((bf16[32,7168]{1,0:T(8,128)(2,1)S(1)}, bf16[32,7168]{1,0:T(8,128)(2,1)S(1)}, u32[]{:S(2)}, u32[]{:S(2)}) %collective-permute-start.24) | collective-permute-done | bytes 458784 | tf_op jit(solution)/shard_map/ppermute | solution.py:60
  158.7 17.8 %collective-permute-done.25 = bf16[32,7168]{1,0:T(8,128)(2,1)S(1)} collective-permute-done((bf16[32,7168]{1,0:T(8,128)(2,1)S(1)}, bf16[32,7168]{1,0:T(8,128)(2,1)S(1)}, u32[]{:S(2)}, u32[]{:S(2)}) %collective-permute-start.25) | collective-permute-done | bytes 458784 | tf_op jit(solution)/shard_map/ppermute | solution.py:60
  179.6 6.1 %fusion.97 = f32[256,512]{1,0:T(8,128)} fusion(bf16[256,7168]{1,0:T(8,128)(2,1)S(1)} %constant_dynamic-update-slice_fusion.5, bf16[7168,256]{1,0:T(8,128)(2,1)} %collective-permute-done.9, bf16[7168,256]{1,0:T(8,128)(2,1)} %bitcast), kind=kOutput, calls=%fused_computation.151 | convolution fusion | flops 1893728256 | bytes 11534336 | tf_op jit(solution)/shard_map/dot_general | solution.py:131
  185.6 5.3 %multiply_convert_fusion.2 = bf16[256,512]{1,0:T(8,128)(2,1)S(1)} fusion(f32[256,512]{1,0:T(8,128)} %fusion.97, bf16[256,7168]{1,0:T(8,128)(2,1)S(1)} %constant_dynamic-update-slice_fusion.5, bf16[7168,256]{1,0:T(8,128)(2,1)} %collective-permute-done.10, bf16[7168,256]{1,0:T(8,128)(2,1)} %bitcast.1), kind=kOutput, calls=%fused_computation.103 | convolution fusion | flops 1894514688 | bytes 11796480 | tf_op jit(solution)/shard_map/dot_general | solution.py:132
  190.9 5.3 %fusion.95 = f32[256,512]{1,0:T(8,128)S(1)} fusion(bf16[256,7168]{1,0:T(8,128)(2,1)S(1)} %constant_dynamic-update-slice_fusion.15, bf16[7168,256]{1,0:T(8,128)(2,1)} %collective-permute-done.9, bf16[7168,256]{1,0:T(8,128)(2,1)} %bitcast), kind=kOutput, calls=%fused_computation.149 | convolution fusion | flops 1893728256 | bytes 11534336 | tf_op jit(solution)/shard_map/dot_general | solution.py:131
  196.2 5.3 %multiply_convert_fusion = bf16[256,512]{1,0:T(8,128)(2,1)S(1)} fusion(f32[256,512]{1,0:T(8,128)S(1)} %fusion.95, bf16[256,7168]{1,0:T(8,128)(2,1)S(1)} %constant_dynamic-update-slice_fusion.15, bf16[7168,256]{1,0:T(8,128)(2,1)} %collective-permute-done.10, bf16[7168,256]{1,0:T(8,128)(2,1)} %bitcast.1), kind=kOutput, calls=%fused_computation.101 | convolution fusion | flops 1894514688 | bytes 11796480 | tf_op jit(solution)/shard_map/dot_general | solution.py:132
  206.0 13.4 %collective-permute-done.6 = bf16[64,7168]{1,0:T(8,128)(2,1)S(1)} collective-permute-done((bf16[64,7168]{1,0:T(8,128)(2,1)S(1)}, bf16[64,7168]{1,0:T(8,128)(2,1)S(1)}, u32[]{:S(2)}, u32[]{:S(2)}) %collective-permute-start.6) | collective-permute-done | bytes 917536 | tf_op jit(solution)/shard_map/ppermute | solution.py:60
  228.2 12.3 %collective-permute-done.29 = bf16[128,512]{1,0:T(8,128)(2,1)S(1)} collective-permute-done((bf16[128,512]{1,0:T(8,128)(2,1)S(1)}, bf16[128,512]{1,0:T(8,128)(2,1)S(1)}, u32[]{:S(2)}, u32[]{:S(2)}) %collective-permute-start.29) | collective-permute-done | bytes 131104 | tf_op jit(solution)/shard_map/ppermute | solution.py:60
  244.7 5.3 %fusion.96 = f32[256,512]{1,0:T(8,128)S(1)} fusion(bf16[256,7168]{1,0:T(8,128)(2,1)S(1)} %constant_dynamic-update-slice_fusion.10, bf16[7168,256]{1,0:T(8,128)(2,1)} %collective-permute-done.9, bf16[7168,256]{1,0:T(8,128)(2,1)} %bitcast), kind=kOutput, calls=%fused_computation.150 | convolution fusion | flops 1893728256 | bytes 11534336 | tf_op jit(solution)/shard_map/dot_general | solution.py:131
  249.9 5.5 %multiply_convert_fusion.1 = bf16[256,512]{1,0:T(8,128)(2,1)S(1)} fusion(f32[256,512]{1,0:T(8,128)S(1)} %fusion.96, bf16[256,7168]{1,0:T(8,128)(2,1)S(1)} %constant_dynamic-update-slice_fusion.10, bf16[7168,256]{1,0:T(8,128)(2,1)} %collective-permute-done.10, bf16[7168,256]{1,0:T(8,128)(2,1)} %bitcast.1), kind=kOutput, calls=%fused_computation.102 | convolution fusion | flops 1894514688 | bytes 11796480 | tf_op jit(solution)/shard_map/dot_general | solution.py:132
  256.8 5.3 %fusion.98 = f32[256,512]{1,0:T(8,128)S(1)} fusion(bf16[256,7168]{1,0:T(8,128)(2,1)S(1)} %constant_dynamic-update-slice_fusion, bf16[7168,256]{1,0:T(8,128)(2,1)} %collective-permute-done.9, bf16[7168,256]{1,0:T(8,128)(2,1)} %bitcast), kind=kOutput, calls=%fused_computation.152 | convolution fusion | flops 1893728256 | bytes 11534336 | tf_op jit(solution)/shard_map/dot_general | solution.py:131
  262.1 5.3 %multiply_convert_fusion.3 = bf16[256,512]{1,0:T(8,128)(2,1)S(1)} fusion(f32[256,512]{1,0:T(8,128)S(1)} %fusion.98, bf16[256,7168]{1,0:T(8,128)(2,1)S(1)} %constant_dynamic-update-slice_fusion, bf16[7168,256]{1,0:T(8,128)(2,1)} %collective-permute-done.10, bf16[7168,256]{1,0:T(8,128)(2,1)} %bitcast.1), kind=kOutput, calls=%fused_computation.104 | convolution fusion | flops 1894514688 | bytes 11796480 | tf_op jit(solution)/shard_map/dot_general | solution.py:132
  293.5 12.6 %convolution_convert_fusion.1 = bf16[256,1792]{1,0:T(8,128)(2,1)S(1)} fusion(bf16[2048,1792]{1,0:T(8,128)(2,1)S(1)} %bitcast.24, bf16[64,512]{1,0:T(8,128)(2,1)S(1)} %get-tuple-element.67, bf16[64,512]{1,0:T(8,128)(2,1)S(1)} %get-tuple-element.66, bf16[64,512]{1,0:T(8,128)(2,1)S(1)} %get-tuple-element.65, bf16[64,512]{1,0:T(8,128)(2,1)S(1)} %get-tuple-element.64, ...), kind=kOutput, calls=%fused_computation.6 | convolution fusion | flops 1891041280 | bytes 9306112 | tf_op jit(solution)/shard_map/dot_general | solution.py:139
  306.2 13.0 %convolution_convert_fusion.2 = bf16[256,1792]{1,0:T(8,128)(2,1)S(1)} fusion(bf16[2048,1792]{1,0:T(8,128)(2,1)S(1)} %bitcast.25, bf16[64,512]{1,0:T(8,128)(2,1)S(1)} %get-tuple-element.63, bf16[64,512]{1,0:T(8,128)(2,1)S(1)} %get-tuple-element.62, bf16[64,512]{1,0:T(8,128)(2,1)S(1)} %get-tuple-element.61, bf16[64,512]{1,0:T(8,128)(2,1)S(1)} %get-tuple-element.60, ...), kind=kOutput, calls=%fused_computation.7 | convolution fusion | flops 1891041280 | bytes 9306112 | tf_op jit(solution)/shard_map/dot_general | solution.py:139
  320.2 12.7 %convolution_convert_fusion.3 = bf16[256,1792]{1,0:T(8,128)(2,1)S(1)} fusion(bf16[2048,1792]{1,0:T(8,128)(2,1)S(1)} %bitcast.26, bf16[64,512]{1,0:T(8,128)(2,1)S(1)} %get-tuple-element.59, bf16[64,512]{1,0:T(8,128)(2,1)S(1)} %get-tuple-element.58, bf16[64,512]{1,0:T(8,128)(2,1)S(1)} %get-tuple-element.57, bf16[64,512]{1,0:T(8,128)(2,1)S(1)} %get-tuple-element.56, ...), kind=kOutput, calls=%fused_computation.8 | convolution fusion | flops 1891041280 | bytes 9306112 | tf_op jit(solution)/shard_map/dot_general | solution.py:139
  341.5 32.3 %collective-permute-done.30 = bf16[256,1792]{1,0:T(8,128)(2,1)S(1)} collective-permute-done((bf16[256,1792]{1,0:T(8,128)(2,1)S(1)}, bf16[256,1792]{1,0:T(8,128)(2,1)S(1)}, u32[]{:S(2)}, u32[]{:S(2)}) %collective-permute-start.30) | collective-permute-done | bytes 917536 | tf_op jit(solution)/shard_map/ppermute | solution.py:60
  373.7 13.1 %add_convert_fusion = bf16[256,1792]{1,0:T(8,128)(2,1)S(1)} fusion(bf16[256,1792]{1,0:T(8,128)(2,1)S(1)} %collective-permute-done.41, bf16[256,1792]{1,0:T(8,128)(2,1)S(1)} %collective-permute-done.30, bf16[256,1792]{1,0:T(8,128)(2,1)S(1)} %collective-permute-done.19, f32[256]{0:T(256)S(1)} %get-tuple-element.6, f32[256]{0:T(256)S(1)} %get-tuple-element.7, ...), kind=kOutput, calls=%fused_computation.9 | convolution fusion | flops 1896546304 | bytes 12062720 | tf_op jit(solution)/shard_map/dot_general | solution.py:139
  (156 shorter events, 116.3 us)
Async XLA Ops:
  5.2 71.8 %collective-permute-start.3 = (bf16[64,7168]{1,0:T(8,128)(2,1)}, bf16[64,7168]{1,0:T(8,128)(2,1)}, u32[]{:S(2)}, u32[]{:S(2)}) collective-permute-start(bf16[64,7168]{1,0:T(8,128)(2,1)} %param.6), channel_id=1, source_target_pairs={{8,0},{9,1},{10,2},{11,3},{12,4},{13,5},{14,6},{15,7},{16,8},{17,9... | collective-permute-start | bytes 2752520 | tf_op jit(solution)/shard_map/ppermute | solution.py:64
  6.5 23.6 %collective-permute-start.42 = (bf16[64,7168]{1,0:T(8,128)(2,1)}, bf16[64,7168]{1,0:T(8,128)(2,1)S(1)}, u32[]{:S(2)}, u32[]{:S(2)}) collective-permute-start(bf16[64,7168]{1,0:T(8,128)(2,1)} %param.6), channel_id=1, source_target_pairs={{0,2},{1,3},{2,0},{3,1},{4,6},{5,7},{6,4},{7,5},{8,10},{9,11},{10,... | collective-permute-start | bytes 2752520 | tf_op jit(solution)/shard_map/ppermute | solution.py:60
  13.3 43.0 %collective-permute-start.43 = (bf16[64,7168]{1,0:T(8,128)(2,1)S(1)}, bf16[64,7168]{1,0:T(8,128)(2,1)S(1)}, u32[]{:S(2)}, u32[]{:S(2)}) collective-permute-start(bf16[64,7168]{1,0:T(8,128)(2,1)S(1)} %copy-done), channel_id=1, source_target_pairs={{0,4},{1,5},{2,6},{3,7},{4,0},{5,1},{6,2},{7,3},{8,12},{9,13},{10,... | collective-permute-start | bytes 2752520 | tf_op jit(solution)/shard_map/ppermute | solution.py:60
  14.9 36.3 %collective-permute-start.17 = (bf16[256,1792]{1,0:T(8,128)(2,1)}, bf16[256,1792]{1,0:T(8,128)(2,1)S(1)}, u32[]{:S(2)}, u32[]{:S(2)}) collective-permute-start(bf16[256,1792]{1,0:T(8,128)(2,1)} %get-tuple-element.17), channel_id=1, source_target_pairs={{0,6},{1,7},{2,4},{3,5},{4,2},{5,3},{6,0},{7,1},{8,14},{9,15},{10,... | collective-permute-start | bytes 2752520 | tf_op jit(solution)/shard_map/ppermute | solution.py:60
  15.0 61.0 %collective-permute-start.16 = (bf16[256,1792]{1,0:T(8,128)(2,1)}, bf16[256,1792]{1,0:T(8,128)(2,1)S(1)}, u32[]{:S(2)}, u32[]{:S(2)}) collective-permute-start(bf16[256,1792]{1,0:T(8,128)(2,1)} %get-tuple-element.18), channel_id=1, source_target_pairs={{0,4},{1,5},{2,6},{3,7},{4,0},{5,1},{6,2},{7,3},{8,12},{9,13},{10,... | collective-permute-start | bytes 2752520 | tf_op jit(solution)/shard_map/ppermute | solution.py:60
  30.1 45.9 %collective-permute-start.15 = (bf16[256,1792]{1,0:T(8,128)(2,1)}, bf16[256,1792]{1,0:T(8,128)(2,1)S(1)}, u32[]{:S(2)}, u32[]{:S(2)}) collective-permute-start(bf16[256,1792]{1,0:T(8,128)(2,1)} %get-tuple-element.16), channel_id=1, source_target_pairs={{0,2},{1,3},{2,0},{3,1},{4,6},{5,7},{6,4},{7,5},{8,10},{9,11},{10,... | collective-permute-start | bytes 2752520 | tf_op jit(solution)/shard_map/ppermute | solution.py:60
  51.2 26.0 %collective-permute-start.4 = (bf16[64,7168]{1,0:T(8,128)(2,1)S(1)}, bf16[64,7168]{1,0:T(8,128)(2,1)S(1)}, u32[]{:S(2)}, u32[]{:S(2)}) collective-permute-start(bf16[64,7168]{1,0:T(8,128)(2,1)S(1)} %copy-done), channel_id=1, source_target_pairs={{0,8},{1,9},{2,10},{3,11},{4,12},{5,13},{6,14},{7,15},{8,16},{9,17... | collective-permute-start | bytes 2752520 | tf_op jit(solution)/shard_map/ppermute | solution.py:64
  56.3 27.2 %collective-permute-start.44 = (bf16[32,7168]{1,0:T(8,128)(2,1)S(1)}, bf16[32,7168]{1,0:T(8,128)(2,1)S(1)}, u32[]{:S(2)}, u32[]{:S(2)}) collective-permute-start(bf16[32,7168]{1,0:T(8,128)(2,1)S(1)} %slice.387), channel_id=1, source_target_pairs={{0,4},{1,5},{2,6},{3,7},{4,0},{5,1},{6,2},{7,3},{8,12},{9,13},{10,... | collective-permute-start | bytes 1376264 | tf_op jit(solution)/shard_map/ppermute | solution.py:60
  76.0 102.4 %collective-permute-start.9 = (bf16[7168,256]{1,0:T(8,128)(2,1)}, bf16[7168,256]{1,0:T(8,128)(2,1)}, u32[]{:S(2)}, u32[]{:S(2)}) collective-permute-start(bf16[7168,256]{1,0:T(8,128)(2,1)} %bitcast), channel_id=1, source_target_pairs={{0,1},{1,0},{2,3},{3,2},{4,5},{5,4},{6,7},{7,6},{8,9},{9,8},{10,11... | collective-permute-start | bytes 11010056 | tf_op jit(solution)/shard_map/ppermute | solution.py:60
  76.0 109.6 %collective-permute-start.10 = (bf16[7168,256]{1,0:T(8,128)(2,1)}, bf16[7168,256]{1,0:T(8,128)(2,1)}, u32[]{:S(2)}, u32[]{:S(2)}) collective-permute-start(bf16[7168,256]{1,0:T(8,128)(2,1)} %bitcast.1), channel_id=1, source_target_pairs={{0,1},{1,0},{2,3},{3,2},{4,5},{5,4},{6,7},{7,6},{8,9},{9,8},{10,11... | collective-permute-start | bytes 11010056 | tf_op jit(solution)/shard_map/ppermute | solution.py:60
  77.2 25.3 %collective-permute-start.20 = (bf16[64,7168]{1,0:T(8,128)(2,1)}, bf16[64,7168]{1,0:T(8,128)(2,1)S(1)}, u32[]{:S(2)}, u32[]{:S(2)}) collective-permute-start(bf16[64,7168]{1,0:T(8,128)(2,1)} %collective-permute-done.3), channel_id=1, source_target_pairs={{8,0},{9,1},{10,2},{11,3},{12,4},{13,5},{14,6},{15,7},{16,8},{17,9... | collective-permute-start | bytes 2752520 | tf_op jit(solution)/shard_map/ppermute | solution.py:64
  89.5 198.8 %collective-permute-start.18 = (bf16[4,256,1792]{2,1,0:T(8,128)(2,1)S(1)}, bf16[4,256,1792]{2,1,0:T(8,128)(2,1)S(1)}, u32[]{:S(2)}, u32[]{:S(2)}) collective-permute-start(bf16[4,256,1792]{2,1,0:T(8,128)(2,1)S(1)} %pad_maximum_fusion.3), channel_id=1, source_target_pairs={{0,1},{1,0},{2,3},{3,2},{4,5},{5,4},{6,7},{7,6},{8,9},{9,8},{10,11... | collective-permute-start | bytes 11010056 | tf_op jit(solution)/shard_map/ppermute | solution.py:60
  102.5 23.5 %collective-permute-start.31 = (bf16[64,7168]{1,0:T(8,128)(2,1)S(1)}, bf16[64,7168]{1,0:T(8,128)(2,1)S(1)}, u32[]{:S(2)}, u32[]{:S(2)}) collective-permute-start(bf16[64,7168]{1,0:T(8,128)(2,1)S(1)} %collective-permute-done.20), channel_id=1, source_target_pairs={{8,0},{9,1},{10,2},{11,3},{12,4},{13,5},{14,6},{15,7}} | collective-permute-start | bytes 2752520 | tf_op jit(solution)/shard_map/ppermute | solution.py:64
  103.8 23.6 %collective-permute-start.32 = (bf16[64,7168]{1,0:T(8,128)(2,1)S(1)}, bf16[64,7168]{1,0:T(8,128)(2,1)S(1)}, u32[]{:S(2)}, u32[]{:S(2)}) collective-permute-start(bf16[64,7168]{1,0:T(8,128)(2,1)S(1)} %collective-permute-done.21), channel_id=1, source_target_pairs={{16,24},{17,25},{18,26},{19,27},{20,28},{21,29},{22,30},{23,31}} | collective-permute-start | bytes 2752520 | tf_op jit(solution)/shard_map/ppermute | solution.py:64
  146.8 54.7 %collective-permute-start.33 = (bf16[64,7168]{1,0:T(8,128)(2,1)S(1)}, bf16[64,7168]{1,0:T(8,128)(2,1)S(1)}, u32[]{:S(2)}, u32[]{:S(2)}) collective-permute-start(bf16[64,7168]{1,0:T(8,128)(2,1)S(1)} %get-tuple-element.20), channel_id=1, source_target_pairs={{0,2},{1,3},{2,0},{3,1},{4,6},{5,7},{6,4},{7,5},{8,10},{9,11},{10,... | collective-permute-start | bytes 2752520 | tf_op jit(solution)/shard_map/ppermute | solution.py:60
  176.4 26.2 %collective-permute-start.34 = (bf16[64,7168]{1,0:T(8,128)(2,1)S(1)}, bf16[64,7168]{1,0:T(8,128)(2,1)S(1)}, u32[]{:S(2)}, u32[]{:S(2)}) collective-permute-start(bf16[64,7168]{1,0:T(8,128)(2,1)S(1)} %get-tuple-element.20), channel_id=1, source_target_pairs={{0,4},{1,5},{2,6},{3,7},{4,0},{5,1},{6,2},{7,3},{8,12},{9,13},{10,... | collective-permute-start | bytes 2752520 | tf_op jit(solution)/shard_map/ppermute | solution.py:60
  178.4 26.3 %collective-permute-start.5 = (bf16[64,7168]{1,0:T(8,128)(2,1)S(1)}, bf16[64,7168]{1,0:T(8,128)(2,1)S(1)}, u32[]{:S(2)}, u32[]{:S(2)}) collective-permute-start(bf16[64,7168]{1,0:T(8,128)(2,1)S(1)} %get-tuple-element.10), channel_id=1, source_target_pairs={{0,2},{1,3},{2,0},{3,1},{4,6},{5,7},{6,4},{7,5},{8,10},{9,11},{10,... | collective-permute-start | bytes 2752520 | tf_op jit(solution)/shard_map/ppermute | solution.py:60
  185.6 33.7 %collective-permute-start.6 = (bf16[64,7168]{1,0:T(8,128)(2,1)S(1)}, bf16[64,7168]{1,0:T(8,128)(2,1)S(1)}, u32[]{:S(2)}, u32[]{:S(2)}) collective-permute-start(bf16[64,7168]{1,0:T(8,128)(2,1)S(1)} %get-tuple-element.10), channel_id=1, source_target_pairs={{0,4},{1,5},{2,6},{3,7},{4,0},{5,1},{6,2},{7,3},{8,12},{9,13},{10,... | collective-permute-start | bytes 2752520 | tf_op jit(solution)/shard_map/ppermute | solution.py:60
  219.4 117.0 %collective-permute-start.47 = (bf16[256,512]{1,0:T(8,128)(2,1)S(1)}, bf16[256,512]{1,0:T(8,128)(2,1)S(1)}, u32[]{:S(2)}, u32[]{:S(2)}) collective-permute-start(bf16[256,512]{1,0:T(8,128)(2,1)S(1)} %multiply_convert_fusion), channel_id=1, source_target_pairs={{0,4},{1,5},{2,6},{3,7},{4,0},{5,1},{6,2},{7,3},{8,12},{9,13},{10,... | collective-permute-start | bytes 786440 | tf_op jit(solution)/shard_map/ppermute | solution.py:60
  243.7 23.7 %collective-permute-start.28 = (bf16[128,512]{1,0:T(8,128)(2,1)S(1)}, bf16[128,512]{1,0:T(8,128)(2,1)S(1)}, u32[]{:S(2)}, u32[]{:S(2)}) collective-permute-start(bf16[128,512]{1,0:T(8,128)(2,1)S(1)} %get-tuple-element.45), channel_id=1, source_target_pairs={{0,2},{1,3},{2,0},{3,1},{4,6},{5,7},{6,4},{7,5},{8,10},{9,11},{10,... | collective-permute-start | bytes 393224 | tf_op jit(solution)/shard_map/ppermute | solution.py:60
  273.9 63.1 %collective-permute-start.49 = (bf16[128,512]{1,0:T(8,128)(2,1)S(1)}, bf16[128,512]{1,0:T(8,128)(2,1)S(1)}, u32[]{:S(2)}, u32[]{:S(2)}) collective-permute-start(bf16[128,512]{1,0:T(8,128)(2,1)S(1)} %slice.397), channel_id=1, source_target_pairs={{0,4},{1,5},{2,6},{3,7},{4,0},{5,1},{6,2},{7,3},{8,12},{9,13},{10,... | collective-permute-start | bytes 393224 | tf_op jit(solution)/shard_map/ppermute | solution.py:60
  306.1 35.4 %collective-permute-start.41 = (bf16[256,1792]{1,0:T(8,128)(2,1)S(1)}, bf16[256,1792]{1,0:T(8,128)(2,1)S(1)}, u32[]{:S(2)}, u32[]{:S(2)}) collective-permute-start(bf16[256,1792]{1,0:T(8,128)(2,1)S(1)} %convolution_convert_fusion.1), channel_id=1, source_target_pairs={{0,24},{1,25},{2,26},{3,27},{4,28},{5,29},{6,30},{7,31},{8,16},{9,... | collective-permute-start | bytes 2752520 | tf_op jit(solution)/shard_map/ppermute | solution.py:60
  319.2 54.6 %collective-permute-start.30 = (bf16[256,1792]{1,0:T(8,128)(2,1)S(1)}, bf16[256,1792]{1,0:T(8,128)(2,1)S(1)}, u32[]{:S(2)}, u32[]{:S(2)}) collective-permute-start(bf16[256,1792]{1,0:T(8,128)(2,1)S(1)} %convolution_convert_fusion.2), channel_id=1, source_target_pairs={{0,16},{1,17},{2,18},{3,19},{4,20},{5,21},{6,22},{7,23},{8,24},{9,... | collective-permute-start | bytes 2752520 | tf_op jit(solution)/shard_map/ppermute | solution.py:60
  333.0 40.8 %collective-permute-start.19 = (bf16[256,1792]{1,0:T(8,128)(2,1)S(1)}, bf16[256,1792]{1,0:T(8,128)(2,1)S(1)}, u32[]{:S(2)}, u32[]{:S(2)}) collective-permute-start(bf16[256,1792]{1,0:T(8,128)(2,1)S(1)} %convolution_convert_fusion.3), channel_id=1, source_target_pairs={{0,8},{1,9},{2,10},{3,11},{4,12},{5,13},{6,14},{7,15},{8,0},{9,1},... | collective-permute-start | bytes 2752520 | tf_op jit(solution)/shard_map/ppermute | solution.py:60
  (31 other events, 391.8 us)

commit v2 on v0

--- a/solution.py
+++ b/solution.py
@@ -1,12 +1,15 @@
 import jax
 import jax.numpy as jnp
 from jax import lax
+from jax.experimental import pallas as pl
+from jax.experimental.pallas import tpu as pltpu
 from jax.sharding import PartitionSpec as P
 
 GROUP = 8
-
-
-def per_device(tokens, routes, probs, w_gate, w_up, w_down):
+PLANES = 4
+
+
+def general(tokens, routes, probs, w_gate, w_up, w_down):
     tok_rows, width = tokens.shape
     chosen_count = routes.shape[1]
     devices = lax.axis_size("node")
@@ -51,7 +54,238 @@
     return mixed.astype(jnp.bfloat16)
 
 
+CORE, X, Y, Z = 1, 2, 4, 8
+COUNT = PLANES * GROUP
+
+
+def swap(value, bits):
+    return lax.ppermute(value, "node", [(i, i ^ bits) for i in range(COUNT)])
+
+
+VMEM = 56 * 2**20
+
+
+def shift(value, by, planes):
+    moves = ((1, 0), (2, 3)) if by is None else [(p, p + by) for p in planes]
+    return lax.ppermute(
+        value,
+        "node",
+        [(p * GROUP + m, q * GROUP + m) for p, q in moves for m in range(GROUP)],
+    )
+
+
+def swiglu_kernel(own, by_x, by_y, low, high, gate_a, gate_b, up_a, up_b, out, gate, up):
+    step = pl.program_id(0)
+
+    @pl.when(step == 0)
+    def _():
+        gate[...] = jnp.zeros_like(gate)
+        up[...] = jnp.zeros_like(up)
+
+    block = jnp.concatenate([own[...], by_x[...], by_y[...], low[...], high[...]], axis=0)
+    gate_w = jnp.concatenate([gate_a[...], gate_b[...]], axis=1)
+    up_w = jnp.concatenate([up_a[...], up_b[...]], axis=1)
+    gate[...] += jnp.dot(block, gate_w, preferred_element_type=jnp.float32)
+    up[...] += jnp.dot(block, up_w, preferred_element_type=jnp.float32)
+
+    @pl.when(step == pl.num_programs(0) - 1)
+    def _():
+        out[...] = (jax.nn.silu(gate[...]) * up[...]).astype(out.dtype)
+
+
+def swiglu(pieces, weights):
+    rows = sum(n for p, n, place in pieces)
+    width = pieces[0][0].shape[1]
+    hidden = sum(w.shape[1] for w in weights) // 2
+    depth = width // 7
+    return pl.pallas_call(
+        swiglu_kernel,
+        out_shape=jax.ShapeDtypeStruct((rows, hidden), jnp.bfloat16),
+        grid=(7,),
+        in_specs=[
+            pl.BlockSpec((n, depth), lambda i, place=place: (place, i))
+            for p, n, place in pieces
+        ]
+        + [pl.BlockSpec((depth, w.shape[1]), lambda i: (i, 0)) for w in weights],
+        out_specs=pl.BlockSpec((rows, hidden), lambda i: (0, 0)),
+        scratch_shapes=[pltpu.VMEM((rows, hidden), jnp.float32)] * 2,
+        compiler_params=pltpu.CompilerParams(vmem_limit_bytes=VMEM),
+        cost_estimate=pl.CostEstimate(flops=1000, bytes_accessed=1000, transcendentals=0),
+    )(*[p for p, n, place in pieces], *weights)
+
+
+def down_kernel(own, by_x, by_y, across, mine, other, out, hidden):
+    rows = own.shape[0] // 4
+    half = own.shape[1] // 2
+
+    @pl.when(pl.program_id(0) == 0)
+    def _():
+        for r, unit in enumerate((own, by_x, by_y, across)):
+            for j in range(4):
+                block = unit[(j ^ r) * rows : (j ^ r) * rows + rows]
+                for h in range(2):
+                    hidden[
+                        j * rows : j * rows + rows, (h * 4 + r) * half : (h * 4 + r + 1) * half
+                    ] = block[:, h * half : (h + 1) * half]
+
+    total = jnp.dot(hidden[:, : 4 * half], mine[...], preferred_element_type=jnp.float32)
+    total += jnp.dot(hidden[:, 4 * half :], other[...], preferred_element_type=jnp.float32)
+    out[...] = total.astype(out.dtype)
+
+
+def down(pieces, weights):
+    rows, hidden = pieces[0].shape
+    width = weights[0].shape[1]
+    cols = width // 2
+    return pl.pallas_call(
+        down_kernel,
+        out_shape=jax.ShapeDtypeStruct((rows, width), jnp.bfloat16),
+        grid=(2,),
+        in_specs=[pl.BlockSpec(p.shape, lambda i: (0, 0)) for p in pieces]
+        + [pl.BlockSpec((w.shape[0], cols), lambda i: (0, i)) for w in weights],
+        out_specs=pl.BlockSpec((rows, cols), lambda i: (0, i)),
+        scratch_shapes=[pltpu.VMEM((rows, 4 * hidden), jnp.bfloat16)],
+        compiler_params=pltpu.CompilerParams(vmem_limit_bytes=VMEM),
+        cost_estimate=pl.CostEstimate(
+            flops=1000,
+            bytes_accessed=1000,
+            transcendentals=0,
+        ),
+    )(*pieces, *weights)
+
+
+def nothing(*refs):
+    pass
+
+
+def after(values, *earlier):
+    values = tuple(values)
+    return pl.pallas_call(
+        nothing,
+        out_shape=[jax.ShapeDtypeStruct(v.shape, v.dtype) for v in values],
+        in_specs=[pl.BlockSpec(memory_space=pl.ANY)] * (len(values) + len(earlier)),
+        out_specs=[pl.BlockSpec(memory_space=pl.ANY)] * len(values),
+        input_output_aliases={i: i for i in range(len(values))},
+        compiler_params=pltpu.CompilerParams(vmem_limit_bytes=2**20),
+        cost_estimate=pl.CostEstimate(flops=0, bytes_accessed=0, transcendentals=0),
+    )(*values, *earlier)
+
+
+def four_planes(tokens, routes, probs, w_gate, w_up, w_down):
+    rows, width = tokens.shape
+    part = width // 4
+    half = rows // 2
+    me = lax.axis_index("node")
+    z = me // GROUP
+    quarter = me // 2 % 4
+    chain = [jnp.zeros((8, 128), jnp.float32)]
+
+    def gate(values, *earlier):
+        chain[0], *values = after([chain[0], *values], *earlier)
+        return values
+
+    def cut(r):
+        return lax.dynamic_slice_in_dim(w_down[0], (quarter ^ r) * part, part, axis=1)
+
+    experts = jnp.arange(PLANES, dtype=jnp.int32)
+    weights = jnp.sum(
+        jnp.where(routes[:, :, None] == experts, probs[:, :, None], 0.0), axis=1
+    )
+
+    up1, dn1 = shift(tokens, 1, (0, 1, 2)), shift(tokens, -1, (1, 2, 3))
+    down_x, down_y = swap(cut(1), X), swap(cut(2), Y)
+    gate_b, up_b = swap(w_gate[0], CORE), swap(w_up[0], CORE)
+
+    up1, dn1, piece = gate([up1, dn1, cut(3)], down_x, down_y)
+    up2, dn2, down_d = shift(up1, 1, (1, 2)), shift(dn1, -1, (1, 2)), swap(piece, X + Y)
+
+    col = {0: tokens, 1: jnp.where(z % 2 == 0, dn1, up1), 2: jnp.where(z < 2, dn2, up2)}
+    onward = jnp.where(z == 2, up2, dn2)
+    mx, onward, down_x = gate([col[2], onward, down_x], down_d, gate_b)
+    col[2] = mx
+    x2, y2 = swap(mx, X), swap(mx, Y)
+    ends = shift(onward, None, None)
+    down_mine = jnp.concatenate([cut(0), down_x, down_y, down_d], axis=0)
+    down_w = [down_mine, swap(down_mine, CORE)]
+    col[3] = jnp.where((z == 0) | (z == 3), ends, jnp.where(z == 1, dn1, up1))
+    swiglu_w = [w_gate[0], gate_b, w_up[0], up_b]
+
+    def join(ahead, by_x, by_y):
+        low, high = by_x[:half], by_y[half:rows]
+        if ahead is None:
+            return high, low
+        return jnp.concatenate([ahead, high], axis=0), jnp.concatenate([ahead, low], axis=0)
+
+    def rows_of(k, by_x, by_y, by_x_later, by_y_later):
+        place = (by_x_later.shape[0] - half) // half
+        return [(col[k], rows, 0), (by_x, rows, 0), (by_y, rows, 0)] + [
+            (by_y_later, half, place),
+            (by_x_later, half, place),
+        ]
+
+    def spread(hidden):
+        (hidden,) = gate([hidden])
+        return [hidden, swap(hidden, X), swap(hidden, Y), swap(hidden, X + Y)]
+
+    def send_back(units, k):
+        (units[0],) = gate([units[0]])
+        out = down(units, down_w)
+        low, high = gate([out[: 2 * rows], out[2 * rows :]])
+        return swap(low, k * Z), swap(high, k * Z)
+
+    sums = {}
+    mx, my, w_0 = gate([*join(col[3], x2, y2), weights], down_w[1], up_b)
+    x3, y3 = swap(mx, X), swap(my, Y)
+    w_x, w_y, w_d = swap(w_0, X), swap(w_0, Y), swap(w_0, X + Y)
+
+    mx, my = gate(join(col[1], x3, y3), w_x, w_y, w_d)
+    x1, y1 = swap(mx, X), swap(my, Y)
+    (mark,) = gate([x2])
+    all_2 = spread(swiglu(rows_of(2, mark, y2, x3, y3), swiglu_w))
+
+    mx, my, all_2[0] = gate([*join(tokens, x1, y1), all_2[0]], *all_2[1:])
+    x0, y0 = swap(mx, X), swap(my, Y)
+    sums[2] = send_back(all_2, 2)
+    (mark,) = gate([x3])
+    all_3 = spread(swiglu(rows_of(3, mark, y3, x1, y1), swiglu_w))
+
+    mx, my, all_3[0] = gate([*join(None, x0, y0), all_3[0]], sums[2][0], *all_3[1:])
+    xe, ye = swap(mx, X), swap(my, Y)
+    sums[3] = send_back(all_3, 3)
+    (mark,) = gate([x1])
+    all_1 = spread(swiglu(rows_of(1, mark, y1, x0, y0), swiglu_w))
+
+    (ye,) = gate([ye], xe, sums[2][1], sums[3][0], *all_1[1:])
+    all_0 = spread(swiglu(rows_of(0, x0, y0, xe, ye), swiglu_w))
+    sums[1] = send_back(all_1, 1)
+    (all_0[0],) = gate([all_0[0]], *all_0[1:])
+    sums[0] = (down(all_0, down_w),)
+    order = (2, 3, 1, 0)
+    sums = {k: jnp.concatenate(sums[k], axis=0) for k in order}
+
+    weights = jnp.concatenate([w_0, w_x, w_y, w_d], axis=0)
+    total = 0.0
+    for k in order:
+        weight = jnp.sum(jnp.where(experts == (z ^ k), weights, 0.0), axis=1, keepdims=True)
+        total = total + weight * sums[k].astype(jnp.float32)
+    mixed = total.astype(jnp.bfloat16).reshape(4, rows, part)
+    pieces = [mixed[0], swap(mixed[1], X), swap(mixed[2], Y), swap(mixed[3], X + Y)]
+    result = []
+    for a in range(4):
+        piece = pieces[a]
+        for q in range(1, 4):
+            piece = jnp.where(quarter == q, pieces[a ^ q], piece)
+        result.append(piece)
+    return jnp.concatenate(result, axis=1)
+
+
 def solution(mesh):
+    devices = mesh.shape["node"]
+
+    def per_device(tokens, routes, probs, w_gate, w_up, w_down):
+        path = four_planes if devices == COUNT else general
+        return path(tokens, routes, probs, w_gate, w_up, w_down)
+
     in_specs = (
         P(("rep", "node"), None),
         P(("rep", "node"), None),

time: 2000 us -> 320 us (0.16)
  blocking collectives: 1910 us -> 0 us
  waiting for transfers between devices: 0 us -> 158 us
  Pallas kernels: 0 us -> 66 us
  matrix products: 55 us -> 0 us
  starting transfers between devices: 0 us -> 54.9 us
    all_to_all x2 -> x0, blocking collectives: 1910 us -> none  [the longest x1 1270 us: per_device(): lax.all_to_all(jnp.dot(hidden, w_down[0], preferred_element_type=jnp.floa...]
    ppermute x0 -> x45, waiting for transfers between devices: none -> 158 us  [the longest x40 126 us: swap(): return lax.ppermute(value, 'node', [(i, i ^ bits) for i in range(COUNT)])]
    pallas_call x0 -> x29, Pallas kernels: none -> 66 us  [the longest x4 42.8 us: swiglu(): pl.pallas_call(swiglu_kernel, out_shape=jax.ShapeDtypeStruct((rows, hidde...]
    dot_general x5 -> x0, matrix products: 55 us -> none  [the longest x1 21.3 us: per_device(): jnp.dot(hidden, w_down[0], preferred_element_type=jnp.float32)]
    ppermute x0 -> x45, starting transfers between devices: none -> 54.9 us  [the longest x40 45.9 us: swap(): return lax.ppermute(value, 'node', [(i, i ^ bits) for i in range(COUNT)])]
    reduce_sum x3 -> x2, other arithmetic: 22.1 us -> 0.15 us  [the longest x1 0.13 us: four_planes(): jnp.sum(jnp.where(experts == z ^ k, weights, 0.0), axis=1, keepdims=True)]
  transfers between devices with their start and end apart: 0 -> 45, of which waited for: 0 -> 24; matrix products, arithmetic and copies ran while one was open for 0% -> 5% of each run, Pallas kernels for 0% -> 21%
where the time goes in v2:
time: 320 us; the launch traced here: 319 us
  waiting for transfers between devices  158 us (49%)
  Pallas kernels  66 us (21%)
  starting transfers between devices  54.9 us (17%)
  local copies, waits for them, and re-layouts  28.7 us (9%)
  other arithmetic  10.7 us (3%)
    ppermute x40, waiting for transfers between devices, swap(): return lax.ppermute(value, 'node', [(i, i ^ bits) for i in range(COUNT)])  126 us
    ppermute x40, starting transfers between devices, swap(): return lax.ppermute(value, 'node', [(i, i ^ bits) for i in range(COUNT)])  45.9 us
    pallas_call x4, Pallas kernels, swiglu(): pl.pallas_call(swiglu_kernel, out_shape=jax.ShapeDtypeStruct((rows, hidde...  42.8 us
    ppermute x5, waiting for transfers between devices, shift(): lax.ppermute(value, 'node', [(p * GROUP + m, q * GROUP + m) for p, q in m...  31.8 us
    pallas_call x4, Pallas kernels, down(): pl.pallas_call(down_kernel, out_shape=jax.ShapeDtypeStruct((rows, width),...  23.3 us
    unnamed x96, local copies, waits for them, and re-layouts  18.5 us
    ppermute x5, starting transfers between devices, shift(): lax.ppermute(value, 'node', [(p * GROUP + m, q * GROUP + m) for p, q in m...  8.97 us
  transfers between devices with their start and end apart: 45, of which 24 were waited for; matrix products, arithmetic and copies ran while one was open for 5% of the time, Pallas kernels for 21%

profile of v2, /device:TPU:0, one launch (start us, length us, event | category | flops | bytes accessed | tf_op | source)
XLA Modules:
  0.0 319.0 jit_solution(2194844761464515922)
XLA Ops:
  0.5 3.6 %dynamic-slice_bitcast_fusion = (bf16[256,1792]{1,0:T(8,128)(2,1)}, bf16[256,1792]{1,0:T(8,128)(2,1)S(1)}, bf16[256,1792]{1,0:T(8,128)(2,1)}, bf16[256,1792]{1,0:T(8,128)(2,1)S(1)}) fusion(bf16[1,256,7168]{2,1,0:T(8,128)(2,1)} %param.11, s32[]{:T(128)S(6)} %select_n.151, s32[]{:T(128)S(6)} %select_n.140, s32[]{:T(128)S(6)} %select_n.139, s32[]{:T(128)S(6)} %select_n.141), kind=kLoop, calls=%fused_computation.9 | loop fusion | bytes 7340048 | tf_op jit(solution)/shard_map/dynamic_slice | solution.py:188
  8.0 3.5 %collective-permute-start = (bf16[64,7168]{1,0:T(8,128)(2,1)S(1)}, bf16[64,7168]{1,0:T(8,128)(2,1)S(1)}, u32[]{:S(2)}, u32[]{:S(2)}) collective-permute-start(bf16[64,7168]{1,0:T(8,128)(2,1)S(1)} %copy-done.44), channel_id=1, source_target_pairs={{0,8},{1,9},{2,10},{3,11},{4,12},{5,13},{6,14},{7,15},{8,16},{9,17... | collective-permute-start | bytes 2752520 | tf_op jit(solution)/shard_map/ppermute | solution.py:70
  12.9 14.7 %collective-permute-done.2.refs_4_.refs_3_ = bf16[256,1792]{1,0:T(8,128)(2,1)S(1)} collective-permute-done((bf16[256,1792]{1,0:T(8,128)(2,1)S(1)}, bf16[256,1792]{1,0:T(8,128)(2,1)S(1)}, u32[]{:S(2)}, u32[]{:S(2)}) %collective-permute-start.2) | collective-permute-done | bytes 917536 | tf_op jit(solution)/shard_map/ppermute | solution.py:62
  31.2 4.3 %collective-permute-done.1.refs_2_ = bf16[64,7168]{1,0:T(8,128)(2,1)} collective-permute-done((bf16[64,7168]{1,0:T(8,128)(2,1)S(1)}, bf16[64,7168]{1,0:T(8,128)(2,1)}, u32[]{:S(2)}, u32[]{:S(2)}) %collective-permute-start.1) | collective-permute-done | bytes 917536 | tf_op jit(solution)/shard_map/ppermute | solution.py:70
  38.9 19.9 %collective-permute-done.4 = bf16[64,7168]{1,0:T(8,128)(2,1)} collective-permute-done((bf16[64,7168]{1,0:T(8,128)(2,1)}, bf16[64,7168]{1,0:T(8,128)(2,1)}, u32[]{:S(2)}, u32[]{:S(2)}) %collective-permute-start.4) | collective-permute-done | bytes 917536 | tf_op jit(solution)/shard_map/ppermute | solution.py:70
  68.3 20.4 %collective-permute-done.9.by_y = bf16[64,7168]{1,0:T(8,128)(2,1)} collective-permute-done((bf16[64,7168]{1,0:T(8,128)(2,1)S(1)}, bf16[64,7168]{1,0:T(8,128)(2,1)}, u32[]{:S(2)}, u32[]{:S(2)}) %collective-permute-start.9) | collective-permute-done | bytes 917536 | tf_op jit(solution)/shard_map/ppermute | solution.py:62
  89.8 5.4 %collective-permute-done.8 = bf16[64,7168]{1,0:T(8,128)(2,1)} collective-permute-done((bf16[64,7168]{1,0:T(8,128)(2,1)}, bf16[64,7168]{1,0:T(8,128)(2,1)}, u32[]{:S(2)}, u32[]{:S(2)}) %collective-permute-start.8) | collective-permute-done | bytes 917536 | tf_op jit(solution)/shard_map/ppermute | solution.py:70
  104.3 25.7 %collective-permute-done.16.low.by_y = bf16[96,7168]{1,0:T(8,128)(2,1)S(1)} collective-permute-done((bf16[96,7168]{1,0:T(8,128)(2,1)S(1)}, bf16[96,7168]{1,0:T(8,128)(2,1)S(1)}, u32[]{:S(2)}, u32[]{:S(2)}) %collective-permute-start.16) | collective-permute-done | bytes 1376288 | tf_op jit(solution)/shard_map/ppermute | solution.py:62
  135.8 10.7 %shard_map.69.refs_1_ = bf16[256,512]{1,0:T(8,128)(2,1)} custom-call(bf16[64,7168]{1,0:T(8,128)(2,1)} %copy-done.6, bf16[64,7168]{1,0:T(8,128)(2,1)} %copy-done.15, bf16[64,7168]{1,0:T(8,128)(2,1)} %collective-permute-done.9.by_y, bf16[96,7168]{1,0:T(8,128)(2,1)} %copy-done.41, bf16[96,7168]{1,0:T(8,128)(2,1)} %copy-done, bf16[7168,256]{1,0:T(8,128)(2,1)} %bitcast.11, ...), custom_call_target="tpu_custom_call" | custom-call | flops 1000 | bytes 1000 | tf_op jit(solution)/shard_map/pallas_call | solution.py:101
  151.7 13.2 %collective-permute-done.18.low.by_y = bf16[96,7168]{1,0:T(8,128)(2,1)S(1)} collective-permute-done((bf16[96,7168]{1,0:T(8,128)(2,1)S(1)}, bf16[96,7168]{1,0:T(8,128)(2,1)S(1)}, u32[]{:S(2)}, u32[]{:S(2)}) %collective-permute-start.18) | collective-permute-done | bytes 1376288 | tf_op jit(solution)/shard_map/ppermute | solution.py:62
  167.7 3.9 %collective-permute-done.20.refs_4_.by_x = bf16[256,512]{1,0:T(8,128)(2,1)S(1)} collective-permute-done((bf16[256,512]{1,0:T(8,128)(2,1)}, bf16[256,512]{1,0:T(8,128)(2,1)S(1)}, u32[]{:S(2)}, u32[]{:S(2)}) %collective-permute-start.20) | collective-permute-done | bytes 262176 | tf_op jit(solution)/shard_map/ppermute | solution.py:62
  178.8 5.9 %shard_map.73 = bf16[256,1792]{1,0:T(8,128)(2,1)} custom-call(bf16[256,512]{1,0:T(8,128)(2,1)} %copy-done.10, bf16[256,512]{1,0:T(8,128)(2,1)} %copy-done.30, bf16[256,512]{1,0:T(8,128)(2,1)} %copy-done.31, bf16[256,512]{1,0:T(8,128)(2,1)} %copy-done.33, bf16[1024,1792]{1,0:T(8,128)(2,1)} %pad_maximum_fusion.mine, ...), custom_call_target="tpu_custom_call" | custom-call | flops 1000 | bytes 1000 | tf_op jit(solution)/shard_map/pallas_call | solution.py:140
  187.4 10.7 %shard_map.76.refs_1_ = bf16[256,512]{1,0:T(8,128)(2,1)} custom-call(bf16[64,7168]{1,0:T(8,128)(2,1)} %copy-done.39, bf16[96,7168]{1,0:T(8,128)(2,1)} %copy-done.2, bf16[96,7168]{1,0:T(8,128)(2,1)} %copy-done.41, bf16[96,7168]{1,0:T(8,128)(2,1)} %copy-done.42, bf16[96,7168]{1,0:T(8,128)(2,1)} %copy-done.3, bf16[7168,256]{1,0:T(8,128)(2,1)} %bitcast.12, ...), custom_call_target="tpu_custom_call" | custom-call | flops 1000 | bytes 1000 | tf_op jit(solution)/shard_map/pallas_call | solution.py:101
  201.0 7.8 %collective-permute-done.25.low.by_y = bf16[96,7168]{1,0:T(8,128)(2,1)S(1)} collective-permute-done((bf16[96,7168]{1,0:T(8,128)(2,1)S(1)}, bf16[96,7168]{1,0:T(8,128)(2,1)S(1)}, u32[]{:S(2)}, u32[]{:S(2)}) %collective-permute-start.25) | collective-permute-done | bytes 1376288 | tf_op jit(solution)/shard_map/ppermute | solution.py:62
  217.1 5.8 %shard_map.80 = bf16[256,1792]{1,0:T(8,128)(2,1)} custom-call(bf16[256,512]{1,0:T(8,128)(2,1)} %copy-done.14, bf16[256,512]{1,0:T(8,128)(2,1)} %copy-done.34, bf16[256,512]{1,0:T(8,128)(2,1)} %copy-done.35, bf16[256,512]{1,0:T(8,128)(2,1)} %copy-done.36, bf16[1024,1792]{1,0:T(8,128)(2,1)} %pad_maximum_fusion.mine, ...), custom_call_target="tpu_custom_call" | custom-call | flops 1000 | bytes 1000 | tf_op jit(solution)/shard_map/pallas_call | solution.py:140
  225.6 10.7 %shard_map.83.refs_1_ = bf16[256,512]{1,0:T(8,128)(2,1)} custom-call(bf16[64,7168]{1,0:T(8,128)(2,1)} %copy-done.38, bf16[96,7168]{1,0:T(8,128)(2,1)} %copy-done.5, bf16[96,7168]{1,0:T(8,128)(2,1)} %copy-done.42, bf16[96,7168]{1,0:T(8,128)(2,1)} %copy-done.40, bf16[96,7168]{1,0:T(8,128)(2,1)} %collective-permute-done.26.high.by_x, ...), custom_call_target="tpu_custom_call" | custom-call | flops 1000 | bytes 1000 | tf_op jit(solution)/shard_map/pallas_call | solution.py:101
  242.0 5.4 %collective-permute-done.34.refs_5_.by_x = bf16[256,512]{1,0:T(8,128)(2,1)S(1)} collective-permute-done((bf16[256,512]{1,0:T(8,128)(2,1)}, bf16[256,512]{1,0:T(8,128)(2,1)S(1)}, u32[]{:S(2)}, u32[]{:S(2)}) %collective-permute-start.34) | collective-permute-done | bytes 262176 | tf_op jit(solution)/shard_map/ppermute | solution.py:62
  249.6 9.0 %collective-permute-done.35.refs_6_.by_y = bf16[256,512]{1,0:T(8,128)(2,1)S(1)} collective-permute-done((bf16[256,512]{1,0:T(8,128)(2,1)}, bf16[256,512]{1,0:T(8,128)(2,1)S(1)}, u32[]{:S(2)}, u32[]{:S(2)}) %collective-permute-start.35) | collective-permute-done | bytes 262176 | tf_op jit(solution)/shard_map/ppermute | solution.py:62
  261.8 10.7 %shard_map.86.refs_1_ = bf16[256,512]{1,0:T(8,128)(2,1)} custom-call(bf16[64,7168]{1,0:T(8,128)(2,1)} %own.1, bf16[96,7168]{1,0:T(8,128)(2,1)} %collective-permute-done.26.high.by_x, bf16[96,7168]{1,0:T(8,128)(2,1)} %copy-done.40, bf16[32,7168]{1,0:T(8,128)(2,1)} %copy-done.27, bf16[32,7168]{1,0:T(8,128)(2,1)} %copy-done.26, bf16[7168,256]{1,0:T(8,128)(2,1)} %bitcast.14, ...), custom_call_target="tpu_custom_call" | custom-call | flops 1000 | bytes 1000 | tf_op jit(solution)/shard_map/pallas_call | solution.py:101
  275.4 5.8 %shard_map.89 = bf16[256,1792]{1,0:T(8,128)(2,1)} custom-call(bf16[256,512]{1,0:T(8,128)(2,1)} %copy-done.23, bf16[256,512]{1,0:T(8,128)(2,1)} %copy-done.28, bf16[256,512]{1,0:T(8,128)(2,1)} %copy-done.29, bf16[256,512]{1,0:T(8,128)(2,1)} %copy-done.32, bf16[1024,1792]{1,0:T(8,128)(2,1)} %pad_maximum_fusion.mine, ...), custom_call_target="tpu_custom_call" | custom-call | flops 1000 | bytes 1000 | tf_op jit(solution)/shard_map/pallas_call | solution.py:140
  285.8 5.9 %collective-permute-start.40 = (bf16[256,512]{1,0:T(8,128)(2,1)S(1)}, bf16[256,512]{1,0:T(8,128)(2,1)}, u32[]{:S(2)}, u32[]{:S(2)}) collective-permute-start(bf16[256,512]{1,0:T(8,128)(2,1)S(1)} %copy-done.18), channel_id=1, source_target_pairs={{0,4},{1,5},{2,6},{3,7},{4,0},{5,1},{6,2},{7,3},{8,12},{9,13},{10,... | collective-permute-start | bytes 786440 | tf_op jit(solution)/shard_map/ppermute | solution.py:62
  292.1 6.2 %collective-permute-done.40.refs_3_.by_y = bf16[256,512]{1,0:T(8,128)(2,1)} collective-permute-done((bf16[256,512]{1,0:T(8,128)(2,1)S(1)}, bf16[256,512]{1,0:T(8,128)(2,1)}, u32[]{:S(2)}, u32[]{:S(2)}) %collective-permute-start.40) | collective-permute-done | bytes 262176 | tf_op jit(solution)/shard_map/ppermute | solution.py:62
  299.7 5.8 %shard_map.92 = bf16[256,1792]{1,0:T(8,128)(2,1)} custom-call(bf16[256,512]{1,0:T(8,128)(2,1)} %copy-done.19, bf16[256,512]{1,0:T(8,128)(2,1)} %copy-done.37, bf16[256,512]{1,0:T(8,128)(2,1)} %collective-permute-done.40.refs_3_.by_y, bf16[256,512]{1,0:T(8,128)(2,1)} %collective-permute-done.41.refs_4_.across, bf16[1024,1792]{1,0:T(8,128)(2,1)} %pad_maximum_fusion.mine, ...), custom_call_target="tpu_custom_call" | custom-call | flops 1000 | bytes 1000 | tf_op jit(solution)/shard_map/pallas_call | solution.py:140
  311.5 3.5 %collective-permute-done.42 = bf16[64,1792]{1,0:T(8,128)(2,1)S(1)} collective-permute-done((bf16[64,1792]{1,0:T(8,128)(2,1)S(1)}, bf16[64,1792]{1,0:T(8,128)(2,1)S(1)}, u32[]{:S(2)}, u32[]{:S(2)}) %collective-permute-start.42) | collective-permute-done | bytes 229408 | tf_op jit(solution)/shard_map/ppermute | solution.py:62
  (223 shorter events, 100.2 us)
Async XLA Ops:
  0.0 62.3 %collective-permute-start.7 = (bf16[7168,256]{1,0:T(8,128)(2,1)}, bf16[7168,256]{1,0:T(8,128)(2,1)}, u32[]{:S(2)}, u32[]{:S(2)}) collective-permute-start(bf16[7168,256]{1,0:T(8,128)(2,1)} %bitcast.10), channel_id=1, source_target_pairs={{0,1},{1,0},{2,3},{3,2},{4,5},{5,4},{6,7},{7,6},{8,9},{9,8},{10,11... | collective-permute-start | bytes 11010056 | tf_op jit(solution)/shard_map/ppermute | solution.py:62
  4.0 23.5 %collective-permute-start.2 = (bf16[256,1792]{1,0:T(8,128)(2,1)S(1)}, bf16[256,1792]{1,0:T(8,128)(2,1)S(1)}, u32[]{:S(2)}, u32[]{:S(2)}) collective-permute-start(bf16[256,1792]{1,0:T(8,128)(2,1)S(1)} %get-tuple-element.120), channel_id=1, source_target_pairs={{0,2},{1,3},{2,0},{3,1},{4,6},{5,7},{6,4},{7,5},{8,10},{9,11},{10,... | collective-permute-start | bytes 2752520 | tf_op jit(solution)/shard_map/ppermute | solution.py:62
  8.0 23.2 %collective-permute-start = (bf16[64,7168]{1,0:T(8,128)(2,1)S(1)}, bf16[64,7168]{1,0:T(8,128)(2,1)S(1)}, u32[]{:S(2)}, u32[]{:S(2)}) collective-permute-start(bf16[64,7168]{1,0:T(8,128)(2,1)S(1)} %copy-done.44), channel_id=1, source_target_pairs={{0,8},{1,9},{2,10},{3,11},{4,12},{5,13},{6,14},{7,15},{8,16},{9,17... | collective-permute-start | bytes 2752520 | tf_op jit(solution)/shard_map/ppermute | solution.py:70
  11.6 23.9 %collective-permute-start.1 = (bf16[64,7168]{1,0:T(8,128)(2,1)S(1)}, bf16[64,7168]{1,0:T(8,128)(2,1)}, u32[]{:S(2)}, u32[]{:S(2)}) collective-permute-start(bf16[64,7168]{1,0:T(8,128)(2,1)S(1)} %copy-done.44), channel_id=1, source_target_pairs={{8,0},{9,1},{10,2},{11,3},{12,4},{13,5},{14,6},{15,7},{16,8},{17,9... | collective-permute-start | bytes 2752520 | tf_op jit(solution)/shard_map/ppermute | solution.py:70
  35.5 23.2 %collective-permute-start.4 = (bf16[64,7168]{1,0:T(8,128)(2,1)}, bf16[64,7168]{1,0:T(8,128)(2,1)}, u32[]{:S(2)}, u32[]{:S(2)}) collective-permute-start(bf16[64,7168]{1,0:T(8,128)(2,1)} %get-tuple-element.61), channel_id=1, source_target_pairs={{8,0},{9,1},{10,2},{11,3},{12,4},{13,5},{14,6},{15,7},{16,8},{17,9... | collective-permute-start | bytes 2752520 | tf_op jit(solution)/shard_map/ppermute | solution.py:70
  38.4 59.4 %collective-permute-start.12 = (bf16[7168,256]{1,0:T(8,128)(2,1)}, bf16[7168,256]{1,0:T(8,128)(2,1)}, u32[]{:S(2)}, u32[]{:S(2)}) collective-permute-start(bf16[7168,256]{1,0:T(8,128)(2,1)} %bitcast.5.up_a), channel_id=1, source_target_pairs={{0,1},{1,0},{2,3},{3,2},{4,5},{5,4},{6,7},{7,6},{8,9},{9,8},{10,11... | collective-permute-start | bytes 11010056 | tf_op jit(solution)/shard_map/ppermute | solution.py:62
  38.4 23.9 %collective-permute-start.6 = (bf16[256,1792]{1,0:T(8,128)(2,1)}, bf16[256,1792]{1,0:T(8,128)(2,1)S(1)}, u32[]{:S(2)}, u32[]{:S(2)}) collective-permute-start(bf16[256,1792]{1,0:T(8,128)(2,1)} %get-tuple-element.63), channel_id=1, source_target_pairs={{0,6},{1,7},{2,4},{3,5},{4,2},{5,3},{6,0},{7,1},{8,14},{9,15},{10,... | collective-permute-start | bytes 2752520 | tf_op jit(solution)/shard_map/ppermute | solution.py:62
  65.8 32.0 %collective-permute-start.11 = (bf16[1024,1792]{1,0:T(8,128)(2,1)}, bf16[1024,1792]{1,0:T(8,128)(2,1)}, u32[]{:S(2)}, u32[]{:S(2)}) collective-permute-start(bf16[1024,1792]{1,0:T(8,128)(2,1)} %pad_maximum_fusion.mine), channel_id=1, source_target_pairs={{0,1},{1,0},{2,3},{3,2},{4,5},{5,4},{6,7},{7,6},{8,9},{9,8},{10,11... | collective-permute-start | bytes 11010056 | tf_op jit(solution)/shard_map/ppermute | solution.py:62
  66.3 23.4 %collective-permute-start.10 = (bf16[64,7168]{1,0:T(8,128)(2,1)S(1)}, bf16[64,7168]{1,0:T(8,128)(2,1)S(1)}, u32[]{:S(2)}, u32[]{:S(2)}) collective-permute-start(bf16[64,7168]{1,0:T(8,128)(2,1)S(1)} %get-tuple-element.66.own), channel_id=1, source_target_pairs={{0,2},{1,3},{2,0},{3,1},{4,6},{5,7},{6,4},{7,5},{8,10},{9,11},{10,... | collective-permute-start | bytes 2752520 | tf_op jit(solution)/shard_map/ppermute | solution.py:62
  66.9 28.4 %collective-permute-start.8 = (bf16[64,7168]{1,0:T(8,128)(2,1)}, bf16[64,7168]{1,0:T(8,128)(2,1)}, u32[]{:S(2)}, u32[]{:S(2)}) collective-permute-start(bf16[64,7168]{1,0:T(8,128)(2,1)} %get-tuple-element.65), channel_id=1, source_target_pairs={{8,0},{9,1},{10,2},{11,3},{12,4},{13,5},{14,6},{15,7},{16,24},{17,... | collective-permute-start | bytes 2752520 | tf_op jit(solution)/shard_map/ppermute | solution.py:70
  97.8 32.2 %collective-permute-start.16 = (bf16[96,7168]{1,0:T(8,128)(2,1)S(1)}, bf16[96,7168]{1,0:T(8,128)(2,1)S(1)}, u32[]{:S(2)}, u32[]{:S(2)}) collective-permute-start(bf16[96,7168]{1,0:T(8,128)(2,1)S(1)} %get-tuple-element.70), channel_id=1, source_target_pairs={{0,4},{1,5},{2,6},{3,7},{4,0},{5,1},{6,2},{7,3},{8,12},{9,13},{10,... | collective-permute-start | bytes 4128776 | tf_op jit(solution)/shard_map/ppermute | solution.py:62
  99.3 31.9 %collective-permute-start.17 = (bf16[96,7168]{1,0:T(8,128)(2,1)S(1)}, bf16[96,7168]{1,0:T(8,128)(2,1)S(1)}, u32[]{:S(2)}, u32[]{:S(2)}) collective-permute-start(bf16[96,7168]{1,0:T(8,128)(2,1)S(1)} %get-tuple-element.71), channel_id=1, source_target_pairs={{0,2},{1,3},{2,0},{3,1},{4,6},{5,7},{6,4},{7,5},{8,10},{9,11},{10,... | collective-permute-start | bytes 4128776 | tf_op jit(solution)/shard_map/ppermute | solution.py:62
  100.8 31.6 %collective-permute-start.13 = (f32[64,4]{1,0:T(8,128)S(1)}, f32[64,4]{1,0:T(8,128)S(1)}, u32[]{:S(2)}, u32[]{:S(2)}) collective-permute-start(f32[64,4]{1,0:T(8,128)S(1)} %get-tuple-element.68), channel_id=1, source_target_pairs={{0,2},{1,3},{2,0},{3,1},{4,6},{5,7},{6,4},{7,5},{8,10},{9,11},{10,... | collective-permute-start | bytes 3080 | tf_op jit(solution)/shard_map/ppermute | solution.py:62
  101.4 31.0 %collective-permute-start.14 = (f32[64,4]{1,0:T(8,128)S(1)}, f32[64,4]{1,0:T(8,128)S(1)}, u32[]{:S(2)}, u32[]{:S(2)}) collective-permute-start(f32[64,4]{1,0:T(8,128)S(1)} %get-tuple-element.68), channel_id=1, source_target_pairs={{0,4},{1,5},{2,6},{3,7},{4,0},{5,1},{6,2},{7,3},{8,12},{9,13},{10,... | collective-permute-start | bytes 3080 | tf_op jit(solution)/shard_map/ppermute | solution.py:62
  101.9 30.5 %collective-permute-start.15 = (f32[64,4]{1,0:T(8,128)S(1)}, f32[64,4]{1,0:T(8,128)S(1)}, u32[]{:S(2)}, u32[]{:S(2)}) collective-permute-start(f32[64,4]{1,0:T(8,128)S(1)} %get-tuple-element.68), channel_id=1, source_target_pairs={{0,6},{1,7},{2,4},{3,5},{4,2},{5,3},{6,0},{7,1},{8,14},{9,15},{10,... | collective-permute-start | bytes 3080 | tf_op jit(solution)/shard_map/ppermute | solution.py:62
  132.4 32.5 %collective-permute-start.18 = (bf16[96,7168]{1,0:T(8,128)(2,1)S(1)}, bf16[96,7168]{1,0:T(8,128)(2,1)S(1)}, u32[]{:S(2)}, u32[]{:S(2)}) collective-permute-start(bf16[96,7168]{1,0:T(8,128)(2,1)S(1)} %get-tuple-element.76), channel_id=1, source_target_pairs={{0,4},{1,5},{2,6},{3,7},{4,0},{5,1},{6,2},{7,3},{8,12},{9,13},{10,... | collective-permute-start | bytes 4128776 | tf_op jit(solution)/shard_map/ppermute | solution.py:62
  133.4 33.1 %collective-permute-start.19 = (bf16[96,7168]{1,0:T(8,128)(2,1)S(1)}, bf16[96,7168]{1,0:T(8,128)(2,1)S(1)}, u32[]{:S(2)}, u32[]{:S(2)}) collective-permute-start(bf16[96,7168]{1,0:T(8,128)(2,1)S(1)} %get-tuple-element.77), channel_id=1, source_target_pairs={{0,2},{1,3},{2,0},{3,1},{4,6},{5,7},{6,4},{7,5},{8,10},{9,11},{10,... | collective-permute-start | bytes 4128776 | tf_op jit(solution)/shard_map/ppermute | solution.py:62
  148.2 23.4 %collective-permute-start.20 = (bf16[256,512]{1,0:T(8,128)(2,1)}, bf16[256,512]{1,0:T(8,128)(2,1)S(1)}, u32[]{:S(2)}, u32[]{:S(2)}) collective-permute-start(bf16[256,512]{1,0:T(8,128)(2,1)} %copy-done.8), channel_id=1, source_target_pairs={{0,2},{1,3},{2,0},{3,1},{4,6},{5,7},{6,4},{7,5},{8,10},{9,11},{10,... | collective-permute-start | bytes 786440 | tf_op jit(solution)/shard_map/ppermute | solution.py:62
  149.8 24.7 %collective-permute-start.22 = (bf16[256,512]{1,0:T(8,128)(2,1)}, bf16[256,512]{1,0:T(8,128)(2,1)S(1)}, u32[]{:S(2)}, u32[]{:S(2)}) collective-permute-start(bf16[256,512]{1,0:T(8,128)(2,1)} %copy-done.8), channel_id=1, source_target_pairs={{0,6},{1,7},{2,4},{3,5},{4,2},{5,3},{6,0},{7,1},{8,14},{9,15},{10,... | collective-permute-start | bytes 786440 | tf_op jit(solution)/shard_map/ppermute | solution.py:62
  175.3 33.5 %collective-permute-start.25 = (bf16[96,7168]{1,0:T(8,128)(2,1)S(1)}, bf16[96,7168]{1,0:T(8,128)(2,1)S(1)}, u32[]{:S(2)}, u32[]{:S(2)}) collective-permute-start(bf16[96,7168]{1,0:T(8,128)(2,1)S(1)} %get-tuple-element.89), channel_id=1, source_target_pairs={{0,4},{1,5},{2,6},{3,7},{4,0},{5,1},{6,2},{7,3},{8,12},{9,13},{10,... | collective-permute-start | bytes 4128776 | tf_op jit(solution)/shard_map/ppermute | solution.py:62
  176.6 33.7 %collective-permute-start.26 = (bf16[96,7168]{1,0:T(8,128)(2,1)S(1)}, bf16[96,7168]{1,0:T(8,128)(2,1)}, u32[]{:S(2)}, u32[]{:S(2)}) collective-permute-start(bf16[96,7168]{1,0:T(8,128)(2,1)S(1)} %get-tuple-element.90), channel_id=1, source_target_pairs={{0,2},{1,3},{2,0},{3,1},{4,6},{5,7},{6,4},{7,5},{8,10},{9,11},{10,... | collective-permute-start | bytes 4128776 | tf_op jit(solution)/shard_map/ppermute | solution.py:62
  186.0 30.3 %collective-permute-start.23 = (bf16[128,1792]{1,0:T(8,128)(2,1)S(1)}, bf16[128,1792]{1,0:T(8,128)(2,1)S(1)}, u32[]{:S(2)}, u32[]{:S(2)}) collective-permute-start(bf16[128,1792]{1,0:T(8,128)(2,1)S(1)} %get-tuple-element.83), channel_id=1, source_target_pairs={{0,16},{1,17},{2,18},{3,19},{4,20},{5,21},{6,22},{7,23},{8,24},{9,... | collective-permute-start | bytes 1376264 | tf_op jit(solution)/shard_map/ppermute | solution.py:62
  210.3 30.9 %collective-permute-start.24 = (bf16[128,1792]{1,0:T(8,128)(2,1)S(1)}, bf16[128,1792]{1,0:T(8,128)(2,1)S(1)}, u32[]{:S(2)}, u32[]{:S(2)}) collective-permute-start(bf16[128,1792]{1,0:T(8,128)(2,1)S(1)} %get-tuple-element.84), channel_id=1, source_target_pairs={{0,16},{1,17},{2,18},{3,19},{4,20},{5,21},{6,22},{7,23},{8,24},{9,... | collective-permute-start | bytes 1376264 | tf_op jit(solution)/shard_map/ppermute | solution.py:62
  258.5 47.0 %collective-permute-start.31 = (bf16[128,1792]{1,0:T(8,128)(2,1)S(1)}, bf16[128,1792]{1,0:T(8,128)(2,1)}, u32[]{:S(2)}, u32[]{:S(2)}) collective-permute-start(bf16[128,1792]{1,0:T(8,128)(2,1)S(1)} %get-tuple-element.97), channel_id=1, source_target_pairs={{0,24},{1,25},{2,26},{3,27},{4,28},{5,29},{6,30},{7,31},{8,16},{9,... | collective-permute-start | bytes 1376264 | tf_op jit(solution)/shard_map/ppermute | solution.py:62
  (69 other events, 605.1 us)

commit v3 on v2

--- a/solution.py
+++ b/solution.py
@@ -62,7 +62,7 @@
     return lax.ppermute(value, "node", [(i, i ^ bits) for i in range(COUNT)])
 
 
-VMEM = 56 * 2**20
+VMEM = 16 * 2**20
 
 
 def shift(value, by, planes):
@@ -74,7 +74,8 @@
     )
 
 
-def swiglu_kernel(own, by_x, by_y, low, high, gate_a, gate_b, up_a, up_b, out, gate, up):
+def swiglu_kernel(*refs):
+    *pieces, gate_a, gate_b, up_a, up_b, out, gate, up = refs
     step = pl.program_id(0)
 
     @pl.when(step == 0)
@@ -82,7 +83,7 @@
         gate[...] = jnp.zeros_like(gate)
         up[...] = jnp.zeros_like(up)
 
-    block = jnp.concatenate([own[...], by_x[...], by_y[...], low[...], high[...]], axis=0)
+    block = jnp.concatenate([p[...] for p in pieces], axis=0)
     gate_w = jnp.concatenate([gate_a[...], gate_b[...]], axis=1)
     up_w = jnp.concatenate([up_a[...], up_b[...]], axis=1)
     gate[...] += jnp.dot(block, gate_w, preferred_element_type=jnp.float32)
@@ -114,7 +115,8 @@
     )(*[p for p, n, place in pieces], *weights)
 
 
-def down_kernel(own, by_x, by_y, across, mine, other, out, hidden):
+def down_kernel(own, by_x, by_y, across, mine, other, *rest):
+    *mix, out, hidden = rest
     rows = own.shape[0] // 4
     half = own.shape[1] // 2
 
@@ -130,10 +132,16 @@
 
     total = jnp.dot(hidden[:, : 4 * half], mine[...], preferred_element_type=jnp.float32)
     total += jnp.dot(hidden[:, 4 * half :], other[...], preferred_element_type=jnp.float32)
+    total = total.astype(out.dtype)
+    if mix:
+        weights, *others = mix
+        total = weights[:, 0:1] * total.astype(jnp.float32)
+        for k, term in enumerate(others, 1):
+            total += weights[:, k : k + 1] * term[...].astype(jnp.float32)
     out[...] = total.astype(out.dtype)
 
 
-def down(pieces, weights):
+def down(pieces, weights, mix=()):
     rows, hidden = pieces[0].shape
     width = weights[0].shape[1]
     cols = width // 2
@@ -142,16 +150,14 @@
         out_shape=jax.ShapeDtypeStruct((rows, width), jnp.bfloat16),
         grid=(2,),
         in_specs=[pl.BlockSpec(p.shape, lambda i: (0, 0)) for p in pieces]
-        + [pl.BlockSpec((w.shape[0], cols), lambda i: (0, i)) for w in weights],
+        + [pl.BlockSpec((w.shape[0], cols), lambda i: (0, i)) for w in weights]
+        + [pl.BlockSpec(m.shape, lambda i: (0, 0)) for m in mix[:1]]
+        + [pl.BlockSpec((rows, cols), lambda i: (0, i)) for m in mix[1:]],
         out_specs=pl.BlockSpec((rows, cols), lambda i: (0, i)),
         scratch_shapes=[pltpu.VMEM((rows, 4 * hidden), jnp.bfloat16)],
-        compiler_params=pltpu.CompilerParams(vmem_limit_bytes=VMEM),
-        cost_estimate=pl.CostEstimate(
-            flops=1000,
-            bytes_accessed=1000,
-            transcendentals=0,
-        ),
-    )(*pieces, *weights)
+        compiler_params=pltpu.CompilerParams(vmem_limit_bytes=56 * 2**20 if mix else VMEM),
+        cost_estimate=pl.CostEstimate(flops=1000, bytes_accessed=1000, transcendentals=0),
+    )(*pieces, *weights, *mix)
 
 
 def nothing(*refs):
@@ -192,83 +198,117 @@
         jnp.where(routes[:, :, None] == experts, probs[:, :, None], 0.0), axis=1
     )
 
+    def join(*pieces):
+        return jnp.concatenate(pieces, axis=0)
+
+    def spread(hidden):
+        (hidden,) = gate([hidden])
+        return [hidden, swap(hidden, X), swap(hidden, Y), swap(hidden, X + Y)]
+
+    def outputs(units, *earlier):
+        (units[0],) = gate([units[0]], *earlier)
+        out = down(units, down_w)
+        return gate([out])
+
     up1, dn1 = shift(tokens, 1, (0, 1, 2)), shift(tokens, -1, (1, 2, 3))
     down_x, down_y = swap(cut(1), X), swap(cut(2), Y)
     gate_b, up_b = swap(w_gate[0], CORE), swap(w_up[0], CORE)
-
-    up1, dn1, piece = gate([up1, dn1, cut(3)], down_x, down_y)
-    up2, dn2, down_d = shift(up1, 1, (1, 2)), shift(dn1, -1, (1, 2)), swap(piece, X + Y)
-
-    col = {0: tokens, 1: jnp.where(z % 2 == 0, dn1, up1), 2: jnp.where(z < 2, dn2, up2)}
-    onward = jnp.where(z == 2, up2, dn2)
-    mx, onward, down_x = gate([col[2], onward, down_x], down_d, gate_b)
-    col[2] = mx
-    x2, y2 = swap(mx, X), swap(mx, Y)
+    up1, dn1 = gate([up1, dn1])
+    up2, dn2 = shift(up1, 1, (1, 2)), shift(dn1, -1, (1, 2))
+    (piece,) = gate([cut(3)], down_x, down_y)
+    down_d = swap(piece, X + Y)
+    (onward,) = gate([jnp.where(z == 2, up2, dn2)])
     ends = shift(onward, None, None)
+
+    col1 = jnp.where(z % 2 == 0, dn1, up1)
+    col2 = jnp.where(z < 2, dn2, up2)
+    col2, down_x, w_0 = gate([col2, down_x, weights], down_y, down_d)
+    x2, y2 = swap(col2, X), swap(col2, Y)
+    w_x = swap(w_0, X)
     down_mine = jnp.concatenate([cut(0), down_x, down_y, down_d], axis=0)
     down_w = [down_mine, swap(down_mine, CORE)]
-    col[3] = jnp.where((z == 0) | (z == 3), ends, jnp.where(z == 1, dn1, up1))
     swiglu_w = [w_gate[0], gate_b, w_up[0], up_b]
 
-    def join(ahead, by_x, by_y):
-        low, high = by_x[:half], by_y[half:rows]
-        if ahead is None:
-            return high, low
-        return jnp.concatenate([ahead, high], axis=0), jnp.concatenate([ahead, low], axis=0)
-
-    def rows_of(k, by_x, by_y, by_x_later, by_y_later):
-        place = (by_x_later.shape[0] - half) // half
-        return [(col[k], rows, 0), (by_x, rows, 0), (by_y, rows, 0)] + [
-            (by_y_later, half, place),
-            (by_x_later, half, place),
-        ]
-
-    def spread(hidden):
-        (hidden,) = gate([hidden])
-        return [hidden, swap(hidden, X), swap(hidden, Y), swap(hidden, X + Y)]
-
-    def send_back(units, k):
-        (units[0],) = gate([units[0]])
-        out = down(units, down_w)
-        low, high = gate([out[: 2 * rows], out[2 * rows :]])
-        return swap(low, k * Z), swap(high, k * Z)
-
-    sums = {}
-    mx, my, w_0 = gate([*join(col[3], x2, y2), weights], down_w[1], up_b)
-    x3, y3 = swap(mx, X), swap(my, Y)
-    w_x, w_y, w_d = swap(w_0, X), swap(w_0, Y), swap(w_0, X + Y)
-
-    mx, my = gate(join(col[1], x3, y3), w_x, w_y, w_d)
-    x1, y1 = swap(mx, X), swap(my, Y)
+    col3 = jnp.where((z == 0) | (z == 3), ends, jnp.where(z == 1, dn1, up1))
+    to_x, to_y, to_z, w_0 = gate(
+        [
+            join(col3[half:], y2[half:]),
+            join(col3[:half], x2[:half]),
+            join(x2[:half], y2[half:]),
+            w_0,
+        ],
+        down_w[1],
+        gate_b,
+        w_x,
+    )
+    x3, y3, z3 = swap(to_x, X), swap(to_y, Y), swap(to_z, Z)
+    w_y = swap(w_0, Y)
+
+    col1, to_z, w_0 = gate([col1, join(y3[half:], x3[half:]), w_0], z3, up_b, w_y)
+    x1, y1, d3 = swap(col1, X), swap(col1, Y), swap(to_z, Z)
+    w_d = swap(w_0, X + Y)
     (mark,) = gate([x2])
-    all_2 = spread(swiglu(rows_of(2, mark, y2, x3, y3), swiglu_w))
-
-    mx, my, all_2[0] = gate([*join(tokens, x1, y1), all_2[0]], *all_2[1:])
-    x0, y0 = swap(mx, X), swap(my, Y)
-    sums[2] = send_back(all_2, 2)
-    (mark,) = gate([x3])
-    all_3 = spread(swiglu(rows_of(3, mark, y3, x1, y1), swiglu_w))
-
-    mx, my, all_3[0] = gate([*join(None, x0, y0), all_3[0]], sums[2][0], *all_3[1:])
-    xe, ye = swap(mx, X), swap(my, Y)
-    sums[3] = send_back(all_3, 3)
-    (mark,) = gate([x1])
-    all_1 = spread(swiglu(rows_of(1, mark, y1, x0, y0), swiglu_w))
-
-    (ye,) = gate([ye], xe, sums[2][1], sums[3][0], *all_1[1:])
-    all_0 = spread(swiglu(rows_of(0, x0, y0, xe, ye), swiglu_w))
-    sums[1] = send_back(all_1, 1)
+    all_2 = spread(
+        swiglu(
+            [(col2, rows, 0), (mark, rows, 0), (y2, rows, 0), (y3, half, 1), (x3, half, 1)],
+            swiglu_w,
+        )
+    )
+
+    to_x, to_y, all_2[0] = gate([y1[half:], x1[:half], all_2[0]], d3, w_d, *all_2[1:])
+    high1, low1 = swap(to_x, X), swap(to_y, Y)
+    (out_2,) = outputs(all_2)
+    back_2 = [swap(out_2, 2 * Z)]
+    (own,) = gate([tokens], low1, high1)
+    x0, y0 = swap(own, X), swap(own, Y)
+    (mark,) = gate([col3])
+    all_3 = spread(
+        swiglu(
+            [
+                (mark, rows, 0),
+                (z3, half, 0),
+                (x3, half, 0),
+                (y3, half, 0),
+                (z3, half, 1),
+                (d3, rows, 0),
+            ],
+            swiglu_w,
+        )
+    )
+    (mark,) = gate([col1])
+    hidden_1 = swiglu(
+        [(mark, rows, 0), (x1, rows, 0), (y1, rows, 0), (low1, half, 0), (high1, half, 0)],
+        swiglu_w,
+    )
+
+    to_x, to_y, all_3[0], hidden_1 = gate(
+        [y0[half:], x0[:half], all_3[0], hidden_1], *all_3[1:]
+    )
+    xe, ye = swap(to_x, X), swap(to_y, Y)
+    (hidden_1,) = gate([hidden_1])
+    all_1 = [hidden_1, swap(hidden_1, X), swap(hidden_1, Y)]
+    (out_3,) = outputs(all_3)
+    back_3 = [swap(out_3, 3 * Z)]
+    xe, all_1[0] = gate([xe, all_1[0]], ye, *back_2)
+    all_1.append(swap(all_1[0], X + Y))
+    all_0 = spread(
+        swiglu(
+            [(own, rows, 0), (x0, rows, 0), (y0, rows, 0), (ye, half, 0), (xe, half, 0)],
+            swiglu_w,
+        )
+    )
+    (out_1,) = outputs(all_1, *all_1[1:])
+    back_1 = [swap(out_1, Z)]
     (all_0[0],) = gate([all_0[0]], *all_0[1:])
-    sums[0] = (down(all_0, down_w),)
-    order = (2, 3, 1, 0)
-    sums = {k: jnp.concatenate(sums[k], axis=0) for k in order}
-
     weights = jnp.concatenate([w_0, w_x, w_y, w_d], axis=0)
-    total = 0.0
-    for k in order:
-        weight = jnp.sum(jnp.where(experts == (z ^ k), weights, 0.0), axis=1, keepdims=True)
-        total = total + weight * sums[k].astype(jnp.float32)
-    mixed = total.astype(jnp.bfloat16).reshape(4, rows, part)
+    weights = jnp.concatenate(
+        [
+            jnp.sum(jnp.where(experts == (z ^ k), weights, 0.0), axis=1, keepdims=True)
+            for k in range(PLANES)
+        ],
+        axis=1,
+    )
+    mixed = down(all_0, down_w, [weights, back_1[0], back_2[0], back_3[0]]).reshape(4, rows, part)
     pieces = [mixed[0], swap(mixed[1], X), swap(mixed[2], Y), swap(mixed[3], X + Y)]
     result = []
     for a in range(4):

time: 320 us -> 265 us (0.83)
  waiting for transfers between devices: 158 us -> 129 us
  local copies, waits for them, and re-layouts: 28.7 us -> 13.6 us
  Pallas kernels: 66 us -> 55.4 us
    ppermute x40 -> x41, waiting for transfers between devices: 126 us -> 96.7 us  [swap(): return lax.ppermute(value, 'node', [(i, i ^ bits) for i in range(COUNT)])]
    unnamed x96 -> x25, local copies, waits for them, and re-layouts: 18.5 us -> 5.02 us
    pallas_call x4, Pallas kernels: 23.3 us -> 17.1 us  [down(): pl.pallas_call(down_kernel, out_shape=jax.ShapeDtypeStruct((rows, width),...]
    pallas_call x4, Pallas kernels: 42.8 us -> 38.2 us  [swiglu(): pl.pallas_call(swiglu_kernel, out_shape=jax.ShapeDtypeStruct((rows, hidde...]
    slice x11 -> x9, local copies, waits for them, and re-layouts: 6.19 us -> 2.34 us  [the longest x1 1.05 us: four_planes(): y2[half:]]
    ppermute x40 -> x41, starting transfers between devices: 45.9 us -> 45.2 us  [swap(): return lax.ppermute(value, 'node', [(i, i ^ bits) for i in range(COUNT)])]
  transfers between devices with their start and end apart: 45 -> 46, of which waited for: 24 -> 24; matrix products, arithmetic and copies ran while one was open for 5% -> 5% of each run, Pallas kernels for 21% -> 18%
where the time goes in v3:
time: 265 us; the launch traced here: 264 us
  waiting for transfers between devices  129 us (49%)
  starting transfers between devices  56.6 us (21%)
  Pallas kernels  55.4 us (21%)
  local copies, waits for them, and re-layouts  13.6 us (5%)
  other arithmetic  8.96 us (3%)
    ppermute x41, waiting for transfers between devices, swap(): return lax.ppermute(value, 'node', [(i, i ^ bits) for i in range(COUNT)])  96.7 us
    ppermute x41, starting transfers between devices, swap(): return lax.ppermute(value, 'node', [(i, i ^ bits) for i in range(COUNT)])  45.2 us
    pallas_call x4, Pallas kernels, swiglu(): pl.pallas_call(swiglu_kernel, out_shape=jax.ShapeDtypeStruct((rows, hidde...  38.2 us
    ppermute x5, waiting for transfers between devices, shift(): lax.ppermute(value, 'node', [(p * GROUP + m, q * GROUP + m) for p, q in m...  32.6 us
    pallas_call x4, Pallas kernels, down(): pl.pallas_call(down_kernel, out_shape=jax.ShapeDtypeStruct((rows, width),...  17.1 us
    ppermute x5, starting transfers between devices, shift(): lax.ppermute(value, 'node', [(p * GROUP + m, q * GROUP + m) for p, q in m...  11.3 us
  transfers between devices with their start and end apart: 46, of which 24 were waited for; matrix products, arithmetic and copies ran while one was open for 5% of the time, Pallas kernels for 18%

profile of v3, /device:TPU:0, one launch (start us, length us, event | category | flops | bytes accessed | tf_op | source)
XLA Modules:
  0.0 264.4 jit_solution(9526033103521522001)
XLA Ops:
  1.2 5.9 %collective-permute-start = (bf16[64,7168]{1,0:T(8,128)(2,1)S(1)}, bf16[64,7168]{1,0:T(8,128)(2,1)}, u32[]{:S(2)}, u32[]{:S(2)}) collective-permute-start(bf16[64,7168]{1,0:T(8,128)(2,1)S(1)} %copy.153.refs_1_), channel_id=1, source_target_pairs={{0,8},{1,9},{2,10},{3,11},{4,12},{5,13},{6,14},{7,15},{8,16},{9,17... | collective-permute-start | bytes 2752520 | tf_op jit(solution)/shard_map/ppermute | solution.py:70
  8.4 3.9 %dynamic-slice_bitcast_fusion = (bf16[256,1792]{1,0:T(8,128)(2,1)}, bf16[256,1792]{1,0:T(8,128)(2,1)}, bf16[256,1792]{1,0:T(8,128)(2,1)}, bf16[256,1792]{1,0:T(8,128)(2,1)}) fusion(bf16[1,256,7168]{2,1,0:T(8,128)(2,1)} %param.11, s32[]{:T(128)S(6)} %select_n.151, s32[]{:T(128)S(6)} %select_n.139, s32[]{:T(128)S(6)} %select_n.138, s32[]{:T(128)S(6)} %select_n.140), kind=kLoop, calls=%fused_computation.6 | loop fusion | bytes 7340048 | tf_op jit(solution)/shard_map/dynamic_slice | solution.py:194
  15.3 10.4 %collective-permute-done.refs_1_ = bf16[64,7168]{1,0:T(8,128)(2,1)} collective-permute-done((bf16[64,7168]{1,0:T(8,128)(2,1)S(1)}, bf16[64,7168]{1,0:T(8,128)(2,1)}, u32[]{:S(2)}, u32[]{:S(2)}) %collective-permute-start) | collective-permute-done | bytes 917536 | tf_op jit(solution)/shard_map/ppermute | solution.py:70
  25.7 5.1 %collective-permute-done.1.refs_2_ = bf16[64,7168]{1,0:T(8,128)(2,1)} collective-permute-done((bf16[64,7168]{1,0:T(8,128)(2,1)S(1)}, bf16[64,7168]{1,0:T(8,128)(2,1)}, u32[]{:S(2)}, u32[]{:S(2)}) %collective-permute-start.1) | collective-permute-done | bytes 917536 | tf_op jit(solution)/shard_map/ppermute | solution.py:70
  39.2 14.8 %collective-permute-done.5 = bf16[64,7168]{1,0:T(8,128)(2,1)} collective-permute-done((bf16[64,7168]{1,0:T(8,128)(2,1)}, bf16[64,7168]{1,0:T(8,128)(2,1)}, u32[]{:S(2)}, u32[]{:S(2)}) %collective-permute-start.5) | collective-permute-done | bytes 917536 | tf_op jit(solution)/shard_map/ppermute | solution.py:70
  65.9 14.4 %collective-permute-done.8.refs_2_ = bf16[64,7168]{1,0:T(8,128)(2,1)} collective-permute-done((bf16[64,7168]{1,0:T(8,128)(2,1)}, bf16[64,7168]{1,0:T(8,128)(2,1)}, u32[]{:S(2)}, u32[]{:S(2)}) %collective-permute-start.8) | collective-permute-done | bytes 917536 | tf_op jit(solution)/shard_map/ppermute | solution.py:62
  89.0 4.0 %collective-permute-start.15 = (bf16[64,7168]{1,0:T(8,128)(2,1)S(1)}, bf16[64,7168]{1,0:T(8,128)(2,1)S(1)}, u32[]{:S(2)}, u32[]{:S(2)}) collective-permute-start(bf16[64,7168]{1,0:T(8,128)(2,1)S(1)} %get-tuple-element.81), channel_id=1, source_target_pairs={{0,8},{1,9},{2,10},{3,11},{4,12},{5,13},{6,14},{7,15},{8,0},{9,1},... | collective-permute-start | bytes 2752520 | tf_op jit(solution)/shard_map/ppermute | solution.py:62
  93.5 15.6 %collective-permute-done.14.refs_4_.refs_2_ = bf16[64,7168]{1,0:T(8,128)(2,1)S(1)} collective-permute-done((bf16[64,7168]{1,0:T(8,128)(2,1)S(1)}, bf16[64,7168]{1,0:T(8,128)(2,1)S(1)}, u32[]{:S(2)}, u32[]{:S(2)}) %collective-permute-start.14) | collective-permute-done | bytes 917536 | tf_op jit(solution)/shard_map/ppermute | solution.py:62
  116.4 9.9 %shard_map.71.refs_1_ = bf16[256,512]{1,0:T(8,128)(2,1)S(1)} custom-call(bf16[64,7168]{1,0:T(8,128)(2,1)} %get-tuple-element.74.refs_0_, bf16[64,7168]{1,0:T(8,128)(2,1)} %get-tuple-element.84.refs_1_, bf16[64,7168]{1,0:T(8,128)(2,1)} %collective-permute-done.8.refs_2_, bf16[64,7168]{1,0:T(8,128)(2,1)S(1)} %collective-permute-done.13.refs_3_, ...), custom_call_target="tpu_custom_call" | custom-call | flops 1000 | bytes 1000 | tf_op jit(solution)/shard_map/pallas_call | solution.py:102
  128.9 7.5 %collective-permute-done.18.refs_2_ = bf16[64,7168]{1,0:T(8,128)(2,1)S(1)} collective-permute-done((bf16[64,7168]{1,0:T(8,128)(2,1)S(1)}, bf16[64,7168]{1,0:T(8,128)(2,1)S(1)}, u32[]{:S(2)}, u32[]{:S(2)}) %collective-permute-start.18) | collective-permute-done | bytes 917536 | tf_op jit(solution)/shard_map/ppermute | solution.py:62
  139.4 8.1 %collective-permute-done.21.refs_5_ = f32[64,4]{1,0:T(8,128)S(1)} collective-permute-done((f32[64,4]{1,0:T(8,128)S(1)}, f32[64,4]{1,0:T(8,128)S(1)}, u32[]{:S(2)}, u32[]{:S(2)}) %collective-permute-start.21) | collective-permute-done | bytes 1056 | tf_op jit(solution)/shard_map/ppermute | solution.py:62
  148.6 3.3 %shard_map.75.refs_1_ = bf16[256,1792]{1,0:T(8,128)(2,1)S(1)} custom-call(bf16[256,512]{1,0:T(8,128)(2,1)S(1)} %get-tuple-element.93.own, bf16[256,512]{1,0:T(8,128)(2,1)S(1)} %collective-permute-done.22.refs_6_.by_x, bf16[256,512]{1,0:T(8,128)(2,1)S(1)} %collective-permute-done.23.refs_7_.by_y, bf16[256,512]{1,0:T(8,128)(2,1)S(1)} %collective-permute-done.24.refs_8_.across, ...), custom_call_target="tpu_custom_call" | custom-call | flops 1000 | bytes 1000 | tf_op jit(solution)/shard_map/pallas_call | solution.py:148
  152.0 6.3 %collective-permute-done.25.refs_2_.refs_3_ = bf16[32,7168]{1,0:T(8,128)(2,1)S(1)} collective-permute-done((bf16[32,7168]{1,0:T(8,128)(2,1)S(1)}, bf16[32,7168]{1,0:T(8,128)(2,1)S(1)}, u32[]{:S(2)}, u32[]{:S(2)}) %collective-permute-start.25) | collective-permute-done | bytes 458784 | tf_op jit(solution)/shard_map/ppermute | solution.py:62
  161.6 9.5 %shard_map.79.refs_1_ = bf16[256,512]{1,0:T(8,128)(2,1)S(1)} custom-call(bf16[64,7168]{1,0:T(8,128)(2,1)S(1)} %get-tuple-element.99.refs_0_, bf16[64,7168]{1,0:T(8,128)(2,1)S(1)} %collective-permute-done.15.refs_4_.refs_1_, bf16[64,7168]{1,0:T(8,128)(2,1)S(1)} %collective-permute-done.14.refs_4_.refs_2_, ...), custom_call_target="tpu_custom_call" | custom-call | flops 1000 | bytes 1000 | tf_op jit(solution)/shard_map/pallas_call | solution.py:102
  173.4 7.3 %collective-permute-done.27.refs_2_ = bf16[64,7168]{1,0:T(8,128)(2,1)S(1)} collective-permute-done((bf16[64,7168]{1,0:T(8,128)(2,1)S(1)}, bf16[64,7168]{1,0:T(8,128)(2,1)S(1)}, u32[]{:S(2)}, u32[]{:S(2)}) %collective-permute-start.27) | collective-permute-done | bytes 917536 | tf_op jit(solution)/shard_map/ppermute | solution.py:62
  182.4 9.4 %shard_map.82.refs_4_ = bf16[256,512]{1,0:T(8,128)(2,1)S(1)} custom-call(bf16[64,7168]{1,0:T(8,128)(2,1)S(1)} %get-tuple-element.104.refs_0_, bf16[64,7168]{1,0:T(8,128)(2,1)S(1)} %collective-permute-done.19.refs_1_, bf16[64,7168]{1,0:T(8,128)(2,1)S(1)} %collective-permute-done.18.refs_2_, bf16[32,7168]{1,0:T(8,128)(2,1)S(1)} %collective-permute-done.25.refs_2_.refs_3_, ...), custom_call_target="tpu_custom_call" | custom-call | flops 1000 | bytes 1000 | tf_op jit(solution)/shard_map/pallas_call | solution.py:102
  196.1 3.3 %shard_map.86.refs_1_ = bf16[256,1792]{1,0:T(8,128)(2,1)S(1)} custom-call(bf16[256,512]{1,0:T(8,128)(2,1)S(1)} %get-tuple-element.110.own, bf16[256,512]{1,0:T(8,128)(2,1)S(1)} %collective-permute-done.29.refs_5_.by_x, bf16[256,512]{1,0:T(8,128)(2,1)S(1)} %collective-permute-done.30.refs_6_.by_y, ...), custom_call_target="tpu_custom_call" | custom-call | flops 1000 | bytes 1000 | tf_op jit(solution)/shard_map/pallas_call | solution.py:148
  199.5 9.0 %collective-permute-done.36.refs_3_.by_y = bf16[256,512]{1,0:T(8,128)(2,1)S(1)} collective-permute-done((bf16[256,512]{1,0:T(8,128)(2,1)S(1)}, bf16[256,512]{1,0:T(8,128)(2,1)S(1)}, u32[]{:S(2)}, u32[]{:S(2)}) %collective-permute-start.36) | collective-permute-done | bytes 262176 | tf_op jit(solution)/shard_map/ppermute | solution.py:62
  211.8 9.4 %shard_map.89.refs_1_ = bf16[256,512]{1,0:T(8,128)(2,1)S(1)} custom-call(bf16[64,7168]{1,0:T(8,128)(2,1)S(1)} %get-tuple-element.102.refs_0_, bf16[64,7168]{1,0:T(8,128)(2,1)S(1)} %collective-permute-done.28.refs_1_, bf16[64,7168]{1,0:T(8,128)(2,1)S(1)} %collective-permute-done.27.refs_2_, bf16[32,7168]{1,0:T(8,128)(2,1)S(1)} %collective-permute-done.33.refs_3_, ...), custom_call_target="tpu_custom_call" | custom-call | flops 1000 | bytes 1000 | tf_op jit(solution)/shard_map/pallas_call | solution.py:102
  221.3 3.4 %shard_map.92.refs_1_ = bf16[256,1792]{1,0:T(8,128)(2,1)S(1)} custom-call(bf16[256,512]{1,0:T(8,128)(2,1)S(1)} %get-tuple-element.121.own, bf16[256,512]{1,0:T(8,128)(2,1)S(1)} %collective-permute-done.35.refs_2_.by_x, bf16[256,512]{1,0:T(8,128)(2,1)S(1)} %collective-permute-done.36.refs_3_.by_y, ...), custom_call_target="tpu_custom_call" | custom-call | flops 1000 | bytes 1000 | tf_op jit(solution)/shard_map/pallas_call | solution.py:148
  231.2 3.8 %collective-permute-done.39.refs_3_.by_y = bf16[256,512]{1,0:T(8,128)(2,1)S(1)} collective-permute-done((bf16[256,512]{1,0:T(8,128)(2,1)S(1)}, bf16[256,512]{1,0:T(8,128)(2,1)S(1)}, u32[]{:S(2)}, u32[]{:S(2)}) %collective-permute-start.39) | collective-permute-done | bytes 262176 | tf_op jit(solution)/shard_map/ppermute | solution.py:62
  235.8 8.4 %collective-permute-done.41.rest_1_ = bf16[256,1792]{1,0:T(8,128)(2,1)} collective-permute-done((bf16[256,1792]{1,0:T(8,128)(2,1)S(1)}, bf16[256,1792]{1,0:T(8,128)(2,1)}, u32[]{:S(2)}, u32[]{:S(2)}) %collective-permute-start.41) | collective-permute-done | bytes 917536 | tf_op jit(solution)/shard_map/ppermute | solution.py:62
  244.2 7.1 %shard_map.95 = bf16[256,1792]{1,0:T(8,128)(2,1)} custom-call(bf16[256,512]{1,0:T(8,128)(2,1)} %copy-done.2, bf16[256,512]{1,0:T(8,128)(2,1)} %copy-done.7, bf16[256,512]{1,0:T(8,128)(2,1)} %copy-done.8, bf16[256,512]{1,0:T(8,128)(2,1)} %copy-done.9, bf16[1024,1792]{1,0:T(8,128)(2,1)} %copy-done, bf16[1024,1792]{1,0:T(8,128)(2,1)} %copy-done.1, ...), custom_call_target="tpu_custom_call" | custom-call | flops 1000 | bytes 1000 | tf_op jit(solution)/shard_map/pallas_call | solution.py:148
  256.0 3.5 %collective-permute-done.43 = bf16[64,1792]{1,0:T(8,128)(2,1)S(1)} collective-permute-done((bf16[64,1792]{1,0:T(8,128)(2,1)S(1)}, bf16[64,1792]{1,0:T(8,128)(2,1)S(1)}, u32[]{:S(2)}, u32[]{:S(2)}) %collective-permute-start.43) | collective-permute-done | bytes 229408 | tf_op jit(solution)/shard_map/ppermute | solution.py:62
  (155 shorter events, 80.6 us)
Async XLA Ops:
  1.2 24.5 %collective-permute-start = (bf16[64,7168]{1,0:T(8,128)(2,1)S(1)}, bf16[64,7168]{1,0:T(8,128)(2,1)}, u32[]{:S(2)}, u32[]{:S(2)}) collective-permute-start(bf16[64,7168]{1,0:T(8,128)(2,1)S(1)} %copy.153.refs_1_), channel_id=1, source_target_pairs={{0,8},{1,9},{2,10},{3,11},{4,12},{5,13},{6,14},{7,15},{8,16},{9,17... | collective-permute-start | bytes 2752520 | tf_op jit(solution)/shard_map/ppermute | solution.py:70
  7.0 23.8 %collective-permute-start.1 = (bf16[64,7168]{1,0:T(8,128)(2,1)S(1)}, bf16[64,7168]{1,0:T(8,128)(2,1)}, u32[]{:S(2)}, u32[]{:S(2)}) collective-permute-start(bf16[64,7168]{1,0:T(8,128)(2,1)S(1)} %copy.153.refs_1_), channel_id=1, source_target_pairs={{8,0},{9,1},{10,2},{11,3},{12,4},{13,5},{14,6},{15,7},{16,8},{17,9... | collective-permute-start | bytes 2752520 | tf_op jit(solution)/shard_map/ppermute | solution.py:70
  12.3 22.0 %collective-permute-start.2 = (bf16[256,1792]{1,0:T(8,128)(2,1)}, bf16[256,1792]{1,0:T(8,128)(2,1)S(1)}, u32[]{:S(2)}, u32[]{:S(2)}) collective-permute-start(bf16[256,1792]{1,0:T(8,128)(2,1)} %get-tuple-element.132), channel_id=1, source_target_pairs={{0,2},{1,3},{2,0},{3,1},{4,6},{5,7},{6,4},{7,5},{8,10},{9,11},{10,... | collective-permute-start | bytes 2752520 | tf_op jit(solution)/shard_map/ppermute | solution.py:62
  13.8 21.7 %collective-permute-start.3 = (bf16[256,1792]{1,0:T(8,128)(2,1)}, bf16[256,1792]{1,0:T(8,128)(2,1)S(1)}, u32[]{:S(2)}, u32[]{:S(2)}) collective-permute-start(bf16[256,1792]{1,0:T(8,128)(2,1)} %get-tuple-element.134), channel_id=1, source_target_pairs={{0,4},{1,5},{2,6},{3,7},{4,0},{5,1},{6,2},{7,3},{8,12},{9,13},{10,... | collective-permute-start | bytes 2752520 | tf_op jit(solution)/shard_map/ppermute | solution.py:62
  30.8 23.1 %collective-permute-start.5 = (bf16[64,7168]{1,0:T(8,128)(2,1)}, bf16[64,7168]{1,0:T(8,128)(2,1)}, u32[]{:S(2)}, u32[]{:S(2)}) collective-permute-start(bf16[64,7168]{1,0:T(8,128)(2,1)} %get-tuple-element.69), channel_id=1, source_target_pairs={{8,0},{9,1},{10,2},{11,3},{12,4},{13,5},{14,6},{15,7},{16,8},{17,9... | collective-permute-start | bytes 2752520 | tf_op jit(solution)/shard_map/ppermute | solution.py:70
  32.1 21.8 %collective-permute-start.4 = (bf16[64,7168]{1,0:T(8,128)(2,1)}, bf16[64,7168]{1,0:T(8,128)(2,1)}, u32[]{:S(2)}, u32[]{:S(2)}) collective-permute-start(bf16[64,7168]{1,0:T(8,128)(2,1)} %get-tuple-element.68), channel_id=1, source_target_pairs={{8,16},{9,17},{10,18},{11,19},{12,20},{13,21},{14,22},{15,23},{16,... | collective-permute-start | bytes 2752520 | tf_op jit(solution)/shard_map/ppermute | solution.py:70
  37.7 21.7 %collective-permute-start.6 = (bf16[256,1792]{1,0:T(8,128)(2,1)}, bf16[256,1792]{1,0:T(8,128)(2,1)S(1)}, u32[]{:S(2)}, u32[]{:S(2)}) collective-permute-start(bf16[256,1792]{1,0:T(8,128)(2,1)} %copy-done.6), channel_id=1, source_target_pairs={{0,6},{1,7},{2,4},{3,5},{4,2},{5,3},{6,0},{7,1},{8,14},{9,15},{10,... | collective-permute-start | bytes 2752520 | tf_op jit(solution)/shard_map/ppermute | solution.py:62
  60.3 20.0 %collective-permute-start.8 = (bf16[64,7168]{1,0:T(8,128)(2,1)}, bf16[64,7168]{1,0:T(8,128)(2,1)}, u32[]{:S(2)}, u32[]{:S(2)}) collective-permute-start(bf16[64,7168]{1,0:T(8,128)(2,1)} %get-tuple-element.74.refs_0_), channel_id=1, source_target_pairs={{0,4},{1,5},{2,6},{3,7},{4,0},{5,1},{6,2},{7,3},{8,12},{9,13},{10,... | collective-permute-start | bytes 2752520 | tf_op jit(solution)/shard_map/ppermute | solution.py:62
  62.4 23.1 %collective-permute-start.7 = (bf16[64,7168]{1,0:T(8,128)(2,1)}, bf16[64,7168]{1,0:T(8,128)(2,1)}, u32[]{:S(2)}, u32[]{:S(2)}) collective-permute-start(bf16[64,7168]{1,0:T(8,128)(2,1)} %get-tuple-element.73), channel_id=1, source_target_pairs={{8,0},{9,1},{10,2},{11,3},{12,4},{13,5},{14,6},{15,7},{16,24},{17,... | collective-permute-start | bytes 2752520 | tf_op jit(solution)/shard_map/ppermute | solution.py:70
  63.7 24.2 %collective-permute-start.11 = (bf16[7168,256]{1,0:T(8,128)(2,1)}, bf16[7168,256]{1,0:T(8,128)(2,1)}, u32[]{:S(2)}, u32[]{:S(2)}) collective-permute-start(bf16[7168,256]{1,0:T(8,128)(2,1)} %bitcast.4.refs_5_.refs_6_), channel_id=1, source_target_pairs={{0,1},{1,0},{2,3},{3,2},{4,5},{5,4},{6,7},{7,6},{8,9},{9,8},{10,11... | collective-permute-start | bytes 11010056 | tf_op jit(solution)/shard_map/ppermute | solution.py:62
  63.8 46.1 %collective-permute-start.16 = (bf16[7168,256]{1,0:T(8,128)(2,1)}, bf16[7168,256]{1,0:T(8,128)(2,1)}, u32[]{:S(2)}, u32[]{:S(2)}) collective-permute-start(bf16[7168,256]{1,0:T(8,128)(2,1)} %bitcast.5.refs_7_.refs_8_), channel_id=1, source_target_pairs={{0,1},{1,0},{2,3},{3,2},{4,5},{5,4},{6,7},{7,6},{8,9},{9,8},{10,11... | collective-permute-start | bytes 11010056 | tf_op jit(solution)/shard_map/ppermute | solution.py:62
  87.9 21.2 %collective-permute-start.14 = (bf16[64,7168]{1,0:T(8,128)(2,1)S(1)}, bf16[64,7168]{1,0:T(8,128)(2,1)S(1)}, u32[]{:S(2)}, u32[]{:S(2)}) collective-permute-start(bf16[64,7168]{1,0:T(8,128)(2,1)S(1)} %get-tuple-element.79), channel_id=1, source_target_pairs={{0,2},{1,3},{2,0},{3,1},{4,6},{5,7},{6,4},{7,5},{8,10},{9,11},{10,... | collective-permute-start | bytes 2752520 | tf_op jit(solution)/shard_map/ppermute | solution.py:62
  88.5 21.3 %collective-permute-start.13 = (bf16[64,7168]{1,0:T(8,128)(2,1)S(1)}, bf16[64,7168]{1,0:T(8,128)(2,1)S(1)}, u32[]{:S(2)}, u32[]{:S(2)}) collective-permute-start(bf16[64,7168]{1,0:T(8,128)(2,1)S(1)} %get-tuple-element.78), channel_id=1, source_target_pairs={{0,4},{1,5},{2,6},{3,7},{4,0},{5,1},{6,2},{7,3},{8,12},{9,13},{10,... | collective-permute-start | bytes 2752520 | tf_op jit(solution)/shard_map/ppermute | solution.py:62
  89.0 24.1 %collective-permute-start.15 = (bf16[64,7168]{1,0:T(8,128)(2,1)S(1)}, bf16[64,7168]{1,0:T(8,128)(2,1)S(1)}, u32[]{:S(2)}, u32[]{:S(2)}) collective-permute-start(bf16[64,7168]{1,0:T(8,128)(2,1)S(1)} %get-tuple-element.81), channel_id=1, source_target_pairs={{0,8},{1,9},{2,10},{3,11},{4,12},{5,13},{6,14},{7,15},{8,0},{9,1},... | collective-permute-start | bytes 2752520 | tf_op jit(solution)/shard_map/ppermute | solution.py:62
  113.1 23.3 %collective-permute-start.18 = (bf16[64,7168]{1,0:T(8,128)(2,1)S(1)}, bf16[64,7168]{1,0:T(8,128)(2,1)S(1)}, u32[]{:S(2)}, u32[]{:S(2)}) collective-permute-start(bf16[64,7168]{1,0:T(8,128)(2,1)S(1)} %get-tuple-element.86.refs_1_), channel_id=1, source_target_pairs={{0,4},{1,5},{2,6},{3,7},{4,0},{5,1},{6,2},{7,3},{8,12},{9,13},{10,... | collective-permute-start | bytes 2752520 | tf_op jit(solution)/shard_map/ppermute | solution.py:62
  113.6 23.3 %collective-permute-start.19 = (bf16[64,7168]{1,0:T(8,128)(2,1)S(1)}, bf16[64,7168]{1,0:T(8,128)(2,1)S(1)}, u32[]{:S(2)}, u32[]{:S(2)}) collective-permute-start(bf16[64,7168]{1,0:T(8,128)(2,1)S(1)} %get-tuple-element.86.refs_1_), channel_id=1, source_target_pairs={{0,2},{1,3},{2,0},{3,1},{4,6},{5,7},{6,4},{7,5},{8,10},{9,11},{10,... | collective-permute-start | bytes 2752520 | tf_op jit(solution)/shard_map/ppermute | solution.py:62
  114.2 33.3 %collective-permute-start.20 = (bf16[64,7168]{1,0:T(8,128)(2,1)S(1)}, bf16[64,7168]{1,0:T(8,128)(2,1)S(1)}, u32[]{:S(2)}, u32[]{:S(2)}) collective-permute-start(bf16[64,7168]{1,0:T(8,128)(2,1)S(1)} %get-tuple-element.88), channel_id=1, source_target_pairs={{0,8},{1,9},{2,10},{3,11},{4,12},{5,13},{6,14},{7,15},{8,0},{9,1},... | collective-permute-start | bytes 2752520 | tf_op jit(solution)/shard_map/ppermute | solution.py:62
  126.3 21.2 %collective-permute-start.22 = (bf16[256,512]{1,0:T(8,128)(2,1)S(1)}, bf16[256,512]{1,0:T(8,128)(2,1)S(1)}, u32[]{:S(2)}, u32[]{:S(2)}) collective-permute-start(bf16[256,512]{1,0:T(8,128)(2,1)S(1)} %get-tuple-element.87.refs_3_), channel_id=1, source_target_pairs={{0,2},{1,3},{2,0},{3,1},{4,6},{5,7},{6,4},{7,5},{8,10},{9,11},{10,... | collective-permute-start | bytes 786440 | tf_op jit(solution)/shard_map/ppermute | solution.py:62
  158.3 22.4 %collective-permute-start.27 = (bf16[64,7168]{1,0:T(8,128)(2,1)S(1)}, bf16[64,7168]{1,0:T(8,128)(2,1)S(1)}, u32[]{:S(2)}, u32[]{:S(2)}) collective-permute-start(bf16[64,7168]{1,0:T(8,128)(2,1)S(1)} %get-tuple-element.102.refs_0_), channel_id=1, source_target_pairs={{0,4},{1,5},{2,6},{3,7},{4,0},{5,1},{6,2},{7,3},{8,12},{9,13},{10,... | collective-permute-start | bytes 2752520 | tf_op jit(solution)/shard_map/ppermute | solution.py:62
  160.0 31.8 %collective-permute-start.28 = (bf16[64,7168]{1,0:T(8,128)(2,1)S(1)}, bf16[64,7168]{1,0:T(8,128)(2,1)S(1)}, u32[]{:S(2)}, u32[]{:S(2)}) collective-permute-start(bf16[64,7168]{1,0:T(8,128)(2,1)S(1)} %get-tuple-element.102.refs_0_), channel_id=1, source_target_pairs={{0,2},{1,3},{2,0},{3,1},{4,6},{5,7},{6,4},{7,5},{8,10},{9,11},{10,... | collective-permute-start | bytes 2752520 | tf_op jit(solution)/shard_map/ppermute | solution.py:62
  160.6 38.9 %collective-permute-start.34 = (bf16[256,1792]{1,0:T(8,128)(2,1)S(1)}, bf16[256,1792]{1,0:T(8,128)(2,1)S(1)}, u32[]{:S(2)}, u32[]{:S(2)}) collective-permute-start(bf16[256,1792]{1,0:T(8,128)(2,1)S(1)} %get-tuple-element.115), channel_id=1, source_target_pairs={{0,16},{1,17},{2,18},{3,19},{4,20},{5,21},{6,22},{7,23},{8,24},{9,... | collective-permute-start | bytes 2752520 | tf_op jit(solution)/shard_map/ppermute | solution.py:62
  171.1 20.8 %collective-permute-start.29 = (bf16[256,512]{1,0:T(8,128)(2,1)S(1)}, bf16[256,512]{1,0:T(8,128)(2,1)S(1)}, u32[]{:S(2)}, u32[]{:S(2)}) collective-permute-start(bf16[256,512]{1,0:T(8,128)(2,1)S(1)} %get-tuple-element.103.refs_3_), channel_id=1, source_target_pairs={{0,2},{1,3},{2,0},{3,1},{4,6},{5,7},{6,4},{7,5},{8,10},{9,11},{10,... | collective-permute-start | bytes 786440 | tf_op jit(solution)/shard_map/ppermute | solution.py:62
  171.7 20.3 %collective-permute-start.30 = (bf16[256,512]{1,0:T(8,128)(2,1)S(1)}, bf16[256,512]{1,0:T(8,128)(2,1)S(1)}, u32[]{:S(2)}, u32[]{:S(2)}) collective-permute-start(bf16[256,512]{1,0:T(8,128)(2,1)S(1)} %get-tuple-element.103.refs_3_), channel_id=1, source_target_pairs={{0,4},{1,5},{2,6},{3,7},{4,0},{5,1},{6,2},{7,3},{8,12},{9,13},{10,... | collective-permute-start | bytes 786440 | tf_op jit(solution)/shard_map/ppermute | solution.py:62
  209.1 26.7 %collective-permute-start.42 = (bf16[256,1792]{1,0:T(8,128)(2,1)S(1)}, bf16[256,1792]{1,0:T(8,128)(2,1)}, u32[]{:S(2)}, u32[]{:S(2)}) collective-permute-start(bf16[256,1792]{1,0:T(8,128)(2,1)S(1)} %get-tuple-element.126), channel_id=1, source_target_pairs={{0,24},{1,25},{2,26},{3,27},{4,28},{5,29},{6,30},{7,31},{8,16},{9,... | collective-permute-start | bytes 2752520 | tf_op jit(solution)/shard_map/ppermute | solution.py:62
  (34 other events, 657.7 us)

commit v4 on v3

--- a/solution.py
+++ b/solution.py
@@ -63,15 +63,6 @@
 
 
 VMEM = 16 * 2**20
-
-
-def shift(value, by, planes):
-    moves = ((1, 0), (2, 3)) if by is None else [(p, p + by) for p in planes]
-    return lax.ppermute(
-        value,
-        "node",
-        [(p * GROUP + m, q * GROUP + m) for p, q in moves for m in range(GROUP)],
-    )
 
 
 def swiglu_kernel(*refs):
@@ -201,105 +192,118 @@
     def join(*pieces):
         return jnp.concatenate(pieces, axis=0)
 
-    def spread(hidden):
-        (hidden,) = gate([hidden])
+    def spread(hidden, *earlier):
+        (hidden,) = gate([hidden], *earlier)
         return [hidden, swap(hidden, X), swap(hidden, Y), swap(hidden, X + Y)]
 
-    def outputs(units, *earlier):
+    def outputs(units, *earlier, split=False):
         (units[0],) = gate([units[0]], *earlier)
         out = down(units, down_w)
-        return gate([out])
-
-    up1, dn1 = shift(tokens, 1, (0, 1, 2)), shift(tokens, -1, (1, 2, 3))
-    down_x, down_y = swap(cut(1), X), swap(cut(2), Y)
-    gate_b, up_b = swap(w_gate[0], CORE), swap(w_up[0], CORE)
-    up1, dn1 = gate([up1, dn1])
-    up2, dn2 = shift(up1, 1, (1, 2)), shift(dn1, -1, (1, 2))
-    (piece,) = gate([cut(3)], down_x, down_y)
-    down_d = swap(piece, X + Y)
-    (onward,) = gate([jnp.where(z == 2, up2, dn2)])
-    ends = shift(onward, None, None)
-
-    col1 = jnp.where(z % 2 == 0, dn1, up1)
-    col2 = jnp.where(z < 2, dn2, up2)
-    col2, down_x, w_0 = gate([col2, down_x, weights], down_y, down_d)
-    x2, y2 = swap(col2, X), swap(col2, Y)
+        return gate([out[: 2 * rows], out[2 * rows :]] if split else [out])
+
+    col2, col1 = swap(tokens, 2 * Z), swap(tokens, Z)
+    down_x, down_y, down_d = swap(cut(1), X), swap(cut(2), Y), swap(cut(3), X + Y)
+
+    col2, down_x = gate([col2, down_x], col1, down_y, down_d)
+    gate_a, up_a = gate([w_gate[0], w_up[0]])
+    x2, y2, col3 = swap(col2, X), swap(col2, Y), swap(col2, Z)
+    gate_b, up_b = swap(gate_a, CORE), swap(up_a, CORE)
+    down_mine = jnp.concatenate([cut(0), down_x, down_y, down_d], axis=0)
+
+    to_x, to_y, to_z, down_mine, w_0 = gate(
+        [y2[half:], x2[:half], x2[:half], down_mine, weights], col3, gate_b, up_b
+    )
+    high2, low2, z_x_low = swap(to_x, X), swap(to_y, Y), swap(to_z, Z)
+    down_w = [down_mine, swap(down_mine, CORE)]
     w_x = swap(w_0, X)
-    down_mine = jnp.concatenate([cut(0), down_x, down_y, down_d], axis=0)
-    down_w = [down_mine, swap(down_mine, CORE)]
     swiglu_w = [w_gate[0], gate_b, w_up[0], up_b]
 
-    col3 = jnp.where((z == 0) | (z == 3), ends, jnp.where(z == 1, dn1, up1))
-    to_x, to_y, to_z, w_0 = gate(
+    col1, low2, w_0, to_z = gate(
+        [col1, low2, w_0, x2[half:]], high2, down_w[1], w_x, z_x_low
+    )
+    x1, y1, z_x_high = swap(col1, X), swap(col1, Y), swap(to_z, Z)
+    hidden_2 = swiglu(
+        [(col2, rows, 0), (x2, rows, 0), (y2, rows, 0), (low2, half, 0), (high2, half, 0)],
+        swiglu_w,
+    )
+    hidden_2, y2 = gate([hidden_2, y2], z_x_high)
+    all_2 = [hidden_2, swap(hidden_2, X), swap(hidden_2, Y)]
+    z_y = swap(y2, Z)
+    x1, all_2[0] = gate([x1, all_2[0]], y1)
+    all_2.append(swap(all_2[0], X + Y))
+
+    to_x, to_y, to_z, all_2[0], w_0 = gate(
         [
-            join(col3[half:], y2[half:]),
-            join(col3[:half], x2[:half]),
-            join(x2[:half], y2[half:]),
+            join(y1[half:], tokens[:half]),
+            join(x1[:half], tokens[half:]),
+            join(low2, high2),
+            all_2[0],
             w_0,
         ],
-        down_w[1],
-        gate_b,
-        w_x,
-    )
-    x3, y3, z3 = swap(to_x, X), swap(to_y, Y), swap(to_z, Z)
+        z_y,
+        *all_2[1:],
+    )
+    x4, y4, zb = swap(to_x, X), swap(to_y, Y), swap(to_z, Z)
     w_y = swap(w_0, Y)
-
-    col1, to_z, w_0 = gate([col1, join(y3[half:], x3[half:]), w_0], z3, up_b, w_y)
-    x1, y1, d3 = swap(col1, X), swap(col1, Y), swap(to_z, Z)
+    first, second = outputs(all_2, split=True)
+    back_2 = [swap(first, 2 * Z)]
+
+    to_x, to_y, second, w_0 = gate(
+        [tokens[half:], tokens[:half], second, w_0], zb, x4, y4, w_y
+    )
+    x5, y5 = swap(to_x, X), swap(to_y, Y)
+    back_2.append(swap(second, 2 * Z))
     w_d = swap(w_0, X + Y)
-    (mark,) = gate([x2])
-    all_2 = spread(
-        swiglu(
-            [(col2, rows, 0), (mark, rows, 0), (y2, rows, 0), (y3, half, 1), (x3, half, 1)],
-            swiglu_w,
-        )
-    )
-
-    to_x, to_y, all_2[0] = gate([y1[half:], x1[:half], all_2[0]], d3, w_d, *all_2[1:])
-    high1, low1 = swap(to_x, X), swap(to_y, Y)
-    (out_2,) = outputs(all_2)
-    back_2 = [swap(out_2, 2 * Z)]
-    (own,) = gate([tokens], low1, high1)
-    x0, y0 = swap(own, X), swap(own, Y)
     (mark,) = gate([col3])
     all_3 = spread(
         swiglu(
             [
                 (mark, rows, 0),
-                (z3, half, 0),
-                (x3, half, 0),
-                (y3, half, 0),
-                (z3, half, 1),
-                (d3, rows, 0),
+                (z_x_low, half, 0),
+                (z_x_high, half, 0),
+                (z_y, rows, 0),
+                (zb, rows, 0),
+            ],
+            swiglu_w,
+        ),
+        x5,
+        y5,
+        back_2[0],
+    )
+    (mark,) = gate([col1])
+    hidden_1 = swiglu(
+        [(mark, rows, 0), (x1, rows, 0), (y1, rows, 0), (y4, half, 0), (x4, half, 0)], swiglu_w
+    )
+
+    to_x, to_y, all_3[0], hidden_1 = gate(
+        [y4[half:], x4[half:], all_3[0], hidden_1], w_d, back_2[1], *all_3[1:]
+    )
+    xe, ye = swap(to_x, X), swap(to_y, Y)
+    (out_3,) = outputs(all_3)
+    back_3 = [swap(out_3, 3 * Z)]
+    (hidden_1,) = gate([hidden_1])
+    all_1 = [hidden_1, swap(hidden_1, X), swap(hidden_1, Y)]
+
+    xe, all_1[0] = gate([xe, all_1[0]], ye)
+    all_1.append(swap(all_1[0], X + Y))
+    all_0 = spread(
+        swiglu(
+            [
+                (tokens, rows, 0),
+                (x4, half, 1),
+                (x5, half, 0),
+                (y5, half, 0),
+                (y4, half, 1),
+                (ye, half, 0),
+                (xe, half, 0),
             ],
             swiglu_w,
         )
     )
-    (mark,) = gate([col1])
-    hidden_1 = swiglu(
-        [(mark, rows, 0), (x1, rows, 0), (y1, rows, 0), (low1, half, 0), (high1, half, 0)],
-        swiglu_w,
-    )
-
-    to_x, to_y, all_3[0], hidden_1 = gate(
-        [y0[half:], x0[:half], all_3[0], hidden_1], *all_3[1:]
-    )
-    xe, ye = swap(to_x, X), swap(to_y, Y)
-    (hidden_1,) = gate([hidden_1])
-    all_1 = [hidden_1, swap(hidden_1, X), swap(hidden_1, Y)]
-    (out_3,) = outputs(all_3)
-    back_3 = [swap(out_3, 3 * Z)]
-    xe, all_1[0] = gate([xe, all_1[0]], ye, *back_2)
-    all_1.append(swap(all_1[0], X + Y))
-    all_0 = spread(
-        swiglu(
-            [(own, rows, 0), (x0, rows, 0), (y0, rows, 0), (ye, half, 0), (xe, half, 0)],
-            swiglu_w,
-        )
-    )
     (out_1,) = outputs(all_1, *all_1[1:])
     back_1 = [swap(out_1, Z)]
     (all_0[0],) = gate([all_0[0]], *all_0[1:])
+    back_2 = [jnp.concatenate(back_2, axis=0)]
     weights = jnp.concatenate([w_0, w_x, w_y, w_d], axis=0)
     weights = jnp.concatenate(
         [
@@ -308,7 +312,9 @@
         ],
         axis=1,
     )
-    mixed = down(all_0, down_w, [weights, back_1[0], back_2[0], back_3[0]]).reshape(4, rows, part)
+    sums = [down(all_0, down_w), back_1[0], back_2[0], back_3[0]]
+    total = sum(weights[:, k : k + 1] * sums[k].astype(jnp.float32) for k in range(PLANES))
+    mixed = total.astype(jnp.bfloat16).reshape(4, rows, part)
     pieces = [mixed[0], swap(mixed[1], X), swap(mixed[2], Y), swap(mixed[3], X + Y)]
     result = []
     for a in range(4):

time: 265 us -> 250 us (0.943)
  Pallas kernels: 55.4 us -> 46.9 us
  waiting for transfers between devices: 129 us -> 124 us
  other arithmetic: 8.96 us -> 5.25 us
  local copies, waits for them, and re-layouts: 13.6 us -> 17 us
    ppermute x5 -> x0, waiting for transfers between devices: 32.6 us -> none  [shift(): lax.ppermute(value, 'node', [(p * GROUP + m, q * GROUP + m) for p, q in m...]
    ppermute x41 -> x47, waiting for transfers between devices: 96.7 us -> 124 us  [swap(): return lax.ppermute(value, 'node', [(i, i ^ bits) for i in range(COUNT)])]
    ppermute x5 -> x0, starting transfers between devices: 11.3 us -> none  [shift(): lax.ppermute(value, 'node', [(p * GROUP + m, q * GROUP + m) for p, q in m...]
    ppermute x41 -> x47, starting transfers between devices: 45.2 us -> 56.2 us  [swap(): return lax.ppermute(value, 'node', [(i, i ^ bits) for i in range(COUNT)])]
    unnamed x25 -> x27, local copies, waits for them, and re-layouts: 5.02 us -> 11.8 us
    pallas_call x4, Pallas kernels: 38.2 us -> 32.8 us  [swiglu(): pl.pallas_call(swiglu_kernel, out_shape=jax.ShapeDtypeStruct((rows, hidde...]
    select_n x2 -> x0, other arithmetic: 4.73 us -> none  [the longest x1 2.85 us: four_planes(): col2 = jnp.where(z < 2, dn2, up2)]
    pallas_call x4, Pallas kernels: 17.1 us -> 14.1 us  [down(): pl.pallas_call(down_kernel, out_shape=jax.ShapeDtypeStruct((rows, width),...]
  transfers between devices with their start and end apart: 46 -> 47, of which waited for: 24 -> 21; matrix products, arithmetic and copies ran while one was open for 5% -> 4% of each run, Pallas kernels for 18% -> 19%
where the time goes in v4:
time: 250 us; the launch traced here: 249 us
  waiting for transfers between devices  124 us (50%)
  starting transfers between devices  56.2 us (22%)
  Pallas kernels  46.9 us (19%)
  local copies, waits for them, and re-layouts  17 us (7%)
  other arithmetic  5.25 us (2%)
    ppermute x47, waiting for transfers between devices, swap(): return lax.ppermute(value, 'node', [(i, i ^ bits) for i in range(COUNT)])  124 us
    ppermute x47, starting transfers between devices, swap(): return lax.ppermute(value, 'node', [(i, i ^ bits) for i in range(COUNT)])  56.2 us
    pallas_call x4, Pallas kernels, swiglu(): pl.pallas_call(swiglu_kernel, out_shape=jax.ShapeDtypeStruct((rows, hidde...  32.8 us
    pallas_call x4, Pallas kernels, down(): pl.pallas_call(down_kernel, out_shape=jax.ShapeDtypeStruct((rows, width),...  14.1 us
    unnamed x27, local copies, waits for them, and re-layouts  11.8 us
  transfers between devices with their start and end apart: 47, of which 21 were waited for; matrix products, arithmetic and copies ran while one was open for 4% of the time, Pallas kernels for 19%

profile of v4, /device:TPU:0, one launch (start us, length us, event | category | flops | bytes accessed | tf_op | source)
XLA Modules:
  0.0 249.5 jit_solution(3346111513076259557)
XLA Ops:
  0.0 3.0 %collective-permute-start.2 = (bf16[64,7168]{1,0:T(8,128)(2,1)}, bf16[64,7168]{1,0:T(8,128)(2,1)S(1)}, u32[]{:S(2)}, u32[]{:S(2)}) collective-permute-start(bf16[64,7168]{1,0:T(8,128)(2,1)} %refs_0_.1), channel_id=1, source_target_pairs={{0,8},{1,9},{2,10},{3,11},{4,12},{5,13},{6,14},{7,15},{8,0},{9,1},... | collective-permute-start | bytes 2752520 | tf_op jit(solution)/shard_map/ppermute | solution.py:62
  5.6 3.3 %dynamic-slice_bitcast_fusion = (bf16[256,1792]{1,0:T(8,128)(2,1)}, bf16[256,1792]{1,0:T(8,128)(2,1)S(1)}, bf16[256,1792]{1,0:T(8,128)(2,1)S(1)}, bf16[256,1792]{1,0:T(8,128)(2,1)S(1)}) fusion(bf16[1,256,7168]{2,1,0:T(8,128)(2,1)} %param.11, s32[]{:T(128)S(6)} %select_n.106, s32[]{:T(128)S(6)} %select_n.104, s32[]{:T(128)S(6)} %select_n.103, s32[]{:T(128)S(6)} %select_n.105), kind=kLoop, calls=%fused_computation.6 | loop fusion | bytes 7340048 | tf_op jit(solution)/shard_map/dynamic_slice | solution.py:185
  17.6 25.5 %collective-permute-done.2.refs_3_.refs_1_ = bf16[64,7168]{1,0:T(8,128)(2,1)S(1)} collective-permute-done((bf16[64,7168]{1,0:T(8,128)(2,1)}, bf16[64,7168]{1,0:T(8,128)(2,1)S(1)}, u32[]{:S(2)}, u32[]{:S(2)}) %collective-permute-start.2) | collective-permute-done | bytes 917536 | tf_op jit(solution)/shard_map/ppermute | solution.py:62
  45.8 5.5 %collective-permute-done.4.refs_5_ = bf16[256,1792]{1,0:T(8,128)(2,1)S(1)} collective-permute-done((bf16[256,1792]{1,0:T(8,128)(2,1)S(1)}, bf16[256,1792]{1,0:T(8,128)(2,1)S(1)}, u32[]{:S(2)}, u32[]{:S(2)}) %collective-permute-start.4) | collective-permute-done | bytes 917536 | tf_op jit(solution)/shard_map/ppermute | solution.py:62
  58.0 17.4 %collective-permute-done.6.refs_1_ = bf16[64,7168]{1,0:T(8,128)(2,1)} collective-permute-done((bf16[64,7168]{1,0:T(8,128)(2,1)}, bf16[64,7168]{1,0:T(8,128)(2,1)}, u32[]{:S(2)}, u32[]{:S(2)}) %collective-permute-start.6) | collective-permute-done | bytes 917536 | tf_op jit(solution)/shard_map/ppermute | solution.py:62
  82.1 9.7 %collective-permute-done.13.refs_7_ = f32[64,4]{1,0:T(8,128)S(1)} collective-permute-done((f32[64,4]{1,0:T(8,128)S(1)}, f32[64,4]{1,0:T(8,128)S(1)}, u32[]{:S(2)}, u32[]{:S(2)}) %collective-permute-start.13) | collective-permute-done | bytes 1056 | tf_op jit(solution)/shard_map/ppermute | solution.py:62
  96.7 8.4 %shard_map.68.refs_1_ = bf16[256,512]{1,0:T(8,128)(2,1)S(1)} custom-call(bf16[64,7168]{1,0:T(8,128)(2,1)} %get-tuple-element.73.refs_0_, bf16[64,7168]{1,0:T(8,128)(2,1)} %collective-permute-done.6.refs_1_, bf16[64,7168]{1,0:T(8,128)(2,1)S(1)} %collective-permute-done.5.refs_2_, bf16[32,7168]{1,0:T(8,128)(2,1)S(1)} %get-tuple-element.84.refs_3_, ...), custom_call_target="tpu_custom_call" | custom-call | flops 1000 | bytes 1000 | tf_op jit(solution)/shard_map/pallas_call | solution.py:93
  108.9 10.3 %collective-permute-done.20.refs_8_.by_y = bf16[256,512]{1,0:T(8,128)(2,1)S(1)} collective-permute-done((bf16[256,512]{1,0:T(8,128)(2,1)S(1)}, bf16[256,512]{1,0:T(8,128)(2,1)S(1)}, u32[]{:S(2)}, u32[]{:S(2)}) %collective-permute-start.20) | collective-permute-done | bytes 262176 | tf_op jit(solution)/shard_map/ppermute | solution.py:62
  122.0 4.8 %collective-permute-done.21.refs_9_.across = bf16[256,512]{1,0:T(8,128)(2,1)S(1)} collective-permute-done((bf16[256,512]{1,0:T(8,128)(2,1)S(1)}, bf16[256,512]{1,0:T(8,128)(2,1)S(1)}, u32[]{:S(2)}, u32[]{:S(2)}) %collective-permute-start.21) | collective-permute-done | bytes 262176 | tf_op jit(solution)/shard_map/ppermute | solution.py:62
  132.1 3.3 %shard_map.73 = bf16[256,1792]{1,0:T(8,128)(2,1)S(1)} custom-call(bf16[256,512]{1,0:T(8,128)(2,1)S(1)} %get-tuple-element.97.own, bf16[256,512]{1,0:T(8,128)(2,1)S(1)} %collective-permute-done.19.refs_7_.by_x, bf16[256,512]{1,0:T(8,128)(2,1)S(1)} %collective-permute-done.20.refs_8_.by_y, bf16[256,512]{1,0:T(8,128)(2,1)S(1)} %collective-permute-done.21.refs_9_.across, ...), custom_call_target="tpu_custom_call" | custom-call | flops 1000 | bytes 1000 | tf_op jit(solution)/shard_map/pallas_call | solution.py:139
  136.0 14.1 %collective-permute-done.25.refs_8_ = f32[64,4]{1,0:T(8,128)S(1)} collective-permute-done((f32[64,4]{1,0:T(8,128)S(1)}, f32[64,4]{1,0:T(8,128)S(1)}, u32[]{:S(2)}, u32[]{:S(2)}) %collective-permute-start.25) | collective-permute-done | bytes 1056 | tf_op jit(solution)/shard_map/ppermute | solution.py:62
  150.1 7.2 %collective-permute-done.22.refs_5_.refs_4_ = bf16[64,7168]{1,0:T(8,128)(2,1)S(1)} collective-permute-done((bf16[64,7168]{1,0:T(8,128)(2,1)S(1)}, bf16[64,7168]{1,0:T(8,128)(2,1)S(1)}, u32[]{:S(2)}, u32[]{:S(2)}) %collective-permute-start.22) | collective-permute-done | bytes 917536 | tf_op jit(solution)/shard_map/ppermute | solution.py:62
  159.8 8.1 %shard_map.77.refs_1_ = bf16[256,512]{1,0:T(8,128)(2,1)S(1)} custom-call(bf16[64,7168]{1,0:T(8,128)(2,1)S(1)} %get-tuple-element.107.refs_0_, bf16[32,7168]{1,0:T(8,128)(2,1)S(1)} %collective-permute-done.14.refs_8_.refs_1_, bf16[32,7168]{1,0:T(8,128)(2,1)S(1)} %collective-permute-done.15.refs_3_.refs_2_, ...), custom_call_target="tpu_custom_call" | custom-call | flops 1000 | bytes 1000 | tf_op jit(solution)/shard_map/pallas_call | solution.py:93
  169.2 3.9 %collective-permute-start.33 = (bf16[256,512]{1,0:T(8,128)(2,1)S(1)}, bf16[256,512]{1,0:T(8,128)(2,1)S(1)}, u32[]{:S(2)}, u32[]{:S(2)}) collective-permute-start(bf16[256,512]{1,0:T(8,128)(2,1)S(1)} %get-tuple-element.113.refs_3_), channel_id=1, source_target_pairs={{0,6},{1,7},{2,4},{3,5},{4,2},{5,3},{6,0},{7,1},{8,14},{9,15},{10,... | collective-permute-start | bytes 786440 | tf_op jit(solution)/shard_map/ppermute | solution.py:62
  173.7 2.9 %collective-permute-start.26 = (f32[64,4]{1,0:T(8,128)S(1)}, f32[64,4]{1,0:T(8,128)S(1)}, u32[]{:S(2)}, u32[]{:S(2)}) collective-permute-start(f32[64,4]{1,0:T(8,128)S(1)} %get-tuple-element.104), channel_id=1, source_target_pairs={{0,6},{1,7},{2,4},{3,5},{4,2},{5,3},{6,0},{7,1},{8,14},{9,15},{10,... | collective-permute-start | bytes 3080 | tf_op jit(solution)/shard_map/ppermute | solution.py:62
  176.7 8.1 %shard_map.80.refs_4_ = bf16[256,512]{1,0:T(8,128)(2,1)S(1)} custom-call(bf16[64,7168]{1,0:T(8,128)(2,1)S(1)} %get-tuple-element.114.refs_0_, bf16[64,7168]{1,0:T(8,128)(2,1)S(1)} %get-tuple-element.90.refs_1_, bf16[64,7168]{1,0:T(8,128)(2,1)S(1)} %collective-permute-done.17.refs_3_.refs_2_, ...), custom_call_target="tpu_custom_call" | custom-call | flops 1000 | bytes 1000 | tf_op jit(solution)/shard_map/pallas_call | solution.py:93
  185.6 3.3 %shard_map.83.refs_1_ = bf16[256,1792]{1,0:T(8,128)(2,1)S(1)} custom-call(bf16[256,512]{1,0:T(8,128)(2,1)S(1)} %get-tuple-element.119.own, bf16[256,512]{1,0:T(8,128)(2,1)S(1)} %collective-permute-done.31.refs_7_.by_x, bf16[256,512]{1,0:T(8,128)(2,1)S(1)} %collective-permute-done.32.refs_8_.by_y, ...), custom_call_target="tpu_custom_call" | custom-call | flops 1000 | bytes 1000 | tf_op jit(solution)/shard_map/pallas_call | solution.py:139
  192.5 8.0 %collective-permute-done.37.refs_3_.by_y = bf16[256,512]{1,0:T(8,128)(2,1)S(1)} collective-permute-done((bf16[256,512]{1,0:T(8,128)(2,1)S(1)}, bf16[256,512]{1,0:T(8,128)(2,1)S(1)}, u32[]{:S(2)}, u32[]{:S(2)}) %collective-permute-start.37) | collective-permute-done | bytes 262176 | tf_op jit(solution)/shard_map/ppermute | solution.py:62
  202.7 8.2 %shard_map.87.refs_1_ = bf16[256,512]{1,0:T(8,128)(2,1)S(1)} custom-call(bf16[64,7168]{1,0:T(8,128)(2,1)S(1)} %copy-done.9, bf16[64,7168]{1,0:T(8,128)(2,1)S(1)} %collective-permute-done.23.refs_6_.refs_4_.refs_1_, bf16[32,7168]{1,0:T(8,128)(2,1)S(1)} %collective-permute-done.27.refs_2_, bf16[32,7168]{1,0:T(8,128)(2,1)S(1)} %collective-permute-done.28.refs_3_, ...), custom_call_target="tpu_custom_call" | custom-call | flops 1000 | bytes 1000 | tf_op jit(solution)/shard_map/pallas_call | solution.py:93
  210.9 3.4 %shard_map.90.refs_1_ = bf16[256,1792]{1,0:T(8,128)(2,1)S(1)} custom-call(bf16[256,512]{1,0:T(8,128)(2,1)S(1)} %get-tuple-element.131.own, bf16[256,512]{1,0:T(8,128)(2,1)S(1)} %collective-permute-done.36.refs_2_.by_x, bf16[256,512]{1,0:T(8,128)(2,1)S(1)} %collective-permute-done.37.refs_3_.by_y, ...), custom_call_target="tpu_custom_call" | custom-call | flops 1000 | bytes 1000 | tf_op jit(solution)/shard_map/pallas_call | solution.py:139
  219.1 3.5 %collective-permute-done.41.refs_4_.across = bf16[256,512]{1,0:T(8,128)(2,1)S(1)} collective-permute-done((bf16[256,512]{1,0:T(8,128)(2,1)S(1)}, bf16[256,512]{1,0:T(8,128)(2,1)S(1)}, u32[]{:S(2)}, u32[]{:S(2)}) %collective-permute-start.41) | collective-permute-done | bytes 262176 | tf_op jit(solution)/shard_map/ppermute | solution.py:62
  229.4 4.1 %shard_map.93 = bf16[256,1792]{1,0:T(8,128)(2,1)S(1)} custom-call(bf16[256,512]{1,0:T(8,128)(2,1)S(1)} %get-tuple-element.134.own, bf16[256,512]{1,0:T(8,128)(2,1)} %collective-permute-done.39.refs_2_.by_x, bf16[256,512]{1,0:T(8,128)(2,1)} %collective-permute-done.40.refs_3_.by_y, bf16[256,512]{1,0:T(8,128)(2,1)S(1)} %collective-permute-done.41.refs_4_.across, ...), custom_call_target="tpu_custom_call" | custom-call | flops 1000 | bytes 1000 | tf_op jit(solution)/shard_map/pallas_call | solution.py:139
  233.5 3.1 %collective-permute-done.42 = bf16[256,1792]{1,0:T(8,128)(2,1)} collective-permute-done((bf16[256,1792]{1,0:T(8,128)(2,1)S(1)}, bf16[256,1792]{1,0:T(8,128)(2,1)}, u32[]{:S(2)}, u32[]{:S(2)}) %collective-permute-start.42) | collective-permute-done | bytes 917536 | tf_op jit(solution)/shard_map/ppermute | solution.py:62
  242.5 3.5 %collective-permute-done.44 = bf16[64,1792]{1,0:T(8,128)(2,1)S(1)} collective-permute-done((bf16[64,1792]{1,0:T(8,128)(2,1)S(1)}, bf16[64,1792]{1,0:T(8,128)(2,1)S(1)}, u32[]{:S(2)}, u32[]{:S(2)}) %collective-permute-start.44) | collective-permute-done | bytes 229408 | tf_op jit(solution)/shard_map/ppermute | solution.py:62
  (154 shorter events, 76.4 us)
Async XLA Ops:
  0.0 43.1 %collective-permute-start.2 = (bf16[64,7168]{1,0:T(8,128)(2,1)}, bf16[64,7168]{1,0:T(8,128)(2,1)S(1)}, u32[]{:S(2)}, u32[]{:S(2)}) collective-permute-start(bf16[64,7168]{1,0:T(8,128)(2,1)} %refs_0_.1), channel_id=1, source_target_pairs={{0,8},{1,9},{2,10},{3,11},{4,12},{5,13},{6,14},{7,15},{8,0},{9,1},... | collective-permute-start | bytes 2752520 | tf_op jit(solution)/shard_map/ppermute | solution.py:62
  3.0 42.7 %collective-permute-start = (bf16[64,7168]{1,0:T(8,128)(2,1)}, bf16[64,7168]{1,0:T(8,128)(2,1)}, u32[]{:S(2)}, u32[]{:S(2)}) collective-permute-start(bf16[64,7168]{1,0:T(8,128)(2,1)} %refs_0_.1), channel_id=1, source_target_pairs={{0,16},{1,17},{2,18},{3,19},{4,20},{5,21},{6,22},{7,23},{8,24},{9,... | collective-permute-start | bytes 2752520 | tf_op jit(solution)/shard_map/ppermute | solution.py:62
  8.9 36.8 %collective-permute-start.3 = (bf16[256,1792]{1,0:T(8,128)(2,1)S(1)}, bf16[256,1792]{1,0:T(8,128)(2,1)S(1)}, u32[]{:S(2)}, u32[]{:S(2)}) collective-permute-start(bf16[256,1792]{1,0:T(8,128)(2,1)S(1)} %get-tuple-element.142), channel_id=1, source_target_pairs={{0,4},{1,5},{2,6},{3,7},{4,0},{5,1},{6,2},{7,3},{8,12},{9,13},{10,... | collective-permute-start | bytes 2752520 | tf_op jit(solution)/shard_map/ppermute | solution.py:62
  10.5 35.3 %collective-permute-start.1 = (bf16[256,1792]{1,0:T(8,128)(2,1)S(1)}, bf16[256,1792]{1,0:T(8,128)(2,1)S(1)}, u32[]{:S(2)}, u32[]{:S(2)}) collective-permute-start(bf16[256,1792]{1,0:T(8,128)(2,1)S(1)} %get-tuple-element.143), channel_id=1, source_target_pairs={{0,2},{1,3},{2,0},{3,1},{4,6},{5,7},{6,4},{7,5},{8,10},{9,11},{10,... | collective-permute-start | bytes 2752520 | tf_op jit(solution)/shard_map/ppermute | solution.py:62
  12.0 39.4 %collective-permute-start.4 = (bf16[256,1792]{1,0:T(8,128)(2,1)S(1)}, bf16[256,1792]{1,0:T(8,128)(2,1)S(1)}, u32[]{:S(2)}, u32[]{:S(2)}) collective-permute-start(bf16[256,1792]{1,0:T(8,128)(2,1)S(1)} %get-tuple-element.144), channel_id=1, source_target_pairs={{0,6},{1,7},{2,4},{3,5},{4,2},{5,3},{6,0},{7,1},{8,14},{9,15},{10,... | collective-permute-start | bytes 2752520 | tf_op jit(solution)/shard_map/ppermute | solution.py:62
  52.3 24.5 %collective-permute-start.8 = (bf16[7168,256]{1,0:T(8,128)(2,1)}, bf16[7168,256]{1,0:T(8,128)(2,1)}, u32[]{:S(2)}, u32[]{:S(2)}) collective-permute-start(bf16[7168,256]{1,0:T(8,128)(2,1)} %get-tuple-element.75), channel_id=1, source_target_pairs={{0,1},{1,0},{2,3},{3,2},{4,5},{5,4},{6,7},{7,6},{8,9},{9,8},{10,11... | collective-permute-start | bytes 11010056 | tf_op jit(solution)/shard_map/ppermute | solution.py:62
  52.3 24.6 %collective-permute-start.9 = (bf16[7168,256]{1,0:T(8,128)(2,1)}, bf16[7168,256]{1,0:T(8,128)(2,1)}, u32[]{:S(2)}, u32[]{:S(2)}) collective-permute-start(bf16[7168,256]{1,0:T(8,128)(2,1)} %get-tuple-element.76), channel_id=1, source_target_pairs={{0,1},{1,0},{2,3},{3,2},{4,5},{5,4},{6,7},{7,6},{8,9},{9,8},{10,11... | collective-permute-start | bytes 11010056 | tf_op jit(solution)/shard_map/ppermute | solution.py:62
  52.8 22.6 %collective-permute-start.6 = (bf16[64,7168]{1,0:T(8,128)(2,1)}, bf16[64,7168]{1,0:T(8,128)(2,1)}, u32[]{:S(2)}, u32[]{:S(2)}) collective-permute-start(bf16[64,7168]{1,0:T(8,128)(2,1)} %get-tuple-element.73.refs_0_), channel_id=1, source_target_pairs={{0,2},{1,3},{2,0},{3,1},{4,6},{5,7},{6,4},{7,5},{8,10},{9,11},{10,... | collective-permute-start | bytes 2752520 | tf_op jit(solution)/shard_map/ppermute | solution.py:62
  54.4 22.4 %collective-permute-start.7 = (bf16[64,7168]{1,0:T(8,128)(2,1)}, bf16[64,7168]{1,0:T(8,128)(2,1)S(1)}, u32[]{:S(2)}, u32[]{:S(2)}) collective-permute-start(bf16[64,7168]{1,0:T(8,128)(2,1)} %get-tuple-element.73.refs_0_), channel_id=1, source_target_pairs={{0,8},{1,9},{2,10},{3,11},{4,12},{5,13},{6,14},{7,15},{8,0},{9,1},... | collective-permute-start | bytes 2752520 | tf_op jit(solution)/shard_map/ppermute | solution.py:62
  54.8 21.9 %collective-permute-start.5 = (bf16[64,7168]{1,0:T(8,128)(2,1)}, bf16[64,7168]{1,0:T(8,128)(2,1)S(1)}, u32[]{:S(2)}, u32[]{:S(2)}) collective-permute-start(bf16[64,7168]{1,0:T(8,128)(2,1)} %get-tuple-element.73.refs_0_), channel_id=1, source_target_pairs={{0,4},{1,5},{2,6},{3,7},{4,0},{5,1},{6,2},{7,3},{8,12},{9,13},{10,... | collective-permute-start | bytes 2752520 | tf_op jit(solution)/shard_map/ppermute | solution.py:62
  76.9 15.3 %collective-permute-start.12 = (bf16[1024,1792]{1,0:T(8,128)(2,1)S(1)}, bf16[1024,1792]{1,0:T(8,128)(2,1)S(1)}, u32[]{:S(2)}, u32[]{:S(2)}) collective-permute-start(bf16[1024,1792]{1,0:T(8,128)(2,1)S(1)} %get-tuple-element.81.mine), channel_id=1, source_target_pairs={{0,1},{1,0},{2,3},{3,2},{4,5},{5,4},{6,7},{7,6},{8,9},{9,8},{10,11... | collective-permute-start | bytes 11010056 | tf_op jit(solution)/shard_map/ppermute | solution.py:62
  92.2 27.2 %collective-permute-start.17 = (bf16[64,7168]{1,0:T(8,128)(2,1)S(1)}, bf16[64,7168]{1,0:T(8,128)(2,1)S(1)}, u32[]{:S(2)}, u32[]{:S(2)}) collective-permute-start(bf16[64,7168]{1,0:T(8,128)(2,1)S(1)} %get-tuple-element.87.refs_1_), channel_id=1, source_target_pairs={{0,4},{1,5},{2,6},{3,7},{4,0},{5,1},{6,2},{7,3},{8,12},{9,13},{10,... | collective-permute-start | bytes 2752520 | tf_op jit(solution)/shard_map/ppermute | solution.py:62
  92.8 26.6 %collective-permute-start.16 = (bf16[64,7168]{1,0:T(8,128)(2,1)S(1)}, bf16[64,7168]{1,0:T(8,128)(2,1)S(1)}, u32[]{:S(2)}, u32[]{:S(2)}) collective-permute-start(bf16[64,7168]{1,0:T(8,128)(2,1)S(1)} %get-tuple-element.87.refs_1_), channel_id=1, source_target_pairs={{0,2},{1,3},{2,0},{3,1},{4,6},{5,7},{6,4},{7,5},{8,10},{9,11},{10,... | collective-permute-start | bytes 2752520 | tf_op jit(solution)/shard_map/ppermute | solution.py:62
  107.3 20.6 %collective-permute-start.18 = (bf16[64,7168]{1,0:T(8,128)(2,1)S(1)}, bf16[64,7168]{1,0:T(8,128)(2,1)S(1)}, u32[]{:S(2)}, u32[]{:S(2)}) collective-permute-start(bf16[64,7168]{1,0:T(8,128)(2,1)S(1)} %get-tuple-element.93), channel_id=1, source_target_pairs={{0,8},{1,9},{2,10},{3,11},{4,12},{5,13},{6,14},{7,15},{8,0},{9,1},... | collective-permute-start | bytes 2752520 | tf_op jit(solution)/shard_map/ppermute | solution.py:62
  127.9 29.4 %collective-permute-start.22 = (bf16[64,7168]{1,0:T(8,128)(2,1)S(1)}, bf16[64,7168]{1,0:T(8,128)(2,1)S(1)}, u32[]{:S(2)}, u32[]{:S(2)}) collective-permute-start(bf16[64,7168]{1,0:T(8,128)(2,1)S(1)} %get-tuple-element.101), channel_id=1, source_target_pairs={{0,8},{1,9},{2,10},{3,11},{4,12},{5,13},{6,14},{7,15},{8,0},{9,1},... | collective-permute-start | bytes 2752520 | tf_op jit(solution)/shard_map/ppermute | solution.py:62
  129.4 27.9 %collective-permute-start.23 = (bf16[64,7168]{1,0:T(8,128)(2,1)S(1)}, bf16[64,7168]{1,0:T(8,128)(2,1)S(1)}, u32[]{:S(2)}, u32[]{:S(2)}) collective-permute-start(bf16[64,7168]{1,0:T(8,128)(2,1)S(1)} %get-tuple-element.102), channel_id=1, source_target_pairs={{0,2},{1,3},{2,0},{3,1},{4,6},{5,7},{6,4},{7,5},{8,10},{9,11},{10,... | collective-permute-start | bytes 2752520 | tf_op jit(solution)/shard_map/ppermute | solution.py:62
  130.1 27.2 %collective-permute-start.24 = (bf16[64,7168]{1,0:T(8,128)(2,1)S(1)}, bf16[64,7168]{1,0:T(8,128)(2,1)S(1)}, u32[]{:S(2)}, u32[]{:S(2)}) collective-permute-start(bf16[64,7168]{1,0:T(8,128)(2,1)S(1)} %get-tuple-element.103), channel_id=1, source_target_pairs={{0,4},{1,5},{2,6},{3,7},{4,0},{5,1},{6,2},{7,3},{8,12},{9,13},{10,... | collective-permute-start | bytes 2752520 | tf_op jit(solution)/shard_map/ppermute | solution.py:62
  131.6 18.5 %collective-permute-start.25 = (f32[64,4]{1,0:T(8,128)S(1)}, f32[64,4]{1,0:T(8,128)S(1)}, u32[]{:S(2)}, u32[]{:S(2)}) collective-permute-start(f32[64,4]{1,0:T(8,128)S(1)} %get-tuple-element.100.refs_4_), channel_id=1, source_target_pairs={{0,4},{1,5},{2,6},{3,7},{4,0},{5,1},{6,2},{7,3},{8,12},{9,13},{10,... | collective-permute-start | bytes 3080 | tf_op jit(solution)/shard_map/ppermute | solution.py:62
  135.6 32.4 %collective-permute-start.29 = (bf16[128,1792]{1,0:T(8,128)(2,1)S(1)}, bf16[128,1792]{1,0:T(8,128)(2,1)S(1)}, u32[]{:S(2)}, u32[]{:S(2)}) collective-permute-start(bf16[128,1792]{1,0:T(8,128)(2,1)S(1)} %get-tuple-element.110), channel_id=1, source_target_pairs={{0,16},{1,17},{2,18},{3,19},{4,20},{5,21},{6,22},{7,23},{8,24},{9,... | collective-permute-start | bytes 1376264 | tf_op jit(solution)/shard_map/ppermute | solution.py:62
  159.8 25.1 %collective-permute-start.30 = (bf16[128,1792]{1,0:T(8,128)(2,1)S(1)}, bf16[128,1792]{1,0:T(8,128)(2,1)S(1)}, u32[]{:S(2)}, u32[]{:S(2)}) collective-permute-start(bf16[128,1792]{1,0:T(8,128)(2,1)S(1)} %get-tuple-element.115), channel_id=1, source_target_pairs={{0,16},{1,17},{2,18},{3,19},{4,20},{5,21},{6,22},{7,23},{8,24},{9,... | collective-permute-start | bytes 1376264 | tf_op jit(solution)/shard_map/ppermute | solution.py:62
  169.2 15.7 %collective-permute-start.33 = (bf16[256,512]{1,0:T(8,128)(2,1)S(1)}, bf16[256,512]{1,0:T(8,128)(2,1)S(1)}, u32[]{:S(2)}, u32[]{:S(2)}) collective-permute-start(bf16[256,512]{1,0:T(8,128)(2,1)S(1)} %get-tuple-element.113.refs_3_), channel_id=1, source_target_pairs={{0,6},{1,7},{2,4},{3,5},{4,2},{5,3},{6,0},{7,1},{8,14},{9,15},{10,... | collective-permute-start | bytes 786440 | tf_op jit(solution)/shard_map/ppermute | solution.py:62
  185.0 15.5 %collective-permute-start.34 = (bf16[32,7168]{1,0:T(8,128)(2,1)S(1)}, bf16[32,7168]{1,0:T(8,128)(2,1)S(1)}, u32[]{:S(2)}, u32[]{:S(2)}) collective-permute-start(bf16[32,7168]{1,0:T(8,128)(2,1)S(1)} %get-tuple-element.123), channel_id=1, source_target_pairs={{0,2},{1,3},{2,0},{3,1},{4,6},{5,7},{6,4},{7,5},{8,10},{9,11},{10,... | collective-permute-start | bytes 1376264 | tf_op jit(solution)/shard_map/ppermute | solution.py:62
  201.3 32.2 %collective-permute-start.43 = (bf16[256,1792]{1,0:T(8,128)(2,1)S(1)}, bf16[256,1792]{1,0:T(8,128)(2,1)}, u32[]{:S(2)}, u32[]{:S(2)}) collective-permute-start(bf16[256,1792]{1,0:T(8,128)(2,1)S(1)} %get-tuple-element.136), channel_id=1, source_target_pairs={{0,24},{1,25},{2,26},{3,27},{4,28},{5,29},{6,30},{7,31},{8,16},{9,... | collective-permute-start | bytes 2752520 | tf_op jit(solution)/shard_map/ppermute | solution.py:62
  214.3 22.4 %collective-permute-start.42 = (bf16[256,1792]{1,0:T(8,128)(2,1)S(1)}, bf16[256,1792]{1,0:T(8,128)(2,1)}, u32[]{:S(2)}, u32[]{:S(2)}) collective-permute-start(bf16[256,1792]{1,0:T(8,128)(2,1)S(1)} %get-tuple-element.135), channel_id=1, source_target_pairs={{0,8},{1,9},{2,10},{3,11},{4,12},{5,13},{6,14},{7,15},{8,0},{9,1},... | collective-permute-start | bytes 2752520 | tf_op jit(solution)/shard_map/ppermute | solution.py:62
  (35 other events, 544.9 us)

commit v5 on v4

--- a/solution.py
+++ b/solution.py
@@ -106,8 +106,7 @@
     )(*[p for p, n, place in pieces], *weights)
 
 
-def down_kernel(own, by_x, by_y, across, mine, other, *rest):
-    *mix, out, hidden = rest
+def down_kernel(own, by_x, by_y, across, mine, other, out, hidden):
     rows = own.shape[0] // 4
     half = own.shape[1] // 2
 
@@ -123,16 +122,10 @@
 
     total = jnp.dot(hidden[:, : 4 * half], mine[...], preferred_element_type=jnp.float32)
     total += jnp.dot(hidden[:, 4 * half :], other[...], preferred_element_type=jnp.float32)
-    total = total.astype(out.dtype)
-    if mix:
-        weights, *others = mix
-        total = weights[:, 0:1] * total.astype(jnp.float32)
-        for k, term in enumerate(others, 1):
-            total += weights[:, k : k + 1] * term[...].astype(jnp.float32)
     out[...] = total.astype(out.dtype)
 
 
-def down(pieces, weights, mix=()):
+def down(pieces, weights, vmem=VMEM):
     rows, hidden = pieces[0].shape
     width = weights[0].shape[1]
     cols = width // 2
@@ -141,14 +134,12 @@
         out_shape=jax.ShapeDtypeStruct((rows, width), jnp.bfloat16),
         grid=(2,),
         in_specs=[pl.BlockSpec(p.shape, lambda i: (0, 0)) for p in pieces]
-        + [pl.BlockSpec((w.shape[0], cols), lambda i: (0, i)) for w in weights]
-        + [pl.BlockSpec(m.shape, lambda i: (0, 0)) for m in mix[:1]]
-        + [pl.BlockSpec((rows, cols), lambda i: (0, i)) for m in mix[1:]],
+        + [pl.BlockSpec((w.shape[0], cols), lambda i: (0, i)) for w in weights],
         out_specs=pl.BlockSpec((rows, cols), lambda i: (0, i)),
         scratch_shapes=[pltpu.VMEM((rows, 4 * hidden), jnp.bfloat16)],
-        compiler_params=pltpu.CompilerParams(vmem_limit_bytes=56 * 2**20 if mix else VMEM),
+        compiler_params=pltpu.CompilerParams(vmem_limit_bytes=vmem),
         cost_estimate=pl.CostEstimate(flops=1000, bytes_accessed=1000, transcendentals=0),
-    )(*pieces, *weights, *mix)
+    )(*pieces, *weights)
 
 
 def nothing(*refs):
@@ -281,11 +272,10 @@
     xe, ye = swap(to_x, X), swap(to_y, Y)
     (out_3,) = outputs(all_3)
     back_3 = [swap(out_3, 3 * Z)]
-    (hidden_1,) = gate([hidden_1])
-    all_1 = [hidden_1, swap(hidden_1, X), swap(hidden_1, Y)]
+    all_1 = [hidden_1]
 
     xe, all_1[0] = gate([xe, all_1[0]], ye)
-    all_1.append(swap(all_1[0], X + Y))
+    all_1 = spread(all_1[0])
     all_0 = spread(
         swiglu(
             [
@@ -312,7 +302,7 @@
         ],
         axis=1,
     )
-    sums = [down(all_0, down_w), back_1[0], back_2[0], back_3[0]]
+    sums = [down(all_0, down_w, 56 * 2**20), back_1[0], back_2[0], back_3[0]]
     total = sum(weights[:, k : k + 1] * sums[k].astype(jnp.float32) for k in range(PLANES))
     mixed = total.astype(jnp.bfloat16).reshape(4, rows, part)
     pieces = [mixed[0], swap(mixed[1], X), swap(mixed[2], Y), swap(mixed[3], X + Y)]

time: 250 us -> 249 us (level)
  local copies, waits for them, and re-layouts: 17 us -> 13.7 us
    unnamed x27, local copies, waits for them, and re-layouts: 11.8 us -> 8.41 us
  transfers between devices with their start and end apart: 47 -> 47, of which waited for: 21 -> 21; matrix products, arithmetic and copies ran while one was open for 4% -> 4% of each run, Pallas kernels for 19% -> 20%
where the time goes in v5:
time: 249 us; the launch traced here: 248 us
  waiting for transfers between devices  125 us (50%)
  starting transfers between devices  55 us (22%)
  Pallas kernels  48.6 us (20%)
  local copies, waits for them, and re-layouts  13.7 us (6%)
  other arithmetic  5.53 us (2%)
    ppermute x47, waiting for transfers between devices, swap(): return lax.ppermute(value, 'node', [(i, i ^ bits) for i in range(COUNT)])  125 us
    ppermute x47, starting transfers between devices, swap(): return lax.ppermute(value, 'node', [(i, i ^ bits) for i in range(COUNT)])  55 us
    pallas_call x4, Pallas kernels, swiglu(): pl.pallas_call(swiglu_kernel, out_shape=jax.ShapeDtypeStruct((rows, hidde...  32.8 us
    pallas_call x4, Pallas kernels, down(): pl.pallas_call(down_kernel, out_shape=jax.ShapeDtypeStruct((rows, width),...  15.8 us
    unnamed x27, local copies, waits for them, and re-layouts  8.41 us
  transfers between devices with their start and end apart: 47, of which 21 were waited for; matrix products, arithmetic and copies ran while one was open for 4% of the time, Pallas kernels for 20%

profile of v5, /device:TPU:0, one launch (start us, length us, event | category | flops | bytes accessed | tf_op | source)
XLA Modules:
  0.0 248.3 jit_solution(1348075700221287475)
XLA Ops:
  0.0 3.0 %collective-permute-start.2 = (bf16[64,7168]{1,0:T(8,128)(2,1)}, bf16[64,7168]{1,0:T(8,128)(2,1)S(1)}, u32[]{:S(2)}, u32[]{:S(2)}) collective-permute-start(bf16[64,7168]{1,0:T(8,128)(2,1)} %refs_0_.1), channel_id=1, source_target_pairs={{0,8},{1,9},{2,10},{3,11},{4,12},{5,13},{6,14},{7,15},{8,0},{9,1},... | collective-permute-start | bytes 2752520 | tf_op jit(solution)/shard_map/ppermute | solution.py:62
  5.6 3.3 %dynamic-slice_bitcast_fusion = (bf16[256,1792]{1,0:T(8,128)(2,1)}, bf16[256,1792]{1,0:T(8,128)(2,1)S(1)}, bf16[256,1792]{1,0:T(8,128)(2,1)S(1)}, bf16[256,1792]{1,0:T(8,128)(2,1)S(1)}) fusion(bf16[1,256,7168]{2,1,0:T(8,128)(2,1)} %param.11, s32[]{:T(128)S(6)} %select_n.106, s32[]{:T(128)S(6)} %select_n.104, s32[]{:T(128)S(6)} %select_n.103, s32[]{:T(128)S(6)} %select_n.105), kind=kLoop, calls=%fused_computation.6 | loop fusion | bytes 7340048 | tf_op jit(solution)/shard_map/dynamic_slice | solution.py:176
  17.6 25.5 %collective-permute-done.2.refs_3_.refs_1_ = bf16[64,7168]{1,0:T(8,128)(2,1)S(1)} collective-permute-done((bf16[64,7168]{1,0:T(8,128)(2,1)}, bf16[64,7168]{1,0:T(8,128)(2,1)S(1)}, u32[]{:S(2)}, u32[]{:S(2)}) %collective-permute-start.2) | collective-permute-done | bytes 917536 | tf_op jit(solution)/shard_map/ppermute | solution.py:62
  45.8 5.5 %collective-permute-done.4.refs_5_ = bf16[256,1792]{1,0:T(8,128)(2,1)S(1)} collective-permute-done((bf16[256,1792]{1,0:T(8,128)(2,1)S(1)}, bf16[256,1792]{1,0:T(8,128)(2,1)S(1)}, u32[]{:S(2)}, u32[]{:S(2)}) %collective-permute-start.4) | collective-permute-done | bytes 917536 | tf_op jit(solution)/shard_map/ppermute | solution.py:62
  58.0 17.4 %collective-permute-done.6.refs_1_ = bf16[64,7168]{1,0:T(8,128)(2,1)} collective-permute-done((bf16[64,7168]{1,0:T(8,128)(2,1)}, bf16[64,7168]{1,0:T(8,128)(2,1)}, u32[]{:S(2)}, u32[]{:S(2)}) %collective-permute-start.6) | collective-permute-done | bytes 917536 | tf_op jit(solution)/shard_map/ppermute | solution.py:62
  82.1 9.7 %collective-permute-done.13.refs_7_ = f32[64,4]{1,0:T(8,128)S(1)} collective-permute-done((f32[64,4]{1,0:T(8,128)S(1)}, f32[64,4]{1,0:T(8,128)S(1)}, u32[]{:S(2)}, u32[]{:S(2)}) %collective-permute-start.13) | collective-permute-done | bytes 1056 | tf_op jit(solution)/shard_map/ppermute | solution.py:62
  96.7 8.4 %shard_map.68.refs_1_ = bf16[256,512]{1,0:T(8,128)(2,1)S(1)} custom-call(bf16[64,7168]{1,0:T(8,128)(2,1)} %get-tuple-element.73.refs_0_, bf16[64,7168]{1,0:T(8,128)(2,1)} %collective-permute-done.6.refs_1_, bf16[64,7168]{1,0:T(8,128)(2,1)S(1)} %collective-permute-done.5.refs_2_, bf16[32,7168]{1,0:T(8,128)(2,1)S(1)} %get-tuple-element.84.refs_3_, ...), custom_call_target="tpu_custom_call" | custom-call | flops 1000 | bytes 1000 | tf_op jit(solution)/shard_map/pallas_call | solution.py:93
  108.9 10.3 %collective-permute-done.20.refs_8_.by_y = bf16[256,512]{1,0:T(8,128)(2,1)S(1)} collective-permute-done((bf16[256,512]{1,0:T(8,128)(2,1)S(1)}, bf16[256,512]{1,0:T(8,128)(2,1)S(1)}, u32[]{:S(2)}, u32[]{:S(2)}) %collective-permute-start.20) | collective-permute-done | bytes 262176 | tf_op jit(solution)/shard_map/ppermute | solution.py:62
  122.0 4.8 %collective-permute-done.21.refs_9_.across = bf16[256,512]{1,0:T(8,128)(2,1)S(1)} collective-permute-done((bf16[256,512]{1,0:T(8,128)(2,1)S(1)}, bf16[256,512]{1,0:T(8,128)(2,1)S(1)}, u32[]{:S(2)}, u32[]{:S(2)}) %collective-permute-start.21) | collective-permute-done | bytes 262176 | tf_op jit(solution)/shard_map/ppermute | solution.py:62
  132.1 3.3 %shard_map.73 = bf16[256,1792]{1,0:T(8,128)(2,1)S(1)} custom-call(bf16[256,512]{1,0:T(8,128)(2,1)S(1)} %get-tuple-element.97.own, bf16[256,512]{1,0:T(8,128)(2,1)S(1)} %collective-permute-done.19.refs_7_.by_x, bf16[256,512]{1,0:T(8,128)(2,1)S(1)} %collective-permute-done.20.refs_8_.by_y, bf16[256,512]{1,0:T(8,128)(2,1)S(1)} %collective-permute-done.21.refs_9_.across, ...), custom_call_target="tpu_custom_call" | custom-call | flops 1000 | bytes 1000 | tf_op jit(solution)/shard_map/pallas_call | solution.py:132
  136.0 14.1 %collective-permute-done.25.refs_8_ = f32[64,4]{1,0:T(8,128)S(1)} collective-permute-done((f32[64,4]{1,0:T(8,128)S(1)}, f32[64,4]{1,0:T(8,128)S(1)}, u32[]{:S(2)}, u32[]{:S(2)}) %collective-permute-start.25) | collective-permute-done | bytes 1056 | tf_op jit(solution)/shard_map/ppermute | solution.py:62
  150.1 7.2 %collective-permute-done.22.refs_5_.refs_4_ = bf16[64,7168]{1,0:T(8,128)(2,1)S(1)} collective-permute-done((bf16[64,7168]{1,0:T(8,128)(2,1)S(1)}, bf16[64,7168]{1,0:T(8,128)(2,1)S(1)}, u32[]{:S(2)}, u32[]{:S(2)}) %collective-permute-start.22) | collective-permute-done | bytes 917536 | tf_op jit(solution)/shard_map/ppermute | solution.py:62
  159.8 8.1 %shard_map.77.refs_1_ = bf16[256,512]{1,0:T(8,128)(2,1)S(1)} custom-call(bf16[64,7168]{1,0:T(8,128)(2,1)S(1)} %get-tuple-element.107.refs_0_, bf16[32,7168]{1,0:T(8,128)(2,1)S(1)} %collective-permute-done.14.refs_8_.refs_1_, bf16[32,7168]{1,0:T(8,128)(2,1)S(1)} %collective-permute-done.15.refs_3_.refs_2_, ...), custom_call_target="tpu_custom_call" | custom-call | flops 1000 | bytes 1000 | tf_op jit(solution)/shard_map/pallas_call | solution.py:93
  169.3 3.9 %collective-permute-start.33 = (bf16[256,512]{1,0:T(8,128)(2,1)S(1)}, bf16[256,512]{1,0:T(8,128)(2,1)S(1)}, u32[]{:S(2)}, u32[]{:S(2)}) collective-permute-start(bf16[256,512]{1,0:T(8,128)(2,1)S(1)} %get-tuple-element.113.refs_3_), channel_id=1, source_target_pairs={{0,6},{1,7},{2,4},{3,5},{4,2},{5,3},{6,0},{7,1},{8,14},{9,15},{10,... | collective-permute-start | bytes 786440 | tf_op jit(solution)/shard_map/ppermute | solution.py:62
  173.7 2.9 %collective-permute-start.26 = (f32[64,4]{1,0:T(8,128)S(1)}, f32[64,4]{1,0:T(8,128)S(1)}, u32[]{:S(2)}, u32[]{:S(2)}) collective-permute-start(f32[64,4]{1,0:T(8,128)S(1)} %get-tuple-element.104), channel_id=1, source_target_pairs={{0,6},{1,7},{2,4},{3,5},{4,2},{5,3},{6,0},{7,1},{8,14},{9,15},{10,... | collective-permute-start | bytes 3080 | tf_op jit(solution)/shard_map/ppermute | solution.py:62
  176.8 8.2 %shard_map.80.refs_4_ = bf16[256,512]{1,0:T(8,128)(2,1)S(1)} custom-call(bf16[64,7168]{1,0:T(8,128)(2,1)S(1)} %get-tuple-element.114.refs_0_, bf16[64,7168]{1,0:T(8,128)(2,1)S(1)} %get-tuple-element.90.refs_1_, bf16[64,7168]{1,0:T(8,128)(2,1)S(1)} %collective-permute-done.17.refs_3_.refs_2_, ...), custom_call_target="tpu_custom_call" | custom-call | flops 1000 | bytes 1000 | tf_op jit(solution)/shard_map/pallas_call | solution.py:93
  185.6 3.3 %shard_map.83.refs_1_ = bf16[256,1792]{1,0:T(8,128)(2,1)S(1)} custom-call(bf16[256,512]{1,0:T(8,128)(2,1)S(1)} %get-tuple-element.119.own, bf16[256,512]{1,0:T(8,128)(2,1)S(1)} %collective-permute-done.31.refs_7_.by_x, bf16[256,512]{1,0:T(8,128)(2,1)S(1)} %collective-permute-done.32.refs_8_.by_y, ...), custom_call_target="tpu_custom_call" | custom-call | flops 1000 | bytes 1000 | tf_op jit(solution)/shard_map/pallas_call | solution.py:132
  189.0 8.9 %collective-permute-done.34.refs_1_ = bf16[32,7168]{1,0:T(8,128)(2,1)S(1)} collective-permute-done((bf16[32,7168]{1,0:T(8,128)(2,1)S(1)}, bf16[32,7168]{1,0:T(8,128)(2,1)S(1)}, u32[]{:S(2)}, u32[]{:S(2)}) %collective-permute-start.34) | collective-permute-done | bytes 458784 | tf_op jit(solution)/shard_map/ppermute | solution.py:62
  204.5 8.2 %shard_map.87.refs_1_ = bf16[256,512]{1,0:T(8,128)(2,1)S(1)} custom-call(bf16[64,7168]{1,0:T(8,128)(2,1)S(1)} %copy-done.8, bf16[64,7168]{1,0:T(8,128)(2,1)S(1)} %collective-permute-done.23.refs_6_.refs_4_.refs_1_, bf16[32,7168]{1,0:T(8,128)(2,1)S(1)} %collective-permute-done.27.refs_2_, bf16[32,7168]{1,0:T(8,128)(2,1)S(1)} %collective-permute-done.28.refs_3_, ...), custom_call_target="tpu_custom_call" | custom-call | flops 1000 | bytes 1000 | tf_op jit(solution)/shard_map/pallas_call | solution.py:93
  214.9 3.4 %shard_map.90.refs_1_ = bf16[256,1792]{1,0:T(8,128)(2,1)S(1)} custom-call(bf16[256,512]{1,0:T(8,128)(2,1)S(1)} %get-tuple-element.131.own, bf16[256,512]{1,0:T(8,128)(2,1)S(1)} %collective-permute-done.36.refs_2_.by_x, bf16[256,512]{1,0:T(8,128)(2,1)S(1)} %collective-permute-done.37.refs_3_.by_y, ...), custom_call_target="tpu_custom_call" | custom-call | flops 1000 | bytes 1000 | tf_op jit(solution)/shard_map/pallas_call | solution.py:132
  222.4 3.5 %collective-permute-done.41.refs_4_.across = bf16[256,512]{1,0:T(8,128)(2,1)S(1)} collective-permute-done((bf16[256,512]{1,0:T(8,128)(2,1)S(1)}, bf16[256,512]{1,0:T(8,128)(2,1)S(1)}, u32[]{:S(2)}, u32[]{:S(2)}) %collective-permute-start.41) | collective-permute-done | bytes 262176 | tf_op jit(solution)/shard_map/ppermute | solution.py:62
  225.8 2.8 %collective-permute-done.40.refs_3_.by_y = bf16[256,512]{1,0:T(8,128)(2,1)} collective-permute-done((bf16[256,512]{1,0:T(8,128)(2,1)S(1)}, bf16[256,512]{1,0:T(8,128)(2,1)}, u32[]{:S(2)}, u32[]{:S(2)}) %collective-permute-start.40) | collective-permute-done | bytes 262176 | tf_op jit(solution)/shard_map/ppermute | solution.py:62
  229.3 5.8 %shard_map.93 = bf16[256,1792]{1,0:T(8,128)(2,1)} custom-call(bf16[256,512]{1,0:T(8,128)(2,1)} %copy-done.6, bf16[256,512]{1,0:T(8,128)(2,1)} %collective-permute-done.39.refs_2_.by_x, bf16[256,512]{1,0:T(8,128)(2,1)} %collective-permute-done.40.refs_3_.by_y, bf16[256,512]{1,0:T(8,128)(2,1)} %copy-done.9, bf16[1024,1792]{1,0:T(8,128)(2,1)} %copy-done, ...), custom_call_target="tpu_custom_call" | custom-call | flops 1000 | bytes 1000 | tf_op jit(solution)/shard_map/pallas_call | solution.py:132
  241.2 3.5 %collective-permute-done.44 = bf16[64,1792]{1,0:T(8,128)(2,1)S(1)} collective-permute-done((bf16[64,1792]{1,0:T(8,128)(2,1)S(1)}, bf16[64,1792]{1,0:T(8,128)(2,1)S(1)}, u32[]{:S(2)}, u32[]{:S(2)}) %collective-permute-start.44) | collective-permute-done | bytes 229408 | tf_op jit(solution)/shard_map/ppermute | solution.py:62
  (154 shorter events, 73.0 us)
Async XLA Ops:
  0.0 43.1 %collective-permute-start.2 = (bf16[64,7168]{1,0:T(8,128)(2,1)}, bf16[64,7168]{1,0:T(8,128)(2,1)S(1)}, u32[]{:S(2)}, u32[]{:S(2)}) collective-permute-start(bf16[64,7168]{1,0:T(8,128)(2,1)} %refs_0_.1), channel_id=1, source_target_pairs={{0,8},{1,9},{2,10},{3,11},{4,12},{5,13},{6,14},{7,15},{8,0},{9,1},... | collective-permute-start | bytes 2752520 | tf_op jit(solution)/shard_map/ppermute | solution.py:62
  3.0 42.7 %collective-permute-start = (bf16[64,7168]{1,0:T(8,128)(2,1)}, bf16[64,7168]{1,0:T(8,128)(2,1)}, u32[]{:S(2)}, u32[]{:S(2)}) collective-permute-start(bf16[64,7168]{1,0:T(8,128)(2,1)} %refs_0_.1), channel_id=1, source_target_pairs={{0,16},{1,17},{2,18},{3,19},{4,20},{5,21},{6,22},{7,23},{8,24},{9,... | collective-permute-start | bytes 2752520 | tf_op jit(solution)/shard_map/ppermute | solution.py:62
  8.9 36.8 %collective-permute-start.3 = (bf16[256,1792]{1,0:T(8,128)(2,1)S(1)}, bf16[256,1792]{1,0:T(8,128)(2,1)S(1)}, u32[]{:S(2)}, u32[]{:S(2)}) collective-permute-start(bf16[256,1792]{1,0:T(8,128)(2,1)S(1)} %get-tuple-element.142), channel_id=1, source_target_pairs={{0,4},{1,5},{2,6},{3,7},{4,0},{5,1},{6,2},{7,3},{8,12},{9,13},{10,... | collective-permute-start | bytes 2752520 | tf_op jit(solution)/shard_map/ppermute | solution.py:62
  10.5 35.3 %collective-permute-start.1 = (bf16[256,1792]{1,0:T(8,128)(2,1)S(1)}, bf16[256,1792]{1,0:T(8,128)(2,1)S(1)}, u32[]{:S(2)}, u32[]{:S(2)}) collective-permute-start(bf16[256,1792]{1,0:T(8,128)(2,1)S(1)} %get-tuple-element.143), channel_id=1, source_target_pairs={{0,2},{1,3},{2,0},{3,1},{4,6},{5,7},{6,4},{7,5},{8,10},{9,11},{10,... | collective-permute-start | bytes 2752520 | tf_op jit(solution)/shard_map/ppermute | solution.py:62
  12.0 39.4 %collective-permute-start.4 = (bf16[256,1792]{1,0:T(8,128)(2,1)S(1)}, bf16[256,1792]{1,0:T(8,128)(2,1)S(1)}, u32[]{:S(2)}, u32[]{:S(2)}) collective-permute-start(bf16[256,1792]{1,0:T(8,128)(2,1)S(1)} %get-tuple-element.144), channel_id=1, source_target_pairs={{0,6},{1,7},{2,4},{3,5},{4,2},{5,3},{6,0},{7,1},{8,14},{9,15},{10,... | collective-permute-start | bytes 2752520 | tf_op jit(solution)/shard_map/ppermute | solution.py:62
  52.3 24.5 %collective-permute-start.8 = (bf16[7168,256]{1,0:T(8,128)(2,1)}, bf16[7168,256]{1,0:T(8,128)(2,1)}, u32[]{:S(2)}, u32[]{:S(2)}) collective-permute-start(bf16[7168,256]{1,0:T(8,128)(2,1)} %get-tuple-element.75), channel_id=1, source_target_pairs={{0,1},{1,0},{2,3},{3,2},{4,5},{5,4},{6,7},{7,6},{8,9},{9,8},{10,11... | collective-permute-start | bytes 11010056 | tf_op jit(solution)/shard_map/ppermute | solution.py:62
  52.3 24.6 %collective-permute-start.9 = (bf16[7168,256]{1,0:T(8,128)(2,1)}, bf16[7168,256]{1,0:T(8,128)(2,1)}, u32[]{:S(2)}, u32[]{:S(2)}) collective-permute-start(bf16[7168,256]{1,0:T(8,128)(2,1)} %get-tuple-element.76), channel_id=1, source_target_pairs={{0,1},{1,0},{2,3},{3,2},{4,5},{5,4},{6,7},{7,6},{8,9},{9,8},{10,11... | collective-permute-start | bytes 11010056 | tf_op jit(solution)/shard_map/ppermute | solution.py:62
  52.8 22.6 %collective-permute-start.6 = (bf16[64,7168]{1,0:T(8,128)(2,1)}, bf16[64,7168]{1,0:T(8,128)(2,1)}, u32[]{:S(2)}, u32[]{:S(2)}) collective-permute-start(bf16[64,7168]{1,0:T(8,128)(2,1)} %get-tuple-element.73.refs_0_), channel_id=1, source_target_pairs={{0,2},{1,3},{2,0},{3,1},{4,6},{5,7},{6,4},{7,5},{8,10},{9,11},{10,... | collective-permute-start | bytes 2752520 | tf_op jit(solution)/shard_map/ppermute | solution.py:62
  54.4 22.4 %collective-permute-start.7 = (bf16[64,7168]{1,0:T(8,128)(2,1)}, bf16[64,7168]{1,0:T(8,128)(2,1)S(1)}, u32[]{:S(2)}, u32[]{:S(2)}) collective-permute-start(bf16[64,7168]{1,0:T(8,128)(2,1)} %get-tuple-element.73.refs_0_), channel_id=1, source_target_pairs={{0,8},{1,9},{2,10},{3,11},{4,12},{5,13},{6,14},{7,15},{8,0},{9,1},... | collective-permute-start | bytes 2752520 | tf_op jit(solution)/shard_map/ppermute | solution.py:62
  54.8 21.9 %collective-permute-start.5 = (bf16[64,7168]{1,0:T(8,128)(2,1)}, bf16[64,7168]{1,0:T(8,128)(2,1)S(1)}, u32[]{:S(2)}, u32[]{:S(2)}) collective-permute-start(bf16[64,7168]{1,0:T(8,128)(2,1)} %get-tuple-element.73.refs_0_), channel_id=1, source_target_pairs={{0,4},{1,5},{2,6},{3,7},{4,0},{5,1},{6,2},{7,3},{8,12},{9,13},{10,... | collective-permute-start | bytes 2752520 | tf_op jit(solution)/shard_map/ppermute | solution.py:62
  76.9 15.3 %collective-permute-start.12 = (bf16[1024,1792]{1,0:T(8,128)(2,1)S(1)}, bf16[1024,1792]{1,0:T(8,128)(2,1)S(1)}, u32[]{:S(2)}, u32[]{:S(2)}) collective-permute-start(bf16[1024,1792]{1,0:T(8,128)(2,1)S(1)} %get-tuple-element.81.mine), channel_id=1, source_target_pairs={{0,1},{1,0},{2,3},{3,2},{4,5},{5,4},{6,7},{7,6},{8,9},{9,8},{10,11... | collective-permute-start | bytes 11010056 | tf_op jit(solution)/shard_map/ppermute | solution.py:62
  76.9 14.9 %collective-permute-start.10 = (bf16[32,7168]{1,0:T(8,128)(2,1)S(1)}, bf16[32,7168]{1,0:T(8,128)(2,1)S(1)}, u32[]{:S(2)}, u32[]{:S(2)}) collective-permute-start(bf16[32,7168]{1,0:T(8,128)(2,1)S(1)} %get-tuple-element.78), channel_id=1, source_target_pairs={{0,4},{1,5},{2,6},{3,7},{4,0},{5,1},{6,2},{7,3},{8,12},{9,13},{10,... | collective-permute-start | bytes 1376264 | tf_op jit(solution)/shard_map/ppermute | solution.py:62
  92.2 27.2 %collective-permute-start.17 = (bf16[64,7168]{1,0:T(8,128)(2,1)S(1)}, bf16[64,7168]{1,0:T(8,128)(2,1)S(1)}, u32[]{:S(2)}, u32[]{:S(2)}) collective-permute-start(bf16[64,7168]{1,0:T(8,128)(2,1)S(1)} %get-tuple-element.87.refs_1_), channel_id=1, source_target_pairs={{0,4},{1,5},{2,6},{3,7},{4,0},{5,1},{6,2},{7,3},{8,12},{9,13},{10,... | collective-permute-start | bytes 2752520 | tf_op jit(solution)/shard_map/ppermute | solution.py:62
  92.8 26.6 %collective-permute-start.16 = (bf16[64,7168]{1,0:T(8,128)(2,1)S(1)}, bf16[64,7168]{1,0:T(8,128)(2,1)S(1)}, u32[]{:S(2)}, u32[]{:S(2)}) collective-permute-start(bf16[64,7168]{1,0:T(8,128)(2,1)S(1)} %get-tuple-element.87.refs_1_), channel_id=1, source_target_pairs={{0,2},{1,3},{2,0},{3,1},{4,6},{5,7},{6,4},{7,5},{8,10},{9,11},{10,... | collective-permute-start | bytes 2752520 | tf_op jit(solution)/shard_map/ppermute | solution.py:62
  107.3 20.6 %collective-permute-start.18 = (bf16[64,7168]{1,0:T(8,128)(2,1)S(1)}, bf16[64,7168]{1,0:T(8,128)(2,1)S(1)}, u32[]{:S(2)}, u32[]{:S(2)}) collective-permute-start(bf16[64,7168]{1,0:T(8,128)(2,1)S(1)} %get-tuple-element.93), channel_id=1, source_target_pairs={{0,8},{1,9},{2,10},{3,11},{4,12},{5,13},{6,14},{7,15},{8,0},{9,1},... | collective-permute-start | bytes 2752520 | tf_op jit(solution)/shard_map/ppermute | solution.py:62
  127.9 29.4 %collective-permute-start.22 = (bf16[64,7168]{1,0:T(8,128)(2,1)S(1)}, bf16[64,7168]{1,0:T(8,128)(2,1)S(1)}, u32[]{:S(2)}, u32[]{:S(2)}) collective-permute-start(bf16[64,7168]{1,0:T(8,128)(2,1)S(1)} %get-tuple-element.101), channel_id=1, source_target_pairs={{0,8},{1,9},{2,10},{3,11},{4,12},{5,13},{6,14},{7,15},{8,0},{9,1},... | collective-permute-start | bytes 2752520 | tf_op jit(solution)/shard_map/ppermute | solution.py:62
  129.4 27.9 %collective-permute-start.23 = (bf16[64,7168]{1,0:T(8,128)(2,1)S(1)}, bf16[64,7168]{1,0:T(8,128)(2,1)S(1)}, u32[]{:S(2)}, u32[]{:S(2)}) collective-permute-start(bf16[64,7168]{1,0:T(8,128)(2,1)S(1)} %get-tuple-element.102), channel_id=1, source_target_pairs={{0,2},{1,3},{2,0},{3,1},{4,6},{5,7},{6,4},{7,5},{8,10},{9,11},{10,... | collective-permute-start | bytes 2752520 | tf_op jit(solution)/shard_map/ppermute | solution.py:62
  130.1 27.2 %collective-permute-start.24 = (bf16[64,7168]{1,0:T(8,128)(2,1)S(1)}, bf16[64,7168]{1,0:T(8,128)(2,1)S(1)}, u32[]{:S(2)}, u32[]{:S(2)}) collective-permute-start(bf16[64,7168]{1,0:T(8,128)(2,1)S(1)} %get-tuple-element.103), channel_id=1, source_target_pairs={{0,4},{1,5},{2,6},{3,7},{4,0},{5,1},{6,2},{7,3},{8,12},{9,13},{10,... | collective-permute-start | bytes 2752520 | tf_op jit(solution)/shard_map/ppermute | solution.py:62
  131.6 18.5 %collective-permute-start.25 = (f32[64,4]{1,0:T(8,128)S(1)}, f32[64,4]{1,0:T(8,128)S(1)}, u32[]{:S(2)}, u32[]{:S(2)}) collective-permute-start(f32[64,4]{1,0:T(8,128)S(1)} %get-tuple-element.100.refs_4_), channel_id=1, source_target_pairs={{0,4},{1,5},{2,6},{3,7},{4,0},{5,1},{6,2},{7,3},{8,12},{9,13},{10,... | collective-permute-start | bytes 3080 | tf_op jit(solution)/shard_map/ppermute | solution.py:62
  135.6 32.4 %collective-permute-start.29 = (bf16[128,1792]{1,0:T(8,128)(2,1)S(1)}, bf16[128,1792]{1,0:T(8,128)(2,1)S(1)}, u32[]{:S(2)}, u32[]{:S(2)}) collective-permute-start(bf16[128,1792]{1,0:T(8,128)(2,1)S(1)} %get-tuple-element.110), channel_id=1, source_target_pairs={{0,16},{1,17},{2,18},{3,19},{4,20},{5,21},{6,22},{7,23},{8,24},{9,... | collective-permute-start | bytes 1376264 | tf_op jit(solution)/shard_map/ppermute | solution.py:62
  159.8 25.1 %collective-permute-start.30 = (bf16[128,1792]{1,0:T(8,128)(2,1)S(1)}, bf16[128,1792]{1,0:T(8,128)(2,1)S(1)}, u32[]{:S(2)}, u32[]{:S(2)}) collective-permute-start(bf16[128,1792]{1,0:T(8,128)(2,1)S(1)} %get-tuple-element.115), channel_id=1, source_target_pairs={{0,16},{1,17},{2,18},{3,19},{4,20},{5,21},{6,22},{7,23},{8,24},{9,... | collective-permute-start | bytes 1376264 | tf_op jit(solution)/shard_map/ppermute | solution.py:62
  169.3 15.7 %collective-permute-start.33 = (bf16[256,512]{1,0:T(8,128)(2,1)S(1)}, bf16[256,512]{1,0:T(8,128)(2,1)S(1)}, u32[]{:S(2)}, u32[]{:S(2)}) collective-permute-start(bf16[256,512]{1,0:T(8,128)(2,1)S(1)} %get-tuple-element.113.refs_3_), channel_id=1, source_target_pairs={{0,6},{1,7},{2,4},{3,5},{4,2},{5,3},{6,0},{7,1},{8,14},{9,15},{10,... | collective-permute-start | bytes 786440 | tf_op jit(solution)/shard_map/ppermute | solution.py:62
  202.8 32.3 %collective-permute-start.43 = (bf16[256,1792]{1,0:T(8,128)(2,1)S(1)}, bf16[256,1792]{1,0:T(8,128)(2,1)}, u32[]{:S(2)}, u32[]{:S(2)}) collective-permute-start(bf16[256,1792]{1,0:T(8,128)(2,1)S(1)} %get-tuple-element.136), channel_id=1, source_target_pairs={{0,24},{1,25},{2,26},{3,27},{4,28},{5,29},{6,30},{7,31},{8,16},{9,... | collective-permute-start | bytes 2752520 | tf_op jit(solution)/shard_map/ppermute | solution.py:62
  218.3 16.8 %collective-permute-start.42 = (bf16[256,1792]{1,0:T(8,128)(2,1)S(1)}, bf16[256,1792]{1,0:T(8,128)(2,1)}, u32[]{:S(2)}, u32[]{:S(2)}) collective-permute-start(bf16[256,1792]{1,0:T(8,128)(2,1)S(1)} %get-tuple-element.135), channel_id=1, source_target_pairs={{0,8},{1,9},{2,10},{3,11},{4,12},{5,13},{6,14},{7,15},{8,0},{9,1},... | collective-permute-start | bytes 2752520 | tf_op jit(solution)/shard_map/ppermute | solution.py:62
  (35 other events, 560.5 us)

commit v6 on v5

--- a/solution.py
+++ b/solution.py
@@ -62,7 +62,7 @@
     return lax.ppermute(value, "node", [(i, i ^ bits) for i in range(COUNT)])
 
 
-VMEM = 16 * 2**20
+VMEM = 20 * 2**20
 
 
 def swiglu_kernel(*refs):
@@ -89,11 +89,11 @@
     rows = sum(n for p, n, place in pieces)
     width = pieces[0][0].shape[1]
     hidden = sum(w.shape[1] for w in weights) // 2
-    depth = width // 7
+    depth = width // 4
     return pl.pallas_call(
         swiglu_kernel,
         out_shape=jax.ShapeDtypeStruct((rows, hidden), jnp.bfloat16),
-        grid=(7,),
+        grid=(4,),
         in_specs=[
             pl.BlockSpec((n, depth), lambda i, place=place: (place, i))
             for p, n, place in pieces

time: 249 us -> 247 us (level)
  waiting for transfers between devices: 125 us -> 133 us
  Pallas kernels: 48.6 us -> 43.3 us
  starting transfers between devices: 55 us -> 51 us
    ppermute x47, waiting for transfers between devices: 125 us -> 133 us  [swap(): return lax.ppermute(value, 'node', [(i, i ^ bits) for i in range(COUNT)])]
    pallas_call x4, Pallas kernels: 32.8 us -> 27.3 us  [swiglu(): pl.pallas_call(swiglu_kernel, out_shape=jax.ShapeDtypeStruct((rows, hidde...]
    ppermute x47, starting transfers between devices: 55 us -> 51 us  [swap(): return lax.ppermute(value, 'node', [(i, i ^ bits) for i in range(COUNT)])]
  transfers between devices with their start and end apart: 47 -> 47, of which waited for: 21 -> 25; matrix products, arithmetic and copies ran while one was open for 4% -> 4% of each run, Pallas kernels for 20% -> 18%
where the time goes in v6:
time: 247 us; the launch traced here: 246 us
  waiting for transfers between devices  133 us (54%)
  starting transfers between devices  51 us (21%)
  Pallas kernels  43.3 us (18%)
  local copies, waits for them, and re-layouts  13.7 us (6%)
  other arithmetic  5.52 us (2%)
    ppermute x47, waiting for transfers between devices, swap(): return lax.ppermute(value, 'node', [(i, i ^ bits) for i in range(COUNT)])  133 us
    ppermute x47, starting transfers between devices, swap(): return lax.ppermute(value, 'node', [(i, i ^ bits) for i in range(COUNT)])  51 us
    pallas_call x4, Pallas kernels, swiglu(): pl.pallas_call(swiglu_kernel, out_shape=jax.ShapeDtypeStruct((rows, hidde...  27.3 us
    pallas_call x4, Pallas kernels, down(): pl.pallas_call(down_kernel, out_shape=jax.ShapeDtypeStruct((rows, width),...  16 us
    unnamed x27, local copies, waits for them, and re-layouts  8.41 us
  transfers between devices with their start and end apart: 47, of which 25 were waited for; matrix products, arithmetic and copies ran while one was open for 4% of the time, Pallas kernels for 18%

profile of v6, /device:TPU:0, one launch (start us, length us, event | category | flops | bytes accessed | tf_op | source)
XLA Modules:
  0.0 246.4 jit_solution(16063614331413562978)
XLA Ops:
  0.0 3.0 %collective-permute-start.2 = (bf16[64,7168]{1,0:T(8,128)(2,1)}, bf16[64,7168]{1,0:T(8,128)(2,1)S(1)}, u32[]{:S(2)}, u32[]{:S(2)}) collective-permute-start(bf16[64,7168]{1,0:T(8,128)(2,1)} %refs_0_.1), channel_id=1, source_target_pairs={{0,8},{1,9},{2,10},{3,11},{4,12},{5,13},{6,14},{7,15},{8,0},{9,1},... | collective-permute-start | bytes 2752520 | tf_op jit(solution)/shard_map/ppermute | solution.py:62
  5.6 3.3 %dynamic-slice_bitcast_fusion = (bf16[256,1792]{1,0:T(8,128)(2,1)}, bf16[256,1792]{1,0:T(8,128)(2,1)S(1)}, bf16[256,1792]{1,0:T(8,128)(2,1)S(1)}, bf16[256,1792]{1,0:T(8,128)(2,1)S(1)}) fusion(bf16[1,256,7168]{2,1,0:T(8,128)(2,1)} %param.11, s32[]{:T(128)S(6)} %select_n.106, s32[]{:T(128)S(6)} %select_n.104, s32[]{:T(128)S(6)} %select_n.103, s32[]{:T(128)S(6)} %select_n.105), kind=kLoop, calls=%fused_computation.6 | loop fusion | bytes 7340048 | tf_op jit(solution)/shard_map/dynamic_slice | solution.py:176
  17.6 25.5 %collective-permute-done.2.refs_3_.refs_1_ = bf16[64,7168]{1,0:T(8,128)(2,1)S(1)} collective-permute-done((bf16[64,7168]{1,0:T(8,128)(2,1)}, bf16[64,7168]{1,0:T(8,128)(2,1)S(1)}, u32[]{:S(2)}, u32[]{:S(2)}) %collective-permute-start.2) | collective-permute-done | bytes 917536 | tf_op jit(solution)/shard_map/ppermute | solution.py:62
  45.8 5.5 %collective-permute-done.4.refs_5_ = bf16[256,1792]{1,0:T(8,128)(2,1)S(1)} collective-permute-done((bf16[256,1792]{1,0:T(8,128)(2,1)S(1)}, bf16[256,1792]{1,0:T(8,128)(2,1)S(1)}, u32[]{:S(2)}, u32[]{:S(2)}) %collective-permute-start.4) | collective-permute-done | bytes 917536 | tf_op jit(solution)/shard_map/ppermute | solution.py:62
  58.0 17.4 %collective-permute-done.6.refs_1_ = bf16[64,7168]{1,0:T(8,128)(2,1)} collective-permute-done((bf16[64,7168]{1,0:T(8,128)(2,1)}, bf16[64,7168]{1,0:T(8,128)(2,1)}, u32[]{:S(2)}, u32[]{:S(2)}) %collective-permute-start.6) | collective-permute-done | bytes 917536 | tf_op jit(solution)/shard_map/ppermute | solution.py:62
  82.1 9.7 %collective-permute-done.13.refs_7_ = f32[64,4]{1,0:T(8,128)S(1)} collective-permute-done((f32[64,4]{1,0:T(8,128)S(1)}, f32[64,4]{1,0:T(8,128)S(1)}, u32[]{:S(2)}, u32[]{:S(2)}) %collective-permute-start.13) | collective-permute-done | bytes 1056 | tf_op jit(solution)/shard_map/ppermute | solution.py:62
  96.7 7.0 %shard_map.68.refs_1_ = bf16[256,512]{1,0:T(8,128)(2,1)S(1)} custom-call(bf16[64,7168]{1,0:T(8,128)(2,1)} %get-tuple-element.73.refs_0_, bf16[64,7168]{1,0:T(8,128)(2,1)} %collective-permute-done.6.refs_1_, bf16[64,7168]{1,0:T(8,128)(2,1)S(1)} %collective-permute-done.5.refs_2_, bf16[32,7168]{1,0:T(8,128)(2,1)S(1)} %get-tuple-element.84.refs_3_, ...), custom_call_target="tpu_custom_call" | custom-call | flops 1000 | bytes 1000 | tf_op jit(solution)/shard_map/pallas_call | solution.py:93
  108.9 10.3 %collective-permute-done.20.refs_8_.by_y = bf16[256,512]{1,0:T(8,128)(2,1)S(1)} collective-permute-done((bf16[256,512]{1,0:T(8,128)(2,1)S(1)}, bf16[256,512]{1,0:T(8,128)(2,1)S(1)}, u32[]{:S(2)}, u32[]{:S(2)}) %collective-permute-start.20) | collective-permute-done | bytes 262176 | tf_op jit(solution)/shard_map/ppermute | solution.py:62
  122.0 4.8 %collective-permute-done.21.refs_9_.across = bf16[256,512]{1,0:T(8,128)(2,1)S(1)} collective-permute-done((bf16[256,512]{1,0:T(8,128)(2,1)S(1)}, bf16[256,512]{1,0:T(8,128)(2,1)S(1)}, u32[]{:S(2)}, u32[]{:S(2)}) %collective-permute-start.21) | collective-permute-done | bytes 262176 | tf_op jit(solution)/shard_map/ppermute | solution.py:62
  131.3 3.3 %shard_map.73 = bf16[256,1792]{1,0:T(8,128)(2,1)S(1)} custom-call(bf16[256,512]{1,0:T(8,128)(2,1)S(1)} %get-tuple-element.97.own, bf16[256,512]{1,0:T(8,128)(2,1)S(1)} %collective-permute-done.19.refs_7_.by_x, bf16[256,512]{1,0:T(8,128)(2,1)S(1)} %collective-permute-done.20.refs_8_.by_y, bf16[256,512]{1,0:T(8,128)(2,1)S(1)} %collective-permute-done.21.refs_9_.across, ...), custom_call_target="tpu_custom_call" | custom-call | flops 1000 | bytes 1000 | tf_op jit(solution)/shard_map/pallas_call | solution.py:132
  135.1 13.0 %collective-permute-done.25.refs_8_ = f32[64,4]{1,0:T(8,128)S(1)} collective-permute-done((f32[64,4]{1,0:T(8,128)S(1)}, f32[64,4]{1,0:T(8,128)S(1)}, u32[]{:S(2)}, u32[]{:S(2)}) %collective-permute-start.25) | collective-permute-done | bytes 1056 | tf_op jit(solution)/shard_map/ppermute | solution.py:62
  148.1 8.1 %collective-permute-done.22.refs_5_.refs_4_ = bf16[64,7168]{1,0:T(8,128)(2,1)S(1)} collective-permute-done((bf16[64,7168]{1,0:T(8,128)(2,1)S(1)}, bf16[64,7168]{1,0:T(8,128)(2,1)S(1)}, u32[]{:S(2)}, u32[]{:S(2)}) %collective-permute-start.22) | collective-permute-done | bytes 917536 | tf_op jit(solution)/shard_map/ppermute | solution.py:62
  158.7 6.7 %shard_map.77.refs_1_ = bf16[256,512]{1,0:T(8,128)(2,1)S(1)} custom-call(bf16[64,7168]{1,0:T(8,128)(2,1)S(1)} %get-tuple-element.107.refs_0_, bf16[32,7168]{1,0:T(8,128)(2,1)S(1)} %collective-permute-done.14.refs_8_.refs_1_, bf16[32,7168]{1,0:T(8,128)(2,1)S(1)} %collective-permute-done.15.refs_3_.refs_2_, ...), custom_call_target="tpu_custom_call" | custom-call | flops 1000 | bytes 1000 | tf_op jit(solution)/shard_map/pallas_call | solution.py:93
  165.5 5.0 %collective-permute-done.28.refs_3_ = bf16[32,7168]{1,0:T(8,128)(2,1)S(1)} collective-permute-done((bf16[32,7168]{1,0:T(8,128)(2,1)S(1)}, bf16[32,7168]{1,0:T(8,128)(2,1)S(1)}, u32[]{:S(2)}, u32[]{:S(2)}) %collective-permute-start.28) | collective-permute-done | bytes 458784 | tf_op jit(solution)/shard_map/ppermute | solution.py:62
  175.0 6.8 %shard_map.80.refs_4_ = bf16[256,512]{1,0:T(8,128)(2,1)S(1)} custom-call(bf16[64,7168]{1,0:T(8,128)(2,1)S(1)} %get-tuple-element.114.refs_0_, bf16[64,7168]{1,0:T(8,128)(2,1)S(1)} %get-tuple-element.90.refs_1_, bf16[64,7168]{1,0:T(8,128)(2,1)S(1)} %collective-permute-done.17.refs_3_.refs_2_, ...), custom_call_target="tpu_custom_call" | custom-call | flops 1000 | bytes 1000 | tf_op jit(solution)/shard_map/pallas_call | solution.py:93
  184.5 3.3 %shard_map.83.refs_1_ = bf16[256,1792]{1,0:T(8,128)(2,1)S(1)} custom-call(bf16[256,512]{1,0:T(8,128)(2,1)S(1)} %get-tuple-element.119.own, bf16[256,512]{1,0:T(8,128)(2,1)S(1)} %collective-permute-done.31.refs_7_.by_x, bf16[256,512]{1,0:T(8,128)(2,1)S(1)} %collective-permute-done.32.refs_8_.by_y, ...), custom_call_target="tpu_custom_call" | custom-call | flops 1000 | bytes 1000 | tf_op jit(solution)/shard_map/pallas_call | solution.py:132
  187.8 6.9 %collective-permute-done.34.refs_1_ = bf16[32,7168]{1,0:T(8,128)(2,1)S(1)} collective-permute-done((bf16[32,7168]{1,0:T(8,128)(2,1)S(1)}, bf16[32,7168]{1,0:T(8,128)(2,1)S(1)}, u32[]{:S(2)}, u32[]{:S(2)}) %collective-permute-start.34) | collective-permute-done | bytes 458784 | tf_op jit(solution)/shard_map/ppermute | solution.py:62
  200.9 6.8 %shard_map.87.refs_1_ = bf16[256,512]{1,0:T(8,128)(2,1)S(1)} custom-call(bf16[64,7168]{1,0:T(8,128)(2,1)S(1)} %copy-done.8, bf16[64,7168]{1,0:T(8,128)(2,1)S(1)} %collective-permute-done.23.refs_6_.refs_4_.refs_1_, bf16[32,7168]{1,0:T(8,128)(2,1)S(1)} %collective-permute-done.27.refs_2_, bf16[32,7168]{1,0:T(8,128)(2,1)S(1)} %collective-permute-done.28.refs_3_, ...), custom_call_target="tpu_custom_call" | custom-call | flops 1000 | bytes 1000 | tf_op jit(solution)/shard_map/pallas_call | solution.py:93
  207.7 5.1 %collective-permute-done.37.refs_3_.by_y = bf16[256,512]{1,0:T(8,128)(2,1)S(1)} collective-permute-done((bf16[256,512]{1,0:T(8,128)(2,1)S(1)}, bf16[256,512]{1,0:T(8,128)(2,1)S(1)}, u32[]{:S(2)}, u32[]{:S(2)}) %collective-permute-start.37) | collective-permute-done | bytes 262176 | tf_op jit(solution)/shard_map/ppermute | solution.py:62
  212.9 3.5 %shard_map.90.refs_1_ = bf16[256,1792]{1,0:T(8,128)(2,1)S(1)} custom-call(bf16[256,512]{1,0:T(8,128)(2,1)S(1)} %get-tuple-element.131.own, bf16[256,512]{1,0:T(8,128)(2,1)S(1)} %collective-permute-done.36.refs_2_.by_x, bf16[256,512]{1,0:T(8,128)(2,1)S(1)} %collective-permute-done.37.refs_3_.by_y, ...), custom_call_target="tpu_custom_call" | custom-call | flops 1000 | bytes 1000 | tf_op jit(solution)/shard_map/pallas_call | solution.py:132
  220.5 3.5 %collective-permute-done.41.refs_4_.across = bf16[256,512]{1,0:T(8,128)(2,1)S(1)} collective-permute-done((bf16[256,512]{1,0:T(8,128)(2,1)S(1)}, bf16[256,512]{1,0:T(8,128)(2,1)S(1)}, u32[]{:S(2)}, u32[]{:S(2)}) %collective-permute-start.41) | collective-permute-done | bytes 262176 | tf_op jit(solution)/shard_map/ppermute | solution.py:62
  224.0 2.8 %collective-permute-done.40.refs_3_.by_y = bf16[256,512]{1,0:T(8,128)(2,1)} collective-permute-done((bf16[256,512]{1,0:T(8,128)(2,1)S(1)}, bf16[256,512]{1,0:T(8,128)(2,1)}, u32[]{:S(2)}, u32[]{:S(2)}) %collective-permute-start.40) | collective-permute-done | bytes 262176 | tf_op jit(solution)/shard_map/ppermute | solution.py:62
  227.5 5.8 %shard_map.93 = bf16[256,1792]{1,0:T(8,128)(2,1)} custom-call(bf16[256,512]{1,0:T(8,128)(2,1)} %copy-done.6, bf16[256,512]{1,0:T(8,128)(2,1)} %collective-permute-done.39.refs_2_.by_x, bf16[256,512]{1,0:T(8,128)(2,1)} %collective-permute-done.40.refs_3_.by_y, bf16[256,512]{1,0:T(8,128)(2,1)} %copy-done.9, bf16[1024,1792]{1,0:T(8,128)(2,1)} %copy-done, ...), custom_call_target="tpu_custom_call" | custom-call | flops 1000 | bytes 1000 | tf_op jit(solution)/shard_map/pallas_call | solution.py:132
  239.4 3.5 %collective-permute-done.44 = bf16[64,1792]{1,0:T(8,128)(2,1)S(1)} collective-permute-done((bf16[64,1792]{1,0:T(8,128)(2,1)S(1)}, bf16[64,1792]{1,0:T(8,128)(2,1)S(1)}, u32[]{:S(2)}, u32[]{:S(2)}) %collective-permute-start.44) | collective-permute-done | bytes 229408 | tf_op jit(solution)/shard_map/ppermute | solution.py:62
  (154 shorter events, 75.4 us)
Async XLA Ops:
  0.0 43.1 %collective-permute-start.2 = (bf16[64,7168]{1,0:T(8,128)(2,1)}, bf16[64,7168]{1,0:T(8,128)(2,1)S(1)}, u32[]{:S(2)}, u32[]{:S(2)}) collective-permute-start(bf16[64,7168]{1,0:T(8,128)(2,1)} %refs_0_.1), channel_id=1, source_target_pairs={{0,8},{1,9},{2,10},{3,11},{4,12},{5,13},{6,14},{7,15},{8,0},{9,1},... | collective-permute-start | bytes 2752520 | tf_op jit(solution)/shard_map/ppermute | solution.py:62
  3.0 42.7 %collective-permute-start = (bf16[64,7168]{1,0:T(8,128)(2,1)}, bf16[64,7168]{1,0:T(8,128)(2,1)}, u32[]{:S(2)}, u32[]{:S(2)}) collective-permute-start(bf16[64,7168]{1,0:T(8,128)(2,1)} %refs_0_.1), channel_id=1, source_target_pairs={{0,16},{1,17},{2,18},{3,19},{4,20},{5,21},{6,22},{7,23},{8,24},{9,... | collective-permute-start | bytes 2752520 | tf_op jit(solution)/shard_map/ppermute | solution.py:62
  8.9 36.8 %collective-permute-start.3 = (bf16[256,1792]{1,0:T(8,128)(2,1)S(1)}, bf16[256,1792]{1,0:T(8,128)(2,1)S(1)}, u32[]{:S(2)}, u32[]{:S(2)}) collective-permute-start(bf16[256,1792]{1,0:T(8,128)(2,1)S(1)} %get-tuple-element.142), channel_id=1, source_target_pairs={{0,4},{1,5},{2,6},{3,7},{4,0},{5,1},{6,2},{7,3},{8,12},{9,13},{10,... | collective-permute-start | bytes 2752520 | tf_op jit(solution)/shard_map/ppermute | solution.py:62
  10.5 35.3 %collective-permute-start.1 = (bf16[256,1792]{1,0:T(8,128)(2,1)S(1)}, bf16[256,1792]{1,0:T(8,128)(2,1)S(1)}, u32[]{:S(2)}, u32[]{:S(2)}) collective-permute-start(bf16[256,1792]{1,0:T(8,128)(2,1)S(1)} %get-tuple-element.143), channel_id=1, source_target_pairs={{0,2},{1,3},{2,0},{3,1},{4,6},{5,7},{6,4},{7,5},{8,10},{9,11},{10,... | collective-permute-start | bytes 2752520 | tf_op jit(solution)/shard_map/ppermute | solution.py:62
  12.0 39.4 %collective-permute-start.4 = (bf16[256,1792]{1,0:T(8,128)(2,1)S(1)}, bf16[256,1792]{1,0:T(8,128)(2,1)S(1)}, u32[]{:S(2)}, u32[]{:S(2)}) collective-permute-start(bf16[256,1792]{1,0:T(8,128)(2,1)S(1)} %get-tuple-element.144), channel_id=1, source_target_pairs={{0,6},{1,7},{2,4},{3,5},{4,2},{5,3},{6,0},{7,1},{8,14},{9,15},{10,... | collective-permute-start | bytes 2752520 | tf_op jit(solution)/shard_map/ppermute | solution.py:62
  52.3 24.5 %collective-permute-start.8 = (bf16[7168,256]{1,0:T(8,128)(2,1)}, bf16[7168,256]{1,0:T(8,128)(2,1)}, u32[]{:S(2)}, u32[]{:S(2)}) collective-permute-start(bf16[7168,256]{1,0:T(8,128)(2,1)} %get-tuple-element.75), channel_id=1, source_target_pairs={{0,1},{1,0},{2,3},{3,2},{4,5},{5,4},{6,7},{7,6},{8,9},{9,8},{10,11... | collective-permute-start | bytes 11010056 | tf_op jit(solution)/shard_map/ppermute | solution.py:62
  52.3 24.6 %collective-permute-start.9 = (bf16[7168,256]{1,0:T(8,128)(2,1)}, bf16[7168,256]{1,0:T(8,128)(2,1)}, u32[]{:S(2)}, u32[]{:S(2)}) collective-permute-start(bf16[7168,256]{1,0:T(8,128)(2,1)} %get-tuple-element.76), channel_id=1, source_target_pairs={{0,1},{1,0},{2,3},{3,2},{4,5},{5,4},{6,7},{7,6},{8,9},{9,8},{10,11... | collective-permute-start | bytes 11010056 | tf_op jit(solution)/shard_map/ppermute | solution.py:62
  52.8 22.6 %collective-permute-start.6 = (bf16[64,7168]{1,0:T(8,128)(2,1)}, bf16[64,7168]{1,0:T(8,128)(2,1)}, u32[]{:S(2)}, u32[]{:S(2)}) collective-permute-start(bf16[64,7168]{1,0:T(8,128)(2,1)} %get-tuple-element.73.refs_0_), channel_id=1, source_target_pairs={{0,2},{1,3},{2,0},{3,1},{4,6},{5,7},{6,4},{7,5},{8,10},{9,11},{10,... | collective-permute-start | bytes 2752520 | tf_op jit(solution)/shard_map/ppermute | solution.py:62
  54.4 22.4 %collective-permute-start.7 = (bf16[64,7168]{1,0:T(8,128)(2,1)}, bf16[64,7168]{1,0:T(8,128)(2,1)S(1)}, u32[]{:S(2)}, u32[]{:S(2)}) collective-permute-start(bf16[64,7168]{1,0:T(8,128)(2,1)} %get-tuple-element.73.refs_0_), channel_id=1, source_target_pairs={{0,8},{1,9},{2,10},{3,11},{4,12},{5,13},{6,14},{7,15},{8,0},{9,1},... | collective-permute-start | bytes 2752520 | tf_op jit(solution)/shard_map/ppermute | solution.py:62
  54.8 21.9 %collective-permute-start.5 = (bf16[64,7168]{1,0:T(8,128)(2,1)}, bf16[64,7168]{1,0:T(8,128)(2,1)S(1)}, u32[]{:S(2)}, u32[]{:S(2)}) collective-permute-start(bf16[64,7168]{1,0:T(8,128)(2,1)} %get-tuple-element.73.refs_0_), channel_id=1, source_target_pairs={{0,4},{1,5},{2,6},{3,7},{4,0},{5,1},{6,2},{7,3},{8,12},{9,13},{10,... | collective-permute-start | bytes 2752520 | tf_op jit(solution)/shard_map/ppermute | solution.py:62
  76.9 15.3 %collective-permute-start.12 = (bf16[1024,1792]{1,0:T(8,128)(2,1)S(1)}, bf16[1024,1792]{1,0:T(8,128)(2,1)S(1)}, u32[]{:S(2)}, u32[]{:S(2)}) collective-permute-start(bf16[1024,1792]{1,0:T(8,128)(2,1)S(1)} %get-tuple-element.81.mine), channel_id=1, source_target_pairs={{0,1},{1,0},{2,3},{3,2},{4,5},{5,4},{6,7},{7,6},{8,9},{9,8},{10,11... | collective-permute-start | bytes 11010056 | tf_op jit(solution)/shard_map/ppermute | solution.py:62
  76.9 14.9 %collective-permute-start.10 = (bf16[32,7168]{1,0:T(8,128)(2,1)S(1)}, bf16[32,7168]{1,0:T(8,128)(2,1)S(1)}, u32[]{:S(2)}, u32[]{:S(2)}) collective-permute-start(bf16[32,7168]{1,0:T(8,128)(2,1)S(1)} %get-tuple-element.78), channel_id=1, source_target_pairs={{0,4},{1,5},{2,6},{3,7},{4,0},{5,1},{6,2},{7,3},{8,12},{9,13},{10,... | collective-permute-start | bytes 1376264 | tf_op jit(solution)/shard_map/ppermute | solution.py:62
  92.2 27.2 %collective-permute-start.17 = (bf16[64,7168]{1,0:T(8,128)(2,1)S(1)}, bf16[64,7168]{1,0:T(8,128)(2,1)S(1)}, u32[]{:S(2)}, u32[]{:S(2)}) collective-permute-start(bf16[64,7168]{1,0:T(8,128)(2,1)S(1)} %get-tuple-element.87.refs_1_), channel_id=1, source_target_pairs={{0,4},{1,5},{2,6},{3,7},{4,0},{5,1},{6,2},{7,3},{8,12},{9,13},{10,... | collective-permute-start | bytes 2752520 | tf_op jit(solution)/shard_map/ppermute | solution.py:62
  92.8 26.6 %collective-permute-start.16 = (bf16[64,7168]{1,0:T(8,128)(2,1)S(1)}, bf16[64,7168]{1,0:T(8,128)(2,1)S(1)}, u32[]{:S(2)}, u32[]{:S(2)}) collective-permute-start(bf16[64,7168]{1,0:T(8,128)(2,1)S(1)} %get-tuple-element.87.refs_1_), channel_id=1, source_target_pairs={{0,2},{1,3},{2,0},{3,1},{4,6},{5,7},{6,4},{7,5},{8,10},{9,11},{10,... | collective-permute-start | bytes 2752520 | tf_op jit(solution)/shard_map/ppermute | solution.py:62
  105.0 14.2 %collective-permute-start.20 = (bf16[256,512]{1,0:T(8,128)(2,1)S(1)}, bf16[256,512]{1,0:T(8,128)(2,1)S(1)}, u32[]{:S(2)}, u32[]{:S(2)}) collective-permute-start(bf16[256,512]{1,0:T(8,128)(2,1)S(1)} %get-tuple-element.88.refs_2_), channel_id=1, source_target_pairs={{0,4},{1,5},{2,6},{3,7},{4,0},{5,1},{6,2},{7,3},{8,12},{9,13},{10,... | collective-permute-start | bytes 786440 | tf_op jit(solution)/shard_map/ppermute | solution.py:62
  107.3 19.9 %collective-permute-start.18 = (bf16[64,7168]{1,0:T(8,128)(2,1)S(1)}, bf16[64,7168]{1,0:T(8,128)(2,1)S(1)}, u32[]{:S(2)}, u32[]{:S(2)}) collective-permute-start(bf16[64,7168]{1,0:T(8,128)(2,1)S(1)} %get-tuple-element.93), channel_id=1, source_target_pairs={{0,8},{1,9},{2,10},{3,11},{4,12},{5,13},{6,14},{7,15},{8,0},{9,1},... | collective-permute-start | bytes 2752520 | tf_op jit(solution)/shard_map/ppermute | solution.py:62
  127.2 29.1 %collective-permute-start.22 = (bf16[64,7168]{1,0:T(8,128)(2,1)S(1)}, bf16[64,7168]{1,0:T(8,128)(2,1)S(1)}, u32[]{:S(2)}, u32[]{:S(2)}) collective-permute-start(bf16[64,7168]{1,0:T(8,128)(2,1)S(1)} %get-tuple-element.101), channel_id=1, source_target_pairs={{0,8},{1,9},{2,10},{3,11},{4,12},{5,13},{6,14},{7,15},{8,0},{9,1},... | collective-permute-start | bytes 2752520 | tf_op jit(solution)/shard_map/ppermute | solution.py:62
  128.9 27.3 %collective-permute-start.23 = (bf16[64,7168]{1,0:T(8,128)(2,1)S(1)}, bf16[64,7168]{1,0:T(8,128)(2,1)S(1)}, u32[]{:S(2)}, u32[]{:S(2)}) collective-permute-start(bf16[64,7168]{1,0:T(8,128)(2,1)S(1)} %get-tuple-element.102), channel_id=1, source_target_pairs={{0,2},{1,3},{2,0},{3,1},{4,6},{5,7},{6,4},{7,5},{8,10},{9,11},{10,... | collective-permute-start | bytes 2752520 | tf_op jit(solution)/shard_map/ppermute | solution.py:62
  129.3 27.0 %collective-permute-start.24 = (bf16[64,7168]{1,0:T(8,128)(2,1)S(1)}, bf16[64,7168]{1,0:T(8,128)(2,1)S(1)}, u32[]{:S(2)}, u32[]{:S(2)}) collective-permute-start(bf16[64,7168]{1,0:T(8,128)(2,1)S(1)} %get-tuple-element.103), channel_id=1, source_target_pairs={{0,4},{1,5},{2,6},{3,7},{4,0},{5,1},{6,2},{7,3},{8,12},{9,13},{10,... | collective-permute-start | bytes 2752520 | tf_op jit(solution)/shard_map/ppermute | solution.py:62
  130.6 17.5 %collective-permute-start.25 = (f32[64,4]{1,0:T(8,128)S(1)}, f32[64,4]{1,0:T(8,128)S(1)}, u32[]{:S(2)}, u32[]{:S(2)}) collective-permute-start(f32[64,4]{1,0:T(8,128)S(1)} %get-tuple-element.100.refs_4_), channel_id=1, source_target_pairs={{0,4},{1,5},{2,6},{3,7},{4,0},{5,1},{6,2},{7,3},{8,12},{9,13},{10,... | collective-permute-start | bytes 3080 | tf_op jit(solution)/shard_map/ppermute | solution.py:62
  134.7 30.8 %collective-permute-start.29 = (bf16[128,1792]{1,0:T(8,128)(2,1)S(1)}, bf16[128,1792]{1,0:T(8,128)(2,1)S(1)}, u32[]{:S(2)}, u32[]{:S(2)}) collective-permute-start(bf16[128,1792]{1,0:T(8,128)(2,1)S(1)} %get-tuple-element.110), channel_id=1, source_target_pairs={{0,16},{1,17},{2,18},{3,19},{4,20},{5,21},{6,22},{7,23},{8,24},{9,... | collective-permute-start | bytes 1376264 | tf_op jit(solution)/shard_map/ppermute | solution.py:62
  158.7 24.2 %collective-permute-start.30 = (bf16[128,1792]{1,0:T(8,128)(2,1)S(1)}, bf16[128,1792]{1,0:T(8,128)(2,1)S(1)}, u32[]{:S(2)}, u32[]{:S(2)}) collective-permute-start(bf16[128,1792]{1,0:T(8,128)(2,1)S(1)} %get-tuple-element.115), channel_id=1, source_target_pairs={{0,16},{1,17},{2,18},{3,19},{4,20},{5,21},{6,22},{7,23},{8,24},{9,... | collective-permute-start | bytes 1376264 | tf_op jit(solution)/shard_map/ppermute | solution.py:62
  200.9 32.3 %collective-permute-start.43 = (bf16[256,1792]{1,0:T(8,128)(2,1)S(1)}, bf16[256,1792]{1,0:T(8,128)(2,1)}, u32[]{:S(2)}, u32[]{:S(2)}) collective-permute-start(bf16[256,1792]{1,0:T(8,128)(2,1)S(1)} %get-tuple-element.136), channel_id=1, source_target_pairs={{0,24},{1,25},{2,26},{3,27},{4,28},{5,29},{6,30},{7,31},{8,16},{9,... | collective-permute-start | bytes 2752520 | tf_op jit(solution)/shard_map/ppermute | solution.py:62
  216.4 16.9 %collective-permute-start.42 = (bf16[256,1792]{1,0:T(8,128)(2,1)S(1)}, bf16[256,1792]{1,0:T(8,128)(2,1)}, u32[]{:S(2)}, u32[]{:S(2)}) collective-permute-start(bf16[256,1792]{1,0:T(8,128)(2,1)S(1)} %get-tuple-element.135), channel_id=1, source_target_pairs={{0,8},{1,9},{2,10},{3,11},{4,12},{5,13},{6,14},{7,15},{8,0},{9,1},... | collective-permute-start | bytes 2752520 | tf_op jit(solution)/shard_map/ppermute | solution.py:62
  (35 other events, 543.2 us)
